TPU v7x, 32 devices: a whole 2x2x4 slice. The times are simulated.
32 devices in a mesh: row: 4 (over x, core), col: 4 (over z), layer: 2 (over y).
Axes of the slice: x: 2, y: 2, z: 4, core: 2. Of those that a mesh axis runs over, the one named last changes fastest.
Arguments:
- a_tiles: bfloat16 [4096, 16384], P('row', ('layer', 'col')), may hold values from -6 to 6
- a_occupancy: int32 [32, 128], P('row', ('layer', 'col')), may hold values 0 or 1
- b_tiles: bfloat16 [16384, 8192], P(('layer', 'row'), 'col'), may hold values from -0.046875 to 0.046875
- b_occupancy: int32 [128, 64], P(('layer', 'row'), 'col'), may hold values 0 or 1
Outputs:
- product: float32 [4096, 8192], P(('row', 'layer'), 'col')
Inputs may be any that keep to these rules, and one draw needn't show every extreme that they name: `a_occupancy`: each entry is 0 (block absent) or 1 (block present). `b_occupancy`: each entry is 0 (block absent) or 1 (block present).
All inputs are finite; a program needn't handle non-finite values.
Results may differ from a plain program's by a relative error of at most 0.0003.
Values may be sent and summed in bfloat16 or wider, within the bound.
No kernel may reach another device: no remote copies, remote signals or barrier semaphores. Data moves between devices by JAX's collectives and lax.ppermute only.
A program may use at most 128 MiB of HBM per device.

v0:
```python
import jax
import jax.numpy as jnp
from jax import lax
from jax.sharding import PartitionSpec as P

BLOCK = 128


def keep_blocks(values, occupancy):
    height, breadth = values.shape
    tiled = values.reshape(height // BLOCK, BLOCK, breadth // BLOCK, BLOCK)
    flags = occupancy.astype(values.dtype)
    return (tiled * flags[:, None, :, None]).reshape(height, breadth)


def per_device(a_tiles, a_occupancy, b_tiles, b_occupancy):
    a_kept = keep_blocks(a_tiles, a_occupancy)
    b_kept = keep_blocks(b_tiles, b_occupancy)
    b_slab = lax.all_gather(b_kept, "row", axis=0, tiled=True)
    partial_value = jnp.dot(
        lax.all_gather(a_kept, "col", axis=1, tiled=True),
        b_slab,
        preferred_element_type=jnp.float32,
    )
    return lax.psum_scatter(partial_value, "layer", scatter_dimension=0, tiled=True)


def solution(mesh):
    in_specs = (
        P("row", ("layer", "col")),
        P("row", ("layer", "col")),
        P(("layer", "row"), "col"),
        P(("layer", "row"), "col"),
    )
    out_specs = P(("row", "layer"), "col")
    return jax.shard_map(
        per_device, mesh=mesh, in_specs=in_specs, out_specs=out_specs, check_vma=False
    )
```

profile of v0, /device:TPU:0, one launch (start us, length us, event | category | flops | bytes accessed | tf_op | source)
XLA Modules:
  0.0 653.2 jit_solution(13656230010446052378)
XLA Ops:
  6.5 0.0 all-gather.3.cloned.1.call-start
  6.5 0.7 convert_element_type.6
  7.2 0.6 mul.22
  7.8 0.0 copy-start
  7.9 5.2 bitcast_multiply_fusion.1
  13.0 0.0 all-gather.3.cloned.1.call-update
  13.0 0.0 all-gather.5.cloned.1.call-start
  13.1 0.0 copy-done
  13.1 1.1 mul.25
  14.3 7.7 %bitcast_multiply_fusion = bf16[2048,2048]{1,0:T(8,128)(2,1)} fusion(bf16[2048,2048]{1,0:T(8,128)(2,1)} %param.6, bf16[256,8,16,128]{3,2,1,0:T(8,128)(2,1)S(1)} %bitcast.10), kind=kLoop, calls=%fused_computation | loop fusion | flops 4194304 | bytes 25165824 | tf_op jit(solution)/shard_map/mul | solution.py:13
  21.9 0.0 all-gather.5.cloned.1.call-update
  22.0 0.0 reduce-scatter.2.cloned.1.call-start
  22.0 280.6 %all-gather.3.cloned.1.call-done = bf16[1024,8192]{1,0:T(8,128)(2,1)} async-done(((bf16[1024,2048]{1,0:T(8,128)(2,1)}), bf16[1024,8192]{1,0:T(8,128)(2,1)}) %all-gather.3.cloned.1.call-update) | async-done | bytes 16777232 | tf_op jit(solution)/shard_map/all_gather | solution.py:21
  302.7 201.3 %all-gather.5.cloned.1.call-done = bf16[8192,2048]{1,0:T(8,128)(2,1)} async-done(((bf16[2048,2048]{1,0:T(8,128)(2,1)}), bf16[8192,2048]{1,0:T(8,128)(2,1)}) %all-gather.5.cloned.1.call-update) | async-done | bytes 33554448 | tf_op jit(solution)/shard_map/all_gather | solution.py:19
  504.0 43.3 %fusion = f32[1024,2048]{1,0:T(8,128)} fusion(bf16[1024,8192]{1,0:T(8,128)(2,1)} %all-gather.3.cloned.1.call-done, bf16[8192,2048]{1,0:T(8,128)(2,1)} %all-gather.5.cloned.1.call-done), kind=kOutput, calls=%fused_computation.2 | convolution fusion | flops 34359738368 | bytes 58720256 | tf_op jit(solution)/shard_map/dot_general | solution.py:20
  547.2 0.0 reduce-scatter.2.cloned.1.call-update
  547.3 99.4 %reduce-scatter.2.cloned.1.call-done = f32[512,2048]{1,0:T(8,128)} async-done(((f32[1024,2048]{1,0:T(8,128)}), f32[512,2048]{1,0:T(8,128)}) %reduce-scatter.2.cloned.1.call-update) | async-done | bytes 4194320 | tf_op jit(solution)/shard_map/reduce_scatter | solution.py:25
  (1 shorter events, 0.0 us)
Async XLA Ops:
  6.5 296.1 %all-gather.3.cloned.1.call-start = ((), (), s32[]{:S(2)}) async-start(), calls=%async_computation.1 | async-start | bytes 20971520 | tf_op jit(solution)/shard_map/all_gather | solution.py:21
  7.8 5.2 copy-start
  13.0 490.9 %all-gather.5.cloned.1.call-start = ((), (), s32[]{:S(2)}) async-start(), calls=%async_computation.2 | async-start | bytes 41943040 | tf_op jit(solution)/shard_map/all_gather | solution.py:19
  22.0 624.7 %reduce-scatter.2.cloned.1.call-start = ((), (), s32[]{:S(2)}) async-start(), calls=%async_computation.3 | async-start | bytes 12582912 | tf_op jit(solution)/shard_map/reduce_scatter | solution.py:25
Sparse Core Ops, SparseCore 0:
  13.2 289.4 all-gather.2
  304.2 199.7 all-gather.4
  547.4 99.2 reduce-scatter.1
where the time goes:
time: 653 us
  waiting for transfers between devices  581 us (89%)
  matrix products  43.3 us (7%)
  other arithmetic  13.5 us (2%)
  between operations  13.1 us (2%)
    all_gather x1, waiting for transfers between devices, per_device(): lax.all_gather(a_kept, 'col', axis=1, tiled=True)  281 us
    all_gather x1, waiting for transfers between devices, per_device(): b_slab = lax.all_gather(b_kept, 'row', axis=0, tiled=True)  201 us
    reduce_scatter x1, waiting for transfers between devices, per_device(): lax.psum_scatter(partial_value, 'layer', scatter_dimension=0, tiled=True)  99.4 us
    dot_general x1, matrix products, per_device(): jnp.dot(lax.all_gather(a_kept, 'col', axis=1, tiled=True), b_slab, prefer...  43.3 us
  transfers between devices with their start and end apart: 3, of which 3 were waited for; matrix products, arithmetic and copies ran while one was open for 1% of the time, Pallas kernels for 0%

commit v1 on v0

v1 whole, which is shorter than its diff:
```python
import functools

import jax
import jax.numpy as jnp
from jax import lax
from jax.experimental import pallas as pl
from jax.experimental.pallas import tpu as pltpu
from jax.sharding import PartitionSpec as P

BLOCK = 128
VMEM_LIMIT = 56 * 1024 * 1024


def keep_blocks(values, occupancy):
    height, breadth = values.shape
    tiled = values.reshape(height // BLOCK, BLOCK, breadth // BLOCK, BLOCK)
    flags = occupancy.astype(values.dtype)
    return (tiled * flags[:, None, :, None]).reshape(height, breadth)


def whole_slab(a_tiles, a_occupancy, b_tiles, b_occupancy):
    a_kept = keep_blocks(a_tiles, a_occupancy)
    b_kept = keep_blocks(b_tiles, b_occupancy)
    partial_value = jnp.dot(
        lax.all_gather(a_kept, "col", axis=1, tiled=True),
        lax.all_gather(b_kept, "row", axis=0, tiled=True),
        preferred_element_type=jnp.float32,
    )
    return lax.psum_scatter(partial_value, "layer", scatter_dimension=0, tiled=True)


def slots_for(blocks):
    if blocks < 16:
        return blocks + 1
    room = (blocks * 7 + 15) // 16 + int(round(1.56 * blocks**0.5))
    return min(blocks, room) + 1


def cuts_for(stops):
    cuts = [0]
    for blocks in stops:
        cuts.append(max(slots_for(blocks), cuts[-1] + 1))
    return cuts


def header_of(occupancy):
    rows, columns = occupancy.shape
    flags = occupancy.astype(jnp.bfloat16)
    return jnp.pad(flags, ((0, BLOCK - rows), (0, BLOCK - columns)))


def pack_kernel(place, count, cuts, turn_ref, flags_ref, header_ref, values_ref, *refs):
    parts, (held, sems) = refs[: len(cuts) - 1], refs[len(cuts) - 1 :]
    held[0] = header_ref[...]

    def step(t, slot):
        row, column, index = place(t, turn_ref[0])
        at_row = pl.multiple_of(row * BLOCK, BLOCK)
        at_column = pl.multiple_of(column * BLOCK, BLOCK)
        held[jnp.minimum(slot, cuts[-1])] = values_ref[pl.ds(at_row, BLOCK), pl.ds(at_column, BLOCK)]
        return slot + flags_ref[index]

    lax.fori_loop(0, count, step, jnp.int32(1), unroll=8)
    copies = [
        pltpu.make_async_copy(held.at[pl.ds(lo, hi - lo)], part, sems.at[i])
        for i, (part, lo, hi) in enumerate(zip(parts, cuts[:-1], cuts[1:]))
    ]
    for copy in copies:
        copy.start()
    for copy in copies:
        copy.wait()


def pack(values, occupancy, turn, place, cuts):
    count = occupancy.size
    return pl.pallas_call(
        functools.partial(pack_kernel, place, count, cuts),
        grid_spec=pltpu.PrefetchScalarGridSpec(
            num_scalar_prefetch=2,
            grid=(),
            in_specs=[pl.BlockSpec(memory_space=pltpu.VMEM)] * 2,
            out_specs=[pl.BlockSpec(memory_space=pl.ANY)] * (len(cuts) - 1),
            scratch_shapes=[
                pltpu.VMEM((cuts[-1] + 1, BLOCK, BLOCK), values.dtype),
                pltpu.SemaphoreType.DMA((len(cuts) - 1,)),
            ],
        ),
        out_shape=[
            jax.ShapeDtypeStruct((hi - lo, BLOCK, BLOCK), values.dtype) for lo, hi in zip(cuts[:-1], cuts[1:])
        ],
        compiler_params=pltpu.CompilerParams(vmem_limit_bytes=VMEM_LIMIT),
        cost_estimate=pl.CostEstimate(flops=0, bytes_accessed=2 * values.size * 2, transcendentals=0),
        name="pack",
    )(turn, occupancy.reshape(-1), header_of(occupancy), values)


def take(parts, cuts, slot, present):
    block = None
    for part, lo, hi in zip(parts, cuts[:-1], cuts[1:]):
        mine = part[jnp.clip(slot - lo, 0, hi - lo - 1)]
        block = mine if block is None else jnp.where(slot >= lo, mine, block)
    return jnp.where(present, block, jnp.zeros_like(block))


def unpack_a_kernel(place, first, rows, k_blocks, blocks, cuts, turn_ref, flags_ref, *refs):
    parts, out_ref = refs[:-1], refs[-1]
    base = pl.program_id(0) * blocks

    def passed(t, slot):
        return slot + flags_ref[base + place(t, turn_ref[0])[2]]

    def step(t, slot):
        flag = flags_ref[base + place(t + first * k_blocks, turn_ref[0])[2]]
        at_row = pl.multiple_of(t // k_blocks * BLOCK, BLOCK)
        at_column = pl.multiple_of(t % k_blocks * BLOCK, BLOCK)
        out_ref[pl.ds(at_row, BLOCK), pl.ds(at_column, BLOCK)] = take(
            [p.at[0] for p in parts], cuts, slot, flag > 0
        )
        return slot + flag

    slot = lax.fori_loop(0, first * k_blocks, passed, jnp.int32(1))
    lax.fori_loop(0, rows * k_blocks, step, slot, unroll=8)


def unpack_a(parts, flags, turn, place, first, rows, k_blocks, cuts):
    shards = parts[0].shape[0]
    return pl.pallas_call(
        functools.partial(unpack_a_kernel, place, first, rows, k_blocks, flags.size // shards, cuts),
        grid_spec=pltpu.PrefetchScalarGridSpec(
            num_scalar_prefetch=2,
            grid=(shards,),
            in_specs=[pl.BlockSpec((1,) + p.shape[1:], lambda s, *_: (s, 0, 0, 0)) for p in parts],
            out_specs=pl.BlockSpec((rows * BLOCK, k_blocks * BLOCK), lambda s, *_: (0, s)),
        ),
        out_shape=jax.ShapeDtypeStruct((rows * BLOCK, shards * k_blocks * BLOCK), parts[0].dtype),
        compiler_params=pltpu.CompilerParams(vmem_limit_bytes=VMEM_LIMIT),
        cost_estimate=pl.CostEstimate(
            flops=0, bytes_accessed=4 * shards * rows * k_blocks * BLOCK * BLOCK, transcendentals=0
        ),
        name="unpack_a",
    )(turn, flags, *parts)


def unpack_b_kernel(k_blocks, columns, first, wide, cuts, shard_ref, flags_ref, *refs):
    parts, (out_ref, counter) = refs[: len(cuts) - 1], refs[-2:]

    def flag_of(t):
        return flags_ref[t % k_blocks * columns + t // k_blocks]

    @pl.when(pl.program_id(0) == 0)
    def _():
        counter[0] = lax.fori_loop(0, first * k_blocks, lambda t, slot: slot + flag_of(t), jnp.int32(1))

    start = (first + pl.program_id(0) * wide) * k_blocks

    def step(t, slot):
        flag = flag_of(start + t)
        at_row = pl.multiple_of(t % k_blocks * BLOCK, BLOCK)
        at_column = pl.multiple_of(t // k_blocks * BLOCK, BLOCK)
        out_ref[pl.ds(at_row, BLOCK), pl.ds(at_column, BLOCK)] = take(parts, cuts, slot, flag > 0)
        return slot + flag

    counter[0] = lax.fori_loop(0, wide * k_blocks, step, counter[0], unroll=8)


def unpack_b(parts, flags, shard, shards, first, stop, k_blocks, columns, cuts, into):
    wide = 2 if (stop - first) % 2 == 0 else 1
    n = len(parts)
    in_specs = [pl.BlockSpec(p.shape, lambda s, *_: (0, 0, 0)) for p in parts]
    operands = [*parts]
    if into is not None:
        in_specs.append(pl.BlockSpec(memory_space=pl.ANY))
        operands.append(into)
    return pl.pallas_call(
        functools.partial(unpack_b_kernel, k_blocks, columns, first, wide, cuts),
        grid_spec=pltpu.PrefetchScalarGridSpec(
            num_scalar_prefetch=2,
            grid=((stop - first) // wide,),
            in_specs=in_specs,
            out_specs=pl.BlockSpec((k_blocks * BLOCK, wide * BLOCK), lambda s, shard, *_: (shard[0], s)),
            scratch_shapes=[pltpu.SMEM((1,), jnp.int32)],
        ),
        out_shape=jax.ShapeDtypeStruct((shards * k_blocks * BLOCK, (stop - first) * BLOCK), parts[0].dtype),
        input_output_aliases={} if into is None else {2 + n: 0},
        compiler_params=pltpu.CompilerParams(vmem_limit_bytes=VMEM_LIMIT),
        cost_estimate=pl.CostEstimate(
            flops=0, bytes_accessed=4 * (stop - first) * k_blocks * BLOCK * BLOCK, transcendentals=0
        ),
        name="unpack_b",
    )(shard, flags, *operands)


def largest_over(value, axis, size):
    step = 1
    while step < size:
        value = jnp.maximum(value, lax.ppermute(value, axis, [(i, i ^ step) for i in range(size)]))
        step *= 2
    return value


def coded(values):
    height, breadth = values.shape
    tiled = values.reshape(height // BLOCK, BLOCK, breadth)
    top = jnp.max(jnp.abs(tiled), axis=1, keepdims=True)
    factor = jnp.where(top > 0, 32767.0 / top, 0.0)
    return jnp.round(tiled * factor).astype(jnp.int16), top * (1.0 / 32767.0)


def per_device(sizes, a_tiles, a_occupancy, b_tiles, b_occupancy):
    rows, cols, layers = sizes
    me_row, me_layer = lax.axis_index("row"), lax.axis_index("layer")
    a_rows, a_k = a_occupancy.shape
    b_k, b_columns = b_occupancy.shape
    piece = a_rows // layers

    def a_place(t, layer):
        row, k = t // a_k, t % a_k
        at = lax.rem(row + (layer + 1) * piece, a_rows)
        return at, k, at * a_k + k

    def b_place(t, _):
        column, k = t // b_k, t % b_k
        return k, column, k * b_columns + column

    given = a_rows - piece
    row_stops = [given, given + (piece + 1) // 2, a_rows] if piece > 1 else [given, a_rows]
    row_stops = [r for r in row_stops if r > 0]
    column_stops = [b_columns // 2, b_columns] if b_columns % 2 == 0 else [b_columns]
    a_cuts = cuts_for([r * a_k for r in row_stops])
    b_cuts = cuts_for([c * b_k for c in column_stops])

    turn = me_layer.astype(jnp.int32).reshape(1)
    a_parts = pack(a_tiles, a_occupancy, turn, a_place, a_cuts)
    b_parts = pack(b_tiles, b_occupancy, turn, b_place, b_cuts)

    a_turned = jnp.roll(a_occupancy, -(me_layer + 1) * piece, axis=0)
    over = jnp.zeros((), jnp.bool_)
    for stop, cut in zip(row_stops, a_cuts[1:]):
        over |= jnp.sum(a_turned[:stop]) > cut - 1
    for stop, cut in zip(column_stops, b_cuts[1:]):
        over |= jnp.sum(b_occupancy[:, :stop]) > cut - 1
    over = jnp.broadcast_to(over.astype(jnp.float32), (8, BLOCK))
    for axis, size in zip(("row", "layer", "col"), (rows, layers, cols)):
        over = largest_over(over, axis, size)

    a_lists = [lax.all_gather(p, "col", axis=0) for p in a_parts]
    a_flags = a_lists[0][:, 0, :a_rows, :a_k].astype(jnp.int32).reshape(-1)

    pair = 2 if rows % 2 == 0 else 1
    b_lists = []
    for hop in range(rows // pair):
        there = [(r, (r + pair * hop) % rows) for r in range(rows)]
        mine = b_parts if hop == 0 else [lax.ppermute(p, "row", there) for p in b_parts]
        b_lists.append((lax.rem(me_row - pair * hop + rows, rows), mine))
        if pair == 2:
            swap = [(r, r ^ 1) for r in range(rows)]
            b_lists.append((b_lists[-1][0] ^ 1, [lax.ppermute(p, "row", swap) for p in mine]))

    b_halves = []
    for h, stop in enumerate(column_stops):
        first = column_stops[h - 1] if h else 0
        dense = None
        for shard, lists in b_lists:
            flags = lists[0][0, :b_k, :b_columns].astype(jnp.int32).reshape(-1)
            dense = unpack_b(
                lists[: h + 1], flags, shard.astype(jnp.int32).reshape(1), rows, first, stop, b_k, b_columns,
                b_cuts[: h + 2], dense,
            )
        b_halves.append(dense)

    totals = [[None] * len(column_stops) for _ in row_stops]
    for g, stop in enumerate(row_stops):
        first = row_stops[g - 1] if g else 0
        a_dense = unpack_a(a_lists[: g + 1], a_flags, turn, a_place, first, stop - first, a_k, a_cuts[: g + 2])
        for h, b_dense in enumerate(b_halves):
            totals[g][h] = jnp.dot(a_dense, b_dense, preferred_element_type=jnp.float32)

    own = totals
    if given:
        own = totals[1:]
        for h in range(len(column_stops)):
            received = 0.0
            for q in range(layers - 1):
                codes, factors = coded(totals[0][h][q * piece * BLOCK : (q + 1) * piece * BLOCK])
                there = [(i, (i + 1 + q) % layers) for i in range(layers)]
                codes, factors = lax.ppermute(codes, "layer", there), lax.ppermute(factors, "layer", there)
                received += codes.astype(jnp.float32) * factors
            received = received.reshape(piece * BLOCK, -1)
            for g in range(len(own)):
                first, stop = row_stops[g] - given, row_stops[g + 1] - given
                own[g][h] = own[g][h] + received[first * BLOCK : stop * BLOCK]
    product = jnp.concatenate([jnp.concatenate(line, axis=1) for line in own], axis=0)
    return lax.cond(
        over[0, 0] > 0,
        lambda: whole_slab(a_tiles, a_occupancy, b_tiles, b_occupancy),
        lambda: product,
    )


def solution(mesh):
    sizes = tuple(mesh.shape[axis] for axis in ("row", "col", "layer"))
    in_specs = (
        P("row", ("layer", "col")),
        P("row", ("layer", "col")),
        P(("layer", "row"), "col"),
        P(("layer", "row"), "col"),
    )
    out_specs = P(("row", "layer"), "col")
    return jax.shard_map(
        functools.partial(per_device, sizes), mesh=mesh, in_specs=in_specs, out_specs=out_specs, check_vma=False
    )
```

time: 653 us -> 348 us (0.53)
  waiting for transfers between devices: 581 us -> 132 us
  Pallas kernels: 0 us -> 105 us
  starting transfers between devices: 0.09 us -> 17.7 us
  matrix products: 43.3 us -> 55.2 us
  local copies, waits for them, and re-layouts: 1.76 us -> 8.33 us
    all_gather x2 -> x3, waiting for transfers between devices: 482 us -> 0.02 us  [per_device(): a_lists = [lax.all_gather(p, 'col', axis=0) for p in a_parts]]
    ppermute x0 -> x15, waiting for transfers between devices: none -> 132 us  [the longest x2 97.2 us: per_device(): lax.ppermute(p, 'row', there)]
    pallas_call x0 -> x13, Pallas kernels: none -> 105 us  [the longest x8 57.4 us: unpack_b(): pl.pallas_call(functools.partial(unpack_b_kernel, k_blocks, columns, firs...]
    reduce_scatter x1 -> x0, waiting for transfers between devices: 99.4 us -> none  [per_device(): lax.psum_scatter(partial_value, 'layer', scatter_dimension=0, tiled=True)]
    ppermute x0 -> x15, starting transfers between devices: none -> 17.7 us  [the longest x5 8.64 us: largest_over(): lax.ppermute(value, axis, [(i, i ^ step) for i in range(size)])]
    dot_general x1 -> x6, matrix products: 43.3 us -> 55.2 us  [per_device(): totals[g][h] = jnp.dot(a_dense, b_dense, preferred_element_type=jnp.float32)]
    mul x2 -> x4, other arithmetic: 12.8 us -> 1.95 us  [the longest x2 1.93 us: per_device(): received += codes.astype(jnp.float32) * factors]
  transfers between devices with their start and end apart: 3 -> 18, of which waited for: 3 -> 7; matrix products, arithmetic and copies ran while one was open for 1% -> 11% of each run, Pallas kernels for 0% -> 28%
where the time goes in v1:
time: 348 us; the launch traced here: 347 us
  waiting for transfers between devices  132 us (38%)
  Pallas kernels  105 us (30%)
  matrix products  55.2 us (16%)
  starting transfers between devices  17.7 us (5%)
  between operations  17.4 us (5%)
  other arithmetic  11.9 us (3%)
  local copies, waits for them, and re-layouts  8.33 us (2%)
    ppermute x2, waiting for transfers between devices, per_device(): lax.ppermute(p, 'row', there)  97.2 us
    pallas_call x8, Pallas kernels, unpack_b(): pl.pallas_call(functools.partial(unpack_b_kernel, k_blocks, columns, firs...  57.4 us
    dot_general x6, matrix products, per_device(): totals[g][h] = jnp.dot(a_dense, b_dense, preferred_element_type=jnp.float32)  55.2 us
    ppermute x5, waiting for transfers between devices, largest_over(): lax.ppermute(value, axis, [(i, i ^ step) for i in range(size)])  32.9 us
    pallas_call x3, Pallas kernels, unpack_a(): pl.pallas_call(functools.partial(unpack_a_kernel, place, first, rows, k_b...  32 us
    pallas_call x2, Pallas kernels, pack(): pl.pallas_call(functools.partial(pack_kernel, place, count, cuts), grid_s...  15.5 us
    ppermute x5, starting transfers between devices, largest_over(): lax.ppermute(value, axis, [(i, i ^ step) for i in range(size)])  8.64 us
  transfers between devices with their start and end apart: 18, of which 7 were waited for; matrix products, arithmetic and copies ran while one was open for 11% of the time, Pallas kernels for 28%

profile of v1, /device:TPU:0, one launch (start us, length us, event | category | flops | bytes accessed | tf_op | source)
XLA Modules:
  0.0 347.1 jit_solution(11844188610931142511)
XLA Ops:
  10.0 6.2 %pack.2 = (bf16[41,128,128]{2,1,0:T(8,128)(2,1)}, bf16[17,128,128]{2,1,0:T(8,128)(2,1)}, bf16[17,128,128]{2,1,0:T(8,128)(2,1)}) custom-call(s32[1]{0:T(128)} %bitcast.1.turn_ref, s32[128]{0:T(128)} %reshape.110.flags_ref, bf16[128,128]{1,0:T(8,128)(2,1)} %pad.8.header_ref, bf16[1024,2048]{1,0:T(8,128)(2,1)} %values_ref.2), custom_call_target="tpu_custom_call" | custom-call | bytes 8388608 | tf_op jit(solution)/shard_map/pack/pallas_call | solution.py:76
  18.2 9.4 %pack.3 = (bf16[75,128,128]{2,1,0:T(8,128)(2,1)}, bf16[63,128,128]{2,1,0:T(8,128)(2,1)}) custom-call(s32[1]{0:T(128)} %bitcast.1.turn_ref, s32[256]{0:T(256)} %reshape.112.flags_ref, bf16[128,128]{1,0:T(8,128)(2,1)} %pad.9.header_ref, bf16[2048,2048]{1,0:T(8,128)(2,1)} %values_ref.3), custom_call_target="tpu_custom_call" | custom-call | bytes 16777216 | tf_op jit(solution)/shard_map/pack/pallas_call | solution.py:76
  27.6 3.0 collective-permute-start.5
  30.8 54.2 %collective-permute-done.5.refs_0_ = bf16[75,128,128]{2,1,0:T(8,128)(2,1)S(1)} collective-permute-done((bf16[75,128,128]{2,1,0:T(8,128)(2,1)}, bf16[75,128,128]{2,1,0:T(8,128)(2,1)S(1)}, u32[]{:S(2)}, u32[]{:S(2)}) %collective-permute-start.5) | collective-permute-done | bytes 2457632 | tf_op jit(solution)/shard_map/ppermute | solution.py:253
  85.5 43.0 %collective-permute-done.10.refs_1_ = bf16[63,128,128]{2,1,0:T(8,128)(2,1)} collective-permute-done((bf16[63,128,128]{2,1,0:T(8,128)(2,1)}, bf16[63,128,128]{2,1,0:T(8,128)(2,1)}, u32[]{:S(2)}, u32[]{:S(2)}) %collective-permute-start.10) | collective-permute-done | bytes 2064416 | tf_op jit(solution)/shard_map/ppermute | solution.py:253
  135.8 7.6 %unpack_b.12.refs_2_ = bf16[8192,1024]{1,0:T(8,128)(2,1)} custom-call(s32[1]{0:T(128)} %bitcast.7.shard_ref, s32[256]{0:T(256)} %reshape.123.flags_ref, bf16[75,128,128]{2,1,0:T(8,128)(2,1)} %get-tuple-element.28.refs_0_, bf16[63,128,128]{2,1,0:T(8,128)(2,1)} %get-tuple-element.29.refs_1_), custom_call_target="tpu_custom_call" | custom-call | bytes 8388608 | tf_op jit(solution)/shard_map/unpack_b/pallas_call | solution.py:174
  143.4 6.6 %unpack_b.8.refs_1_ = bf16[8192,1024]{1,0:T(8,128)(2,1)} custom-call(s32[1]{0:T(128)} %bitcast.7.shard_ref, s32[256]{0:T(256)} %reshape.123.flags_ref, bf16[75,128,128]{2,1,0:T(8,128)(2,1)} %get-tuple-element.28.refs_0_), custom_call_target="tpu_custom_call" | custom-call | bytes 8388608 | tf_op jit(solution)/shard_map/unpack_b/pallas_call | solution.py:174
  152.0 6.7 %unpack_b.9.refs_1_ = bf16[8192,1024]{1,0:T(8,128)(2,1)} custom-call(s32[1]{0:T(128)} %bitcast.6.shard_ref, s32[256]{0:T(256)} %reshape.122.flags_ref, bf16[75,128,128]{2,1,0:T(8,128)(2,1)} %collective-permute-done.7.refs_0_, bf16[8192,1024]{1,0:T(8,128)(2,1)} %unpack_b.8.refs_1_), custom_call_target="tpu_custom_call", output_to_operand_aliasing={{}: (3, {})} | custom-call | bytes 8388608 | tf_op jit(solution)/shard_map/unpack_b/pallas_call | solution.py:174
  158.8 7.7 %unpack_b.13.refs_2_ = bf16[8192,1024]{1,0:T(8,128)(2,1)} custom-call(s32[1]{0:T(128)} %bitcast.6.shard_ref, s32[256]{0:T(256)} %reshape.122.flags_ref, bf16[75,128,128]{2,1,0:T(8,128)(2,1)} %collective-permute-done.7.refs_0_, bf16[63,128,128]{2,1,0:T(8,128)(2,1)} %collective-permute-done.12.refs_1_, ...), custom_call_target="tpu_custom_call", output_to_operand_aliasing={{}: (4, {})} | custom-call | bytes 8388608 | tf_op jit(solution)/shard_map/unpack_b/pallas_call | solution.py:174
  166.5 7.6 %unpack_b.14.refs_2_ = bf16[8192,1024]{1,0:T(8,128)(2,1)} custom-call(s32[1]{0:T(128)} %bitcast.5.shard_ref, s32[256]{0:T(256)} %reshape.121.flags_ref, bf16[75,128,128]{2,1,0:T(8,128)(2,1)} %copy-done.1, bf16[63,128,128]{2,1,0:T(8,128)(2,1)} %collective-permute-done.10.refs_1_, bf16[8192,1024]{1,0:T(8,128)(2,1)} %unpack_b.13.refs_2_), custom_call_target="tpu_custom_call", output_to_operand_aliasing={{}: (4, {})} | custom-call | bytes 8388608 | tf_op jit(solution)/shard_map/unpack_b/pallas_call | solution.py:174
  174.1 6.8 %unpack_b.10.refs_1_ = bf16[8192,1024]{1,0:T(8,128)(2,1)} custom-call(s32[1]{0:T(128)} %bitcast.5.shard_ref, s32[256]{0:T(256)} %reshape.121.flags_ref, bf16[75,128,128]{2,1,0:T(8,128)(2,1)} %copy-done.1, bf16[8192,1024]{1,0:T(8,128)(2,1)} %unpack_b.9.refs_1_), custom_call_target="tpu_custom_call", output_to_operand_aliasing={{}: (3, {})} | custom-call | bytes 8388608 | tf_op jit(solution)/shard_map/unpack_b/pallas_call | solution.py:174
  182.2 6.7 %unpack_b.11 = bf16[8192,1024]{1,0:T(8,128)(2,1)} custom-call(s32[1]{0:T(128)} %bitcast.4.shard_ref, s32[256]{0:T(256)} %reshape.120.flags_ref, bf16[75,128,128]{2,1,0:T(8,128)(2,1)} %collective-permute-done.6.refs_0_, bf16[8192,1024]{1,0:T(8,128)(2,1)} %unpack_b.10.refs_1_), custom_call_target="tpu_custom_call", output_to_operand_aliasing={{}: (3, {})} | custom-call | bytes 8388608 | tf_op jit(solution)/shard_map/unpack_b/pallas_call | solution.py:174
  188.9 7.7 %unpack_b.15 = bf16[8192,1024]{1,0:T(8,128)(2,1)} custom-call(s32[1]{0:T(128)} %bitcast.4.shard_ref, s32[256]{0:T(256)} %reshape.120.flags_ref, bf16[75,128,128]{2,1,0:T(8,128)(2,1)} %collective-permute-done.6.refs_0_, bf16[63,128,128]{2,1,0:T(8,128)(2,1)} %collective-permute-done.11.refs_1_, ...), custom_call_target="tpu_custom_call", output_to_operand_aliasing={{}: (4, {})} | custom-call | bytes 8388608 | tf_op jit(solution)/shard_map/unpack_b/pallas_call | solution.py:174
  197.9 9.6 %unpack_a.4 = bf16[512,8192]{1,0:T(8,128)(2,1)} custom-call(s32[1]{0:T(128)} %bitcast.1.turn_ref, s32[512]{0:T(512)} %reshape.119.flags_ref, bf16[4,41,128,128]{3,2,1,0:T(8,128)(2,1)} %bitcast.54), custom_call_target="tpu_custom_call" | custom-call | bytes 16777216 | tf_op jit(solution)/shard_map/unpack_a/pallas_call | solution.py:127
  207.6 15.1 %abs_reduce_fusion = (f32[4,1024]{1,0:T(4,128)S(1)}, f32[512,1024]{1,0:T(8,128)S(1)}) fusion(bf16[512,8192]{1,0:T(8,128)(2,1)} %unpack_a.4, bf16[8192,1024]{1,0:T(8,128)(2,1)} %unpack_b.15), kind=kOutput, calls=%fused_computation.5 | convolution fusion | flops 8590979072 | bytes 27279360 | tf_op jit(solution)/shard_map/dot_general | solution.py:276
  223.0 1.8 collective-permute-start.13
  224.8 11.2 %abs_reduce_fusion.1 = (f32[4,1024]{1,0:T(4,128)S(1)}, f32[512,1024]{1,0:T(8,128)S(1)}) fusion(bf16[512,8192]{1,0:T(8,128)(2,1)} %unpack_a.4, bf16[8192,1024]{1,0:T(8,128)(2,1)S(1)} %bitcast.50), kind=kOutput, calls=%fused_computation.8 | convolution fusion | flops 8590979072 | bytes 27279360 | tf_op jit(solution)/shard_map/dot_general | solution.py:276
  236.8 1.8 collective-permute-start.1
  240.4 1.8 collective-permute-start.2
  242.1 28.9 %collective-permute-done.2 = f32[8,128]{1,0:T(8,128)S(1)} collective-permute-done((f32[8,128]{1,0:T(8,128)S(1)}, f32[8,128]{1,0:T(8,128)S(1)}, u32[]{:S(2)}, u32[]{:S(2)}) %collective-permute-start.2) | collective-permute-done | bytes 4128 | tf_op jit(solution)/shard_map/ppermute | solution.py:196
  271.1 1.8 collective-permute-start.3
  272.9 1.8 collective-permute-done.3
  274.7 2.7 collective-permute-start.4
  277.4 1.8 collective-permute-done.4
  280.4 10.0 %unpack_a.3 = bf16[256,8192]{1,0:T(8,128)(2,1)} custom-call(s32[1]{0:T(128)} %bitcast.1.turn_ref, s32[512]{0:T(512)} %reshape.119.flags_ref, bf16[4,41,128,128]{3,2,1,0:T(8,128)(2,1)} %bitcast.55, bf16[4,17,128,128]{3,2,1,0:T(8,128)(2,1)} %bitcast.59), custom_call_target="tpu_custom_call" | custom-call | bytes 8388608 | tf_op jit(solution)/shard_map/unpack_a/pallas_call | solution.py:127
  290.4 12.3 %unpack_a.5 = bf16[256,8192]{1,0:T(8,128)(2,1)} custom-call(s32[1]{0:T(128)} %bitcast.1.turn_ref, s32[512]{0:T(512)} %reshape.119.flags_ref, bf16[4,41,128,128]{3,2,1,0:T(8,128)(2,1)} %bitcast.56, bf16[4,17,128,128]{3,2,1,0:T(8,128)(2,1)} %bitcast.60, bf16[4,17,128,128]{3,2,1,0:T(8,128)(2,1)} %bitcast.61), custom_call_target="tpu_custom_call" | custom-call | bytes 8388608 | tf_op jit(solution)/shard_map/unpack_a/pallas_call | solution.py:127
  302.7 1.7 collective-permute-start.9
  309.2 10.1 %convolution_add_fusion.2 = f32[256,1024]{1,0:T(8,128)} fusion(f32[256,1024]{1,0:T(8,128)S(1)} %bitcast.63, bf16[256,8192]{1,0:T(8,128)(2,1)S(1)} %copy-done.3, bf16[8192,1024]{1,0:T(8,128)(2,1)} %unpack_b.15), kind=kOutput, calls=%fused_computation.11 | convolution fusion | flops 4295229440 | bytes 23068672 | tf_op jit(solution)/shard_map/dot_general | solution.py:276
  319.3 6.0 %convolution_add_fusion.3 = f32[256,1024]{1,0:T(8,128)S(1)} fusion(f32[256,1024]{1,0:T(8,128)} %bitcast.65, bf16[256,8192]{1,0:T(8,128)(2,1)S(1)} %copy-done.3, bf16[8192,1024]{1,0:T(8,128)(2,1)S(1)} %bitcast.52), kind=kOutput, calls=%fused_computation.12 | convolution fusion | flops 4295229440 | bytes 23068672 | tf_op jit(solution)/shard_map/dot_general | solution.py:276
  325.3 8.3 %convolution_add_fusion = f32[256,1024]{1,0:T(8,128)S(1)} fusion(f32[256,1024]{1,0:T(8,128)S(1)} %bitcast.62, bf16[256,8192]{1,0:T(8,128)(2,1)S(1)} %copy-done.2, bf16[8192,1024]{1,0:T(8,128)(2,1)} %unpack_b.15), kind=kOutput, calls=%fused_computation.9 | convolution fusion | flops 4295229440 | bytes 23068672 | tf_op jit(solution)/shard_map/dot_general | solution.py:276
  333.6 4.6 %convolution_add_fusion.1 = f32[256,1024]{1,0:T(8,128)S(1)} fusion(f32[256,1024]{1,0:T(8,128)S(1)} %bitcast.64, bf16[256,8192]{1,0:T(8,128)(2,1)S(1)} %copy-done.2, bf16[8192,1024]{1,0:T(8,128)(2,1)S(1)} %bitcast.52), kind=kOutput, calls=%fused_computation.10 | convolution fusion | flops 4295229440 | bytes 23068672 | tf_op jit(solution)/shard_map/dot_general | solution.py:276
  338.3 2.3 maximum_maximum_fusion
  (94 shorter events, 23.0 us)
Async XLA Ops:
  6.5 9.7 %copy-start.5 = (s32[16,16]{1,0:T(8,128)S(1)}, s32[16,16]{1,0:T(8,128)}, u32[]{:S(2)}) copy-start(s32[16,16]{1,0:T(8,128)} %param.9) | copy-start | bytes 3076
  6.5 190.0 %all-gather.13.cloned.1.call-start = ((), (), s32[]{:S(2)}) async-start(), calls=%async_computation.4 | async-start | bytes 6717440 | tf_op jit(solution)/shard_map/all_gather | solution.py:246
  16.2 264.2 %all-gather.15.cloned.1.call-start = ((), (), s32[]{:S(2)}) async-start(), calls=%async_computation.5 | async-start | bytes 2785280 | tf_op jit(solution)/shard_map/all_gather | solution.py:246
  27.6 57.4 %collective-permute-start.5 = (bf16[75,128,128]{2,1,0:T(8,128)(2,1)}, bf16[75,128,128]{2,1,0:T(8,128)(2,1)S(1)}, u32[]{:S(2)}, u32[]{:S(2)}) collective-permute-start(bf16[75,128,128]{2,1,0:T(8,128)(2,1)} %get-tuple-element.28.refs_0_), channel_id=1, source_target_pairs={{0,16},{8,24},{16,0},{24,8},{1,17},{9,25},{17,1},{25,9},{2,18},{10... | collective-permute-start | bytes 7372808 | tf_op jit(solution)/shard_map/ppermute | solution.py:253
  30.6 259.8 %all-gather.17.cloned.1.call-start = ((), (), s32[]{:S(2)}) async-start(), calls=%async_computation.6 | async-start | bytes 2785280 | tf_op jit(solution)/shard_map/all_gather | solution.py:246
  30.6 97.8 %collective-permute-start.10 = (bf16[63,128,128]{2,1,0:T(8,128)(2,1)}, bf16[63,128,128]{2,1,0:T(8,128)(2,1)}, u32[]{:S(2)}, u32[]{:S(2)}) collective-permute-start(bf16[63,128,128]{2,1,0:T(8,128)(2,1)} %get-tuple-element.29.refs_1_), channel_id=1, source_target_pairs={{0,16},{8,24},{16,0},{24,8},{1,17},{9,25},{17,1},{25,9},{2,18},{10... | collective-permute-start | bytes 6193160 | tf_op jit(solution)/shard_map/ppermute | solution.py:253
  30.7 119.3 %collective-permute-start.7 = (bf16[75,128,128]{2,1,0:T(8,128)(2,1)}, bf16[75,128,128]{2,1,0:T(8,128)(2,1)}, u32[]{:S(2)}, u32[]{:S(2)}) collective-permute-start(bf16[75,128,128]{2,1,0:T(8,128)(2,1)} %get-tuple-element.28.refs_0_), channel_id=1, source_target_pairs={{0,8},{8,0},{16,24},{24,16},{1,9},{9,1},{17,25},{25,17},{2,10},{10... | collective-permute-start | bytes 7372808 | tf_op jit(solution)/shard_map/ppermute | solution.py:257
  85.0 66.4 %copy-start.1 = (bf16[75,128,128]{2,1,0:T(8,128)(2,1)}, bf16[75,128,128]{2,1,0:T(8,128)(2,1)S(1)}, u32[]{:S(2)}) copy-start(bf16[75,128,128]{2,1,0:T(8,128)(2,1)S(1)} %collective-permute-done.5.refs_0_) | copy-start | bytes 7372804
  85.0 95.9 %collective-permute-start.6 = (bf16[75,128,128]{2,1,0:T(8,128)(2,1)S(1)}, bf16[75,128,128]{2,1,0:T(8,128)(2,1)}, u32[]{:S(2)}, u32[]{:S(2)}) collective-permute-start(bf16[75,128,128]{2,1,0:T(8,128)(2,1)S(1)} %collective-permute-done.5.refs_0_), channel_id=1, source_target_pairs={{0,8},{8,0},{16,24},{24,16},{1,9},{9,1},{17,25},{25,17},{2,10},{10... | collective-permute-start | bytes 7372808 | tf_op jit(solution)/shard_map/ppermute | solution.py:257
  85.0 73.8 %collective-permute-start.12 = (bf16[63,128,128]{2,1,0:T(8,128)(2,1)}, bf16[63,128,128]{2,1,0:T(8,128)(2,1)}, u32[]{:S(2)}, u32[]{:S(2)}) collective-permute-start(bf16[63,128,128]{2,1,0:T(8,128)(2,1)} %get-tuple-element.29.refs_1_), channel_id=1, source_target_pairs={{0,8},{8,0},{16,24},{24,16},{1,9},{9,1},{17,25},{25,17},{2,10},{10... | collective-permute-start | bytes 6193160 | tf_op jit(solution)/shard_map/ppermute | solution.py:257
  128.5 60.4 %collective-permute-start.11 = (bf16[63,128,128]{2,1,0:T(8,128)(2,1)}, bf16[63,128,128]{2,1,0:T(8,128)(2,1)}, u32[]{:S(2)}, u32[]{:S(2)}) collective-permute-start(bf16[63,128,128]{2,1,0:T(8,128)(2,1)} %collective-permute-done.10.refs_1_), channel_id=1, source_target_pairs={{0,8},{8,0},{16,24},{24,16},{1,9},{9,1},{17,25},{25,17},{2,10},{10... | collective-permute-start | bytes 6193160 | tf_op jit(solution)/shard_map/ppermute | solution.py:257
  133.8 102.9 %collective-permute-start = (f32[8,128]{1,0:T(8,128)S(1)}, f32[8,128]{1,0:T(8,128)S(1)}, u32[]{:S(2)}, u32[]{:S(2)}) collective-permute-start(f32[8,128]{1,0:T(8,128)S(1)} %broadcast_in_dim.5), channel_id=1, source_target_pairs={{0,8},{8,0},{16,24},{24,16},{1,9},{9,1},{17,25},{25,17},{2,10},{10... | collective-permute-start | bytes 12296 | tf_op jit(solution)/shard_map/ppermute | solution.py:196
  197.9 26.9 %slice-start = ((s8[16777216]{0:T(1024)(128)(4,1)}), s8[4194304]{0:T(1024)(128)(4,1)S(1)}, s32[]{:S(2)}) async-start(s8[16777216]{0:T(1024)(128)(4,1)} %bitcast.49), calls=%async_computation.7 | async-start | bytes 8388608
  207.6 17.3 %slice-start.1 = ((s8[16777216]{0:T(1024)(128)(4,1)}), s8[4194304]{0:T(1024)(128)(4,1)S(1)}, s32[]{:S(2)}) async-start(s8[16777216]{0:T(1024)(128)(4,1)} %bitcast.49), calls=%async_computation.8 | async-start | bytes 8388608
  207.6 17.3 %slice-start.2 = ((s8[16777216]{0:T(1024)(128)(4,1)}), s8[4194304]{0:T(1024)(128)(4,1)S(1)}, s32[]{:S(2)}) async-start(s8[16777216]{0:T(1024)(128)(4,1)} %bitcast.49), calls=%async_computation.9 | async-start | bytes 8388608
  207.6 17.3 %slice-start.3 = ((s8[16777216]{0:T(1024)(128)(4,1)}), s8[4194304]{0:T(1024)(128)(4,1)S(1)}, s32[]{:S(2)}) async-start(s8[16777216]{0:T(1024)(128)(4,1)} %bitcast.49), calls=%async_computation.10 | async-start | bytes 8388608
  223.0 81.5 %collective-permute-start.13 = (s16[4,128,1024]{2,1,0:T(8,128)(2,1)S(1)}, s16[4,128,1024]{2,1,0:T(8,128)(2,1)S(1)}, u32[]{:S(2)}, u32[]{:S(2)}) collective-permute-start(s16[4,128,1024]{2,1,0:T(8,128)(2,1)S(1)} %round-nearest-even_convert_fusion), channel_id=1, source_target_pairs={{0,1},{1,0},{2,3},{3,2},{4,5},{5,4},{6,7},{7,6},{8,9},{9,8},{10,11... | collective-permute-start | bytes 3145736 | tf_op jit(solution)/shard_map/ppermute | solution.py:286
  236.4 70.1 %collective-permute-start.8 = (s16[4,128,1024]{2,1,0:T(8,128)(2,1)S(1)}, s16[4,128,1024]{2,1,0:T(8,128)(2,1)}, u32[]{:S(2)}, u32[]{:S(2)}) collective-permute-start(s16[4,128,1024]{2,1,0:T(8,128)(2,1)S(1)} %round-nearest-even_convert_fusion.1), channel_id=1, source_target_pairs={{0,1},{1,0},{2,3},{3,2},{4,5},{5,4},{6,7},{7,6},{8,9},{9,8},{10,11... | collective-permute-start | bytes 3145736 | tf_op jit(solution)/shard_map/ppermute | solution.py:286
  236.8 3.6 %collective-permute-start.1 = (f32[8,128]{1,0:T(8,128)S(1)}, f32[8,128]{1,0:T(8,128)S(1)}, u32[]{:S(2)}, u32[]{:S(2)}) collective-permute-start(f32[8,128]{1,0:T(8,128)S(1)} %broadcast_maximum_fusion), channel_id=1, source_target_pairs={{0,16},{8,24},{16,0},{24,8},{1,17},{9,25},{17,1},{25,9},{2,18},{10... | collective-permute-start | bytes 12296 | tf_op jit(solution)/shard_map/ppermute | solution.py:196
  238.5 65.9 %collective-permute-start.14 = (f32[4,1,1024]{2,0,1:T(4,128)S(1)}, f32[4,1,1024]{2,0,1:T(4,128)S(1)}, u32[]{:S(2)}, u32[]{:S(2)}) collective-permute-start(f32[4,1,1024]{2,0,1:T(4,128)S(1)} %get-tuple-element.40), channel_id=1, source_target_pairs={{0,1},{1,0},{2,3},{3,2},{4,5},{5,4},{6,7},{7,6},{8,9},{9,8},{10,11... | collective-permute-start | bytes 49160 | tf_op jit(solution)/shard_map/ppermute | solution.py:286
  240.4 30.7 %collective-permute-start.2 = (f32[8,128]{1,0:T(8,128)S(1)}, f32[8,128]{1,0:T(8,128)S(1)}, u32[]{:S(2)}, u32[]{:S(2)}) collective-permute-start(f32[8,128]{1,0:T(8,128)S(1)} %fusion.21), channel_id=1, source_target_pairs={{0,1},{1,0},{2,3},{3,2},{4,5},{5,4},{6,7},{7,6},{8,9},{9,8},{10,11... | collective-permute-start | bytes 12296 | tf_op jit(solution)/shard_map/ppermute | solution.py:196
  271.1 3.6 %collective-permute-start.3 = (f32[8,128]{1,0:T(8,128)S(1)}, f32[8,128]{1,0:T(8,128)S(1)}, u32[]{:S(2)}, u32[]{:S(2)}) collective-permute-start(f32[8,128]{1,0:T(8,128)S(1)} %max.17), channel_id=1, source_target_pairs={{0,2},{2,0},{4,6},{6,4},{1,3},{3,1},{5,7},{7,5},{8,10},{10,8},{12,... | collective-permute-start | bytes 12296 | tf_op jit(solution)/shard_map/ppermute | solution.py:196
  274.7 4.5 %collective-permute-start.4 = (f32[8,128]{1,0:T(8,128)S(1)}, f32[8,128]{1,0:T(8,128)S(1)}, u32[]{:S(2)}, u32[]{:S(2)}) collective-permute-start(f32[8,128]{1,0:T(8,128)S(1)} %max.18), channel_id=1, source_target_pairs={{0,4},{2,6},{4,0},{6,2},{1,5},{3,7},{5,1},{7,3},{8,12},{10,14},{12... | collective-permute-start | bytes 12296 | tf_op jit(solution)/shard_map/ppermute | solution.py:196
  302.7 3.7 %collective-permute-start.9 = (f32[4,1,1024]{2,0,1:T(4,128)S(1)}, f32[4,1,1024]{2,0,1:T(4,128)S(1)}, u32[]{:S(2)}, u32[]{:S(2)}) collective-permute-start(f32[4,1,1024]{2,0,1:T(4,128)S(1)} %get-tuple-element.38), channel_id=1, source_target_pairs={{0,1},{1,0},{2,3},{3,2},{4,5},{5,4},{6,7},{7,6},{8,9},{9,8},{10,11... | collective-permute-start | bytes 49160 | tf_op jit(solution)/shard_map/ppermute | solution.py:286
  305.0 4.3 %copy-start.3 = (bf16[256,8192]{1,0:T(8,128)(2,1)S(1)}, bf16[256,8192]{1,0:T(8,128)(2,1)}, u32[]{:S(2)}) copy-start(bf16[256,8192]{1,0:T(8,128)(2,1)} %unpack_a.3) | copy-start | bytes 12582916
  308.1 11.2 %slice-start.4 = ((s8[16777216]{0:T(1024)(128)(4,1)}), s8[4194304]{0:T(1024)(128)(4,1)S(1)}, s32[]{:S(2)}) async-start(s8[16777216]{0:T(1024)(128)(4,1)} %bitcast.51), calls=%async_computation.11 | async-start | bytes 8388608
  309.2 10.1 %slice-start.5 = ((s8[16777216]{0:T(1024)(128)(4,1)}), s8[4194304]{0:T(1024)(128)(4,1)S(1)}, s32[]{:S(2)}) async-start(s8[16777216]{0:T(1024)(128)(4,1)} %bitcast.51), calls=%async_computation.12 | async-start | bytes 8388608
  309.2 10.1 %slice-start.6 = ((s8[16777216]{0:T(1024)(128)(4,1)}), s8[4194304]{0:T(1024)(128)(4,1)S(1)}, s32[]{:S(2)}) async-start(s8[16777216]{0:T(1024)(128)(4,1)} %bitcast.51), calls=%async_computation.13 | async-start | bytes 8388608
  309.2 10.1 %slice-start.7 = ((s8[16777216]{0:T(1024)(128)(4,1)}), s8[4194304]{0:T(1024)(128)(4,1)S(1)}, s32[]{:S(2)}) async-start(s8[16777216]{0:T(1024)(128)(4,1)} %bitcast.51), calls=%async_computation.14 | async-start | bytes 8388608
  319.3 6.0 %copy-start.2 = (bf16[256,8192]{1,0:T(8,128)(2,1)S(1)}, bf16[256,8192]{1,0:T(8,128)(2,1)}, u32[]{:S(2)}) copy-start(bf16[256,8192]{1,0:T(8,128)(2,1)} %unpack_a.5) | copy-start | bytes 12582916
  333.6 4.6 %copy-start.4 = (f32[256,1024]{1,0:T(8,128)S(1)}, f32[256,1024]{1,0:T(8,128)}, u32[]{:S(2)}) copy-start(f32[256,1024]{1,0:T(8,128)} %convolution_add_fusion.2) | copy-start | bytes 3145732
  338.2 2.3 copy-start.6
  (1 other events, 2.3 us)
Sparse Core Ops, SparseCore 0:
  16.3 102.8 all-gather.12
  120.9 46.6 all-gather.14
  169.3 47.1 all-gather.16

commit v2 on v0

v2 whole, which is shorter than its diff:
```python
import functools
import math
import typing

import jax
import jax.numpy as jnp
from jax import lax
from jax.experimental import pallas as pl
from jax.experimental.pallas import tpu as pltpu
from jax.sharding import PartitionSpec as P

BLOCK = 128
VMEM_LIMIT = 56 * 1024 * 1024
TILE_ROOM = 256 * 16
SMALL = pl.CostEstimate(flops=1, bytes_accessed=1, transcendentals=0)
LARGE = pl.CostEstimate(flops=10**12, bytes_accessed=1, transcendentals=0)


def keep_blocks(values, occupancy):
    height, breadth = values.shape
    tiled = values.reshape(height // BLOCK, BLOCK, breadth // BLOCK, BLOCK)
    flags = occupancy.astype(values.dtype)
    return (tiled * flags[:, None, :, None]).reshape(height, breadth)


def whole_slab(a_tiles, a_occupancy, b_tiles, b_occupancy):
    a_kept = keep_blocks(a_tiles, a_occupancy)
    b_kept = keep_blocks(b_tiles, b_occupancy)
    partial_value = jnp.dot(
        lax.all_gather(a_kept, "col", axis=1, tiled=True),
        lax.all_gather(b_kept, "row", axis=0, tiled=True),
        preferred_element_type=jnp.float32,
    )
    return lax.psum_scatter(partial_value, "layer", scatter_dimension=0, tiled=True)


def slots_for(blocks, spread):
    if blocks < 16:
        return blocks + 1
    room = (blocks * 7 + 15) // 16 + int(round(spread * blocks**0.5))
    return min(blocks, room) + 1


def cuts_for(stages, spread):
    cuts, blocks = [0], 0
    for stage in stages:
        blocks += stage.rows * stage.wide
        cuts.append(max(slots_for(blocks, spread), cuts[-1] + 1))
    return cuts


class Stage(typing.NamedTuple):
    row: int
    rows: int
    first: int
    wide: int


def header_of(occupancy):
    rows, columns = occupancy.shape
    flags = occupancy.astype(jnp.bfloat16)
    return jnp.pad(flags, ((0, BLOCK - rows), (0, BLOCK - columns)))


def mark_row(i):
    return BLOCK - 16 * (i + 1)


def pack_kernel(place, stages, ends, cuts, other, turn_ref, flags_ref, other_ref, header_ref, values_ref, *refs):
    parts, (over_out, held, sem, out_sems) = refs[: len(cuts) - 1], refs[-4:]
    header = pltpu.make_async_copy(header_ref, held.at[0], sem)
    header.start()

    def step_of(stage):
        def step(u, slot):
            row, column = place(stage, u, turn_ref[0])
            flag = flags_ref[row, column]

            @pl.when(flag > 0)
            def _():
                pltpu.make_async_copy(
                    values_ref.at[
                        pl.ds(pl.multiple_of(row * BLOCK, BLOCK), BLOCK),
                        pl.ds(pl.multiple_of(column * BLOCK, BLOCK), BLOCK),
                    ],
                    held.at[jnp.minimum(slot, cuts[-1])],
                    sem,
                ).start()

            return slot + flag

        return step

    slot, over, marks = jnp.int32(1), jnp.int32(0), []
    for stage, cut in zip(stages, ends[1:]):
        marks.append(slot)
        slot = lax.fori_loop(0, stage.rows * stage.wide, step_of(stage), slot, unroll=4)
        over = jnp.maximum(over, jnp.where(slot > cut, 1, 0))
    if other is not None:
        other_place, other_stages, other_ends = other
        spent = jnp.int32(1)
        for stage, cut in zip(other_stages, other_ends[1:]):

            def count(u, spent):
                row, column = other_place(stage, u, turn_ref[0])
                return spent + other_ref[row, column]

            spent = lax.fori_loop(0, stage.rows * stage.wide, count, spent, unroll=16)
            over = jnp.maximum(over, jnp.where(spent > cut, 1, 0))

    def settle(t, _):
        header.wait()
        return 0

    lax.fori_loop(0, slot, settle, 0)
    for i, mark in enumerate([over, *marks]):
        row = mark_row(i)
        held[0, row : row + 16, :] = jnp.full((16, BLOCK), mark.astype(jnp.float32)).astype(held.dtype)
    over_out[0] = over
    copies = [
        pltpu.make_async_copy(held.at[pl.ds(lo, hi - lo)], part, out_sems.at[i])
        for i, (part, lo, hi) in enumerate(zip(parts, cuts[:-1], cuts[1:]))
    ]
    for copy in copies:
        copy.start()
    for copy in copies:
        copy.wait()


def pack(values, occupancy, turn, place, stages, ends, cuts, other_flags, other):
    *parts, done = pl.pallas_call(
        functools.partial(pack_kernel, place, stages, ends, cuts, other),
        grid_spec=pltpu.PrefetchScalarGridSpec(
            num_scalar_prefetch=3,
            grid=(),
            in_specs=[pl.BlockSpec(memory_space=pl.ANY)] * 2,
            out_specs=[pl.BlockSpec(memory_space=pl.ANY)] * (len(cuts) - 1)
            + [pl.BlockSpec(memory_space=pltpu.SMEM)],
            scratch_shapes=[
                pltpu.VMEM((cuts[-1] + 1, BLOCK, BLOCK), values.dtype),
                pltpu.SemaphoreType.DMA,
                pltpu.SemaphoreType.DMA((len(cuts) - 1,)),
            ],
        ),
        out_shape=[
            jax.ShapeDtypeStruct((hi - lo, BLOCK, BLOCK), values.dtype) for lo, hi in zip(cuts[:-1], cuts[1:])
        ]
        + [jax.ShapeDtypeStruct((1,), jnp.int32)],
        compiler_params=pltpu.CompilerParams(vmem_limit_bytes=VMEM_LIMIT),
        cost_estimate=SMALL,
        name="pack",
    )(turn, occupancy, other_flags, header_of(occupancy), values)
    return parts, done


def load_list(parts, cuts, held, sems):
    return [
        pltpu.make_async_copy(part, held.at[pl.ds(lo, hi - lo)], sems.at[i])
        for i, (part, lo, hi) in enumerate(zip(parts, cuts[:-1], cuts[1:]))
    ]


def unpack_b_kernel(k_blocks, first, stop, cuts, shard_ref, flags_ref, *refs):
    parts, (out_ref, done_ref, held, sems, sem) = refs[: len(cuts) - 1], refs[-5:]
    done_ref[0] = 0
    nothing = cuts[-1]
    copies = load_list(parts, cuts, held, sems)
    for copy in copies:
        copy.start()
    held[nothing] = jnp.zeros_like(held[nothing])

    def flag_of(t):
        return flags_ref[t % k_blocks, t // k_blocks]

    slot = lax.fori_loop(0, first * k_blocks, lambda t, slot: slot + flag_of(t), jnp.int32(1), unroll=8)
    for copy in copies:
        copy.wait()
    base = shard_ref[0] * k_blocks

    def step(t, slot):
        flag = flag_of(first * k_blocks + t)
        pltpu.make_async_copy(
            held.at[jnp.where(flag > 0, jnp.minimum(slot, nothing), nothing)],
            out_ref.at[
                pl.ds(pl.multiple_of((base + t % k_blocks) * BLOCK, BLOCK), BLOCK),
                pl.ds(pl.multiple_of(t // k_blocks * BLOCK, BLOCK), BLOCK),
            ],
            sem,
        ).start()
        return slot + flag

    lax.fori_loop(0, (stop - first) * k_blocks, step, slot, unroll=8)
    written = out_ref.at[pl.ds(pl.multiple_of(base * BLOCK, BLOCK), k_blocks * BLOCK)]
    pltpu.make_async_copy(written, written, sem).wait()


def unpack_b(parts, flags, shard, shards, first, stop, k_blocks, cuts, into):
    n = len(parts)
    operands = [*parts] + ([] if into is None else [into])
    return pl.pallas_call(
        functools.partial(unpack_b_kernel, k_blocks, first, stop, cuts),
        grid_spec=pltpu.PrefetchScalarGridSpec(
            num_scalar_prefetch=2,
            grid=(),
            in_specs=[pl.BlockSpec(memory_space=pl.ANY)] * len(operands),
            out_specs=[pl.BlockSpec(memory_space=pl.ANY), pl.BlockSpec(memory_space=pltpu.SMEM)],
            scratch_shapes=[
                pltpu.VMEM((cuts[-1] + 1, BLOCK, BLOCK), parts[0].dtype),
                pltpu.SemaphoreType.DMA((n,)),
                pltpu.SemaphoreType.DMA,
            ],
        ),
        out_shape=[
            jax.ShapeDtypeStruct((shards * k_blocks * BLOCK, (stop - first) * BLOCK), parts[0].dtype),
            jax.ShapeDtypeStruct((1,), jnp.int32),
        ],
        input_output_aliases={} if into is None else {2 + n: 0},
        compiler_params=pltpu.CompilerParams(vmem_limit_bytes=VMEM_LIMIT),
        cost_estimate=SMALL,
        name="unpack_b",
    )(shard, flags, *operands)


def multiply_kernel(plan, turn_ref, column_ref, flags_ref, marks_ref, *refs):
    place, stages, blocks, cuts, shards, halves, given, carried, final, starts, ends = plan
    stage = stages[-1]
    rows, wide = stage.rows, stage.wide
    n = len(cuts) - 2
    gathered_ref, refs = refs[0], refs[1:]
    lists = [refs[s * n : (s + 1) * n] for s in range(shards)]
    refs = refs[shards * n :]
    b_refs, refs = refs[:halves], refs[halves:]
    codes_in, refs = refs[: 2 * halves * given], refs[2 * halves * given :]
    before, refs = refs[:carried], refs[carried:]
    outs, (dense, sem, total) = refs[:-3], refs[-3:]
    turn = turn_ref[0]

    def fill():
        dense[...] = jnp.zeros_like(dense)
        started = jnp.int32(0)
        for s in range(shards):
            column = column_ref[s]
            parts = [gathered_ref.at[column], *lists[s]]

            def flag_of(stage, u):
                row, k = place(stage, u, turn)
                return flags_ref[column * blocks + row, k]

            def step(u, slot):
                flag = flag_of(stage, u)
                target = dense.at[
                    pl.ds(pl.multiple_of(u // wide * BLOCK, BLOCK), BLOCK),
                    pl.ds(pl.multiple_of((column * wide + u % wide) * BLOCK, BLOCK), BLOCK),
                ]
                for part, lo, hi in zip(parts, cuts[:-1], cuts[1:]):

                    @pl.when((flag > 0) & (slot >= lo) & (slot < hi))
                    def _():
                        pltpu.make_async_copy(part.at[slot - lo], target, sem).start()

                return slot + flag

            slot = marks_ref[column, mark_row(len(stages))]
            end = lax.fori_loop(0, rows * wide, step, slot, unroll=4)
            started += jnp.minimum(end, cuts[-1]) - jnp.minimum(slot, cuts[-1])

        def settle(t, _):
            pltpu.make_async_copy(gathered_ref.at[0, 0], dense.at[:BLOCK, :BLOCK], sem).wait()
            return 0

        lax.fori_loop(0, started, settle, 0)

    pl.when(pl.program_id(0) == 0)(fill)

    def finish(value, h):
        if not final:
            codes_ref, factors_ref = outs
            for r in range(rows):
                span = slice(r * BLOCK, (r + 1) * BLOCK)
                top = jnp.max(jnp.abs(value[span]), axis=0, keepdims=True)
                factor = jnp.where(top > 0, 32767.0 / top, 0.0)
                codes_ref[span] = jnp.round(value[span] * factor).astype(jnp.int32).astype(jnp.int16)
                factors_ref[r] = top * (1.0 / 32767.0)
            return
        (out_ref,) = outs
        for r in range(rows):
            span = slice(r * BLOCK, (r + 1) * BLOCK)
            some = value[span]
            for q in range(given):
                codes, factors = codes_in[2 * (q * halves + h) : 2 * (q * halves + h) + 2]
                some += codes[span].astype(jnp.int32).astype(jnp.float32) * factors[r]
            for earlier in before:
                some += earlier[span]
            out_ref[span] = some

    for h, b_ref in enumerate(b_refs):

        @pl.when((pl.program_id(0) >= starts[h]) & (pl.program_id(0) < ends[h]))
        def _():
            b_here = b_ref[...].reshape(-1, b_ref.shape[-1])
            total[...] = jnp.dot(dense[...], b_here, preferred_element_type=jnp.float32)
            finish(total, h)


def multiply(gathered, lists, flags, marks, turn, columns, place, stages, k_blocks, cuts, b_halves, final, cost, received=(), before=()):
    shards, halves = len(lists), len(b_halves)
    stage = stages[-1]
    n = len(cuts) - 2
    widths = [b_half.shape[1] for b_half in b_halves]
    shared = math.gcd(*widths)
    tile = max(t for t in (BLOCK, 256, 512) if shared % t == 0 and t * stage.wide <= TILE_ROOM)
    ends = [sum(widths[: h + 1]) // tile for h in range(halves)]
    starts = [0] + ends[:-1]
    deep = math.gcd(math.gcd(stage.first, stage.wide), k_blocks)
    layers, skip = stage.wide // deep, stage.first // deep
    assert skip % layers == 0
    tall = stage.rows * BLOCK
    whole = pl.BlockSpec(memory_space=pl.ANY)

    def at(h, *fixed):
        return lambda j, *_: (*fixed, jnp.clip(j - starts[h], 0, ends[h] - starts[h] - 1))

    in_specs = [whole] * (1 + shards * n)
    operands = [gathered] + [p for parts in lists for p in parts[:n]]
    for h, b_half in enumerate(b_halves):
        in_specs.append(pl.BlockSpec((shards, layers, deep * BLOCK, tile), at(h, 0, skip // layers, 0)))
        operands.append(b_half.reshape(shards, k_blocks // deep, deep * BLOCK, widths[h]))
    for pairs in received:
        for h, (codes, factors) in enumerate(pairs):
            in_specs.append(pl.BlockSpec((tall, tile), at(h, 0)))
            in_specs.append(pl.BlockSpec((stage.rows, 1, tile), at(h, 0, 0)))
            operands += [codes, factors]
    in_specs += [pl.BlockSpec((tall, tile), lambda j, *_: (0, j))] * len(before)
    operands += [*before]
    out_specs = [pl.BlockSpec((tall, tile), lambda j, *_: (0, j))]
    if final:
        out_shape = [jax.ShapeDtypeStruct((tall, sum(widths)), jnp.float32)]
    else:
        out_specs.append(pl.BlockSpec((stage.rows, 1, tile), lambda j, *_: (0, 0, j)))
        out_shape = [
            jax.ShapeDtypeStruct((tall, sum(widths)), jnp.int16),
            jax.ShapeDtypeStruct((stage.rows, 1, sum(widths)), jnp.float32),
        ]
    blocks = flags.shape[0] // shards
    plan = (place, stages, blocks, cuts, shards, halves, len(received), len(before), final, starts, ends)
    return pl.pallas_call(
        functools.partial(multiply_kernel, plan),
        grid_spec=pltpu.PrefetchScalarGridSpec(
            num_scalar_prefetch=4,
            grid=(ends[-1],),
            in_specs=in_specs,
            out_specs=out_specs,
            scratch_shapes=[
                pltpu.VMEM((tall, shards * stage.wide * BLOCK), b_halves[0].dtype),
                pltpu.SemaphoreType.DMA,
                pltpu.VMEM((tall, tile), jnp.float32),
            ],
        ),
        out_shape=out_shape,
        compiler_params=pltpu.CompilerParams(vmem_limit_bytes=VMEM_LIMIT),
        cost_estimate=cost,
        name="multiply",
    )(turn, columns, flags, marks, *operands)


def largest_over(value, axis, size, step=1, stop=None):
    while step < (stop or size):
        value = jnp.maximum(value, lax.ppermute(value, axis, [(i, i ^ step) for i in range(size)]))
        step *= 2
    return value


def after(value, *others):
    return lax.optimization_barrier((value, *others))[0]


def per_device(sizes, a_tiles, a_occupancy, b_tiles, b_occupancy):
    rows, cols, layers = sizes
    me_row, me_col, me_layer = (lax.axis_index(axis).astype(jnp.int32) for axis in ("row", "col", "layer"))
    a_rows, a_k = a_occupancy.shape
    b_k, b_columns = b_occupancy.shape
    piece = a_rows // layers
    given = a_rows - piece
    turn = me_layer.reshape(1)

    def a_place(stage, u, layer):
        row, k = stage.row + u // stage.wide, stage.first + u % stage.wide
        return lax.rem(row + (layer + 1) * piece, a_rows), k

    def b_place(stage, u, _):
        return stage.first + u % stage.wide, stage.row + u // stage.wide

    early = a_k * 3 // 4
    a_stages = [
        stage
        for stage in (
            Stage(0, given, 0, a_k),
            Stage(given, piece, 0, early),
            Stage(given, piece, early, a_k - early),
        )
        if stage.rows * stage.wide
    ]
    half = b_columns * 5 // 8
    b_stages = [Stage(0, half, 0, b_k), Stage(half, b_columns - half, 0, b_k)]
    a_cuts, b_ends = cuts_for(a_stages, 1.77), cuts_for(b_stages, 2.0)
    b_cuts = sorted({*b_ends, (b_ends[1] + b_ends[2] + 1) // 2})
    b_counts = [b_cuts.index(end) for end in b_ends[1:]]

    a_parts, done = pack(
        a_tiles, a_occupancy, turn, a_place, a_stages, a_cuts, a_cuts, b_occupancy, (b_place, b_stages, b_ends)
    )
    gathered = lax.all_gather(a_parts[0], "col", axis=0)
    b_parts, done = pack(
        b_tiles, b_occupancy, after(turn, done), b_place, b_stages, b_ends, b_cuts, b_occupancy, None
    )

    pair = 2 if rows % 2 == 0 else 1
    swap = [(r, r ^ 1) for r in range(rows)]
    b_dense = [None] * len(b_stages)

    def unpack(h, shard, lists, done):
        stage = b_stages[h]
        flags = lists[0][0, :b_k, :b_columns].astype(jnp.int32)
        b_dense[h], done = unpack_b(
            lists[: b_counts[h]], flags, after(shard.reshape(1), done), rows, stage.row, stage.row + stage.rows, b_k,
            b_cuts[: b_counts[h] + 1], b_dense[h],
        )
        return done

    def across(part, hop):
        return lax.ppermute(part, "row", [(r, (r + pair * hop) % rows) for r in range(rows)])

    hops = range(1, rows // pair)
    shards = [lax.rem(me_row - pair * hop + rows, rows) for hop in range(rows // pair)]
    came = {(0, hop): across(b_parts[0], hop) for hop in hops}
    lists = {0: b_parts}
    if pair == 2:
        lists[1] = [lax.ppermute(part, "row", swap) for part in b_parts]
    for side in range(pair):
        for h in range(len(b_stages)):
            done = unpack(h, shards[0] ^ side, lists[side], done)
    sides = {}
    for hop in hops:
        here = after(came[0, hop], done)
        sides[hop] = [[here], [lax.ppermute(here, "row", swap)]][:pair]
        for i in range(1, len(b_parts)):
            came[i, hop] = across(after(b_parts[i], here), hop)
    for side in range(pair):
        for hop in hops:
            done = unpack(0, shards[hop] ^ side, sides[hop][side], done)

    a_lists = [[] for _ in range(cols)]
    waits = [done] * cols
    for part in a_parts[1:]:
        a_lists[0].append(part)
        for hop in range(1, cols):
            there = [(c, (c + hop) % cols) for c in range(cols)]
            waits[hop] = lax.ppermute(after(part, waits[hop], gathered), "col", there)
            a_lists[hop].append(waits[hop])
    a_columns = lax.rem(me_col - jnp.arange(cols, dtype=jnp.int32) + cols, cols)
    a_flags = gathered[:, 0, :a_rows, :a_k].astype(jnp.int32).reshape(cols * a_rows, a_k)

    a_marks = gathered[:, 0, :, 0].astype(jnp.int32)

    def product_of(g, halves, done, **more):
        return multiply(
            gathered, a_lists, a_flags, a_marks, after(turn, done), a_columns, a_place, a_stages[: g + 1], a_k, a_cuts[: g + 2],
            halves, **more
        )

    over = jnp.max(gathered[:, 0, mark_row(0) : mark_row(0) + 8].astype(jnp.float32), axis=0)
    over = largest_over(over, "layer", layers)

    received = [[] for _ in range(layers - 1)]
    for h in range(len(b_stages)):
        if h:
            for hop in hops:
                here = [after(came[i, hop], done) for i in range(1, b_counts[h])]
                there = [lax.ppermute(part, "row", swap) for part in here]
                for side, more in zip(range(pair), (here, there)):
                    done = unpack(h, shards[hop] ^ side, sides[hop][side] + more, done)
        codes, factors = product_of(0, [b_dense[h]], done, final=False, cost=SMALL if h else LARGE)
        done = factors
        over = largest_over(after(over, done), "row", rows, 1 << h, 2 << h if h + 1 < len(b_stages) else rows)
        for q in range(layers - 1):
            there = [(i, (i + 1 + q) % layers) for i in range(layers)]
            own = codes[q * piece * BLOCK : (q + 1) * piece * BLOCK], factors[q * piece : (q + 1) * piece]
            received[q].append(tuple(lax.ppermute(x, "layer", there) for x in own))

    (product,) = product_of(1, b_dense, done, final=True, cost=LARGE)
    for g in range(2, len(a_stages)):
        last = g == len(a_stages) - 1
        (product,) = product_of(
            g, b_dense, done, final=True, cost=SMALL, received=received if last else (), before=(product,)
        )
    return lax.cond(
        over[0, 0] > 0,
        lambda: whole_slab(a_tiles, a_occupancy, b_tiles, b_occupancy),
        lambda: product,
    )


def solution(mesh):
    sizes = tuple(mesh.shape[axis] for axis in ("row", "col", "layer"))
    in_specs = (
        P("row", ("layer", "col")),
        P("row", ("layer", "col")),
        P(("layer", "row"), "col"),
        P(("layer", "row"), "col"),
    )
    out_specs = P(("row", "layer"), "col")
    return jax.shard_map(
        functools.partial(per_device, sizes), mesh=mesh, in_specs=in_specs, out_specs=out_specs, check_vma=False
    )
```

time: 653 us -> 268 us (0.41)
  waiting for transfers between devices: 581 us -> 70.7 us
  Pallas kernels: 0 us -> 140 us
  matrix products: 43.3 us -> 0 us
  starting transfers between devices: 0.09 us -> 27.3 us
    all_gather x2 -> x1, waiting for transfers between devices: 482 us -> 0.02 us  [per_device(): gathered = lax.all_gather(a_parts[0], 'col', axis=0)]
    pallas_call x0 -> x14, Pallas kernels: none -> 140 us  [the longest x4 78.6 us: multiply(): pl.pallas_call(functools.partial(multiply_kernel, plan), grid_spec=pltpu....]
    reduce_scatter x1 -> x0, waiting for transfers between devices: 99.4 us -> none  [per_device(): lax.psum_scatter(partial_value, 'layer', scatter_dimension=0, tiled=True)]
    ppermute x0 -> x22, waiting for transfers between devices: none -> 70.7 us  [the longest x3 54.3 us: across(): lax.ppermute(part, 'row', [(r, (r + pair * hop) % rows) for r in range(ro...]
    dot_general x1 -> x0, matrix products: 43.3 us -> none  [per_device(): jnp.dot(lax.all_gather(a_kept, 'col', axis=1, tiled=True), b_slab, prefer...]
    ppermute x0 -> x22, starting transfers between devices: none -> 27.3 us  [the longest x6 13.7 us: per_device(): waits[hop] = lax.ppermute(after(part, waits[hop], gathered), 'col', there)]
    mul x2 -> x0, other arithmetic: 12.8 us -> none  [keep_blocks(): return (tiled * flags[:, None, :, None]).reshape(height, breadth)]
    convert_element_type x2 -> x8, other arithmetic: 0.69 us -> 8.02 us  [the longest x4 4.43 us: unpack(): flags = lists[0][0, :b_k, :b_columns].astype(jnp.int32)]
  transfers between devices with their start and end apart: 3 -> 23, of which waited for: 3 -> 5; matrix products, arithmetic and copies ran while one was open for 1% -> 4% of each run, Pallas kernels for 0% -> 44%
where the time goes in v2:
time: 268 us; the launch traced here: 266 us
  Pallas kernels  140 us (52%)
  waiting for transfers between devices  70.7 us (26%)
  starting transfers between devices  27.3 us (10%)
  between operations  14.4 us (5%)
  other arithmetic  10.6 us (4%)
  local copies, waits for them, and re-layouts  3.28 us (1%)
    pallas_call x4, Pallas kernels, multiply(): pl.pallas_call(functools.partial(multiply_kernel, plan), grid_spec=pltpu....  78.6 us
    ppermute x3, waiting for transfers between devices, across(): lax.ppermute(part, 'row', [(r, (r + pair * hop) % rows) for r in range(ro...  54.3 us
    pallas_call x8, Pallas kernels, unpack_b(): pl.pallas_call(functools.partial(unpack_b_kernel, k_blocks, first, stop,...  46.1 us
    pallas_call x2, Pallas kernels, pack(): pl.pallas_call(functools.partial(pack_kernel, place, stages, ends, cuts,...  14.8 us
    ppermute x6, starting transfers between devices, per_device(): waits[hop] = lax.ppermute(after(part, waits[hop], gathered), 'col', there)  13.7 us
    ppermute x4, waiting for transfers between devices, per_device(): received[q].append(tuple((lax.ppermute(x, 'layer', there) for x in own)))  11 us
  transfers between devices with their start and end apart: 23, of which 5 were waited for; matrix products, arithmetic and copies ran while one was open for 4% of the time, Pallas kernels for 44%

profile of v2, /device:TPU:0, one launch (start us, length us, event | category | flops | bytes accessed | tf_op | source)
XLA Modules:
  0.0 265.8 jit_solution(3646066952490184819)
XLA Ops:
  7.9 7.1 %pack.2 = (bf16[43,128,128]{2,1,0:T(8,128)(2,1)}, bf16[26,128,128]{2,1,0:T(8,128)(2,1)}, bf16[8,128,128]{2,1,0:T(8,128)(2,1)}, s32[1]{0:T(128)}) custom-call(s32[1]{0:T(128)} %bitcast.turn_ref, s32[8,16]{1,0:T(8,128)} %flags_ref.2, s32[16,16]{1,0:T(8,128)} %other_ref.3, bf16[128,128]{1,0:T(8,128)(2,1)} %pad.8.header_ref, bf16[1024,2048]{1,0:T(8,128)(2,1)} %values_ref.2), custom_call_target="tpu_custom_call" | custom-call | flops 1 | bytes 1 | tf_op jit(solution)/shard_map/pack/pallas_call | solution.py:131
  15.7 7.7 %pack.3 = (bf16[96,128,128]{2,1,0:T(8,128)(2,1)}, bf16[25,128,128]{2,1,0:T(8,128)(2,1)}, bf16[24,128,128]{2,1,0:T(8,128)(2,1)}, s32[1]{0:T(128)}) custom-call(s32[1]{0:T(128)} %bitcast.turn_ref, s32[16,16]{1,0:T(8,128)S(1)} %copy-done.5, s32[16,16]{1,0:T(8,128)S(1)} %copy-done.5, bf16[128,128]{1,0:T(8,128)(2,1)} %pad.9.header_ref, bf16[2048,2048]{1,0:T(8,128)(2,1)} %values_ref.3), custom_call_target="tpu_custom_call" | custom-call | flops 1 | bytes 1 | tf_op jit(solution)/shard_map/pack/pallas_call | solution.py:131
  23.9 2.6 collective-permute-start.1
  27.0 1.3 bitcast_convert_fusion.1.flags_ref
  28.3 5.8 %unpack_b.8 = (bf16[8192,768]{1,0:T(8,128)(2,1)}, s32[1]{0:T(128)}) custom-call(s32[1]{0:T(128)} %bitcast.5.shard_ref, s32[16,16]{1,0:T(8,128)} %bitcast_convert_fusion.1.flags_ref, bf16[96,128,128]{2,1,0:T(8,128)(2,1)} %get-tuple-element.57.refs_0_, bf16[25,128,128]{2,1,0:T(8,128)(2,1)} %get-tuple-element.72.refs_1_, ...), custom_call_target="tpu_custom_call" | custom-call | flops 1 | bytes 1 | tf_op jit(solution)/shard_map/unpack_b/pallas_call | solution.py:200
  35.3 5.8 %unpack_b.9 = (bf16[8192,768]{1,0:T(8,128)(2,1)}, s32[1]{0:T(128)}) custom-call(s32[1]{0:T(128)} %bitcast.3.shard_ref, s32[16,16]{1,0:T(8,128)} %fusion.2.flags_ref, bf16[96,128,128]{2,1,0:T(8,128)(2,1)} %collective-permute-done.2.refs_0_, bf16[25,128,128]{2,1,0:T(8,128)(2,1)} %collective-permute-done.3.refs_1_, ...), custom_call_target="tpu_custom_call", output_to_operand_aliasing={{0}: (5, {})} | custom-call | flops 1 | bytes 1 | tf_op jit(solution)/shard_map/unpack_b/pallas_call | solution.py:200
  41.1 54.3 %collective-permute-done.1.refs_0_ = bf16[96,128,128]{2,1,0:T(8,128)(2,1)S(1)} collective-permute-done((bf16[96,128,128]{2,1,0:T(8,128)(2,1)}, bf16[96,128,128]{2,1,0:T(8,128)(2,1)S(1)}, u32[]{:S(2)}, u32[]{:S(2)}) %collective-permute-start.1) | collective-permute-done | bytes 3145760 | tf_op jit(solution)/shard_map/ppermute | solution.py:431
  95.4 6.0 %unpack_b.10 = (bf16[8192,1280]{1,0:T(8,128)(2,1)}, s32[1]{0:T(128)}) custom-call(s32[1]{0:T(128)} %bitcast.5.shard_ref, s32[16,16]{1,0:T(8,128)} %bitcast_convert_fusion.1.flags_ref, bf16[96,128,128]{2,1,0:T(8,128)(2,1)} %get-tuple-element.57.refs_0_), custom_call_target="tpu_custom_call" | custom-call | flops 1 | bytes 1 | tf_op jit(solution)/shard_map/unpack_b/pallas_call | solution.py:200
  101.9 1.8 collective-permute-start.9
  104.0 5.8 %unpack_b.11 = (bf16[8192,1280]{1,0:T(8,128)(2,1)}, s32[1]{0:T(128)}) custom-call(s32[1]{0:T(128)} %bitcast.3.shard_ref, s32[16,16]{1,0:T(8,128)} %fusion.2.flags_ref, bf16[96,128,128]{2,1,0:T(8,128)(2,1)} %collective-permute-done.2.refs_0_, bf16[8192,1280]{1,0:T(8,128)(2,1)} %get-tuple-element.64.refs_1_), custom_call_target="tpu_custom_call", output_to_operand_aliasing={{0}: (3, {})} | custom-call | flops 1 | bytes 1 | tf_op jit(solution)/shard_map/unpack_b/pallas_call | solution.py:200
  110.4 5.7 %unpack_b.12 = (bf16[8192,1280]{1,0:T(8,128)(2,1)}, s32[1]{0:T(128)}) custom-call(s32[1]{0:T(128)} %bitcast.8.shard_ref, s32[16,16]{1,0:T(8,128)} %bitcast_convert_fusion.flags_ref, bf16[96,128,128]{2,1,0:T(8,128)(2,1)} %copy-done.1, bf16[8192,1280]{1,0:T(8,128)(2,1)} %get-tuple-element.65.refs_1_), custom_call_target="tpu_custom_call", output_to_operand_aliasing={{0}: (3, {})} | custom-call | flops 1 | bytes 1 | tf_op jit(solution)/shard_map/unpack_b/pallas_call | solution.py:200
  117.3 5.7 %unpack_b.13 = (bf16[8192,1280]{1,0:T(8,128)(2,1)}, s32[1]{0:T(128)}) custom-call(s32[1]{0:T(128)} %bitcast.2.shard_ref, s32[16,16]{1,0:T(8,128)} %fusion.1.flags_ref, bf16[96,128,128]{2,1,0:T(8,128)(2,1)} %collective-permute-done.5.refs_0_, bf16[8192,1280]{1,0:T(8,128)(2,1)} %get-tuple-element.66.refs_1_), custom_call_target="tpu_custom_call", output_to_operand_aliasing={{0}: (3, {})} | custom-call | flops 1 | bytes 1 | tf_op jit(solution)/shard_map/unpack_b/pallas_call | solution.py:200
  123.1 1.3 fusion.flags_ref
  124.4 1.6 convert_reduce_fusion.marks_ref
  126.0 1.9 collective-permute-start.12
  127.8 2.6 collective-permute-start.14
  132.3 1.5 collective-permute-start
  133.8 21.6 %multiply.4 = (s16[512,1280]{1,0:T(8,128)(2,1)}, f32[4,1,1280]{2,1,0:T(1,128)}) custom-call(s32[1]{0:T(128)} %bitcast.turn_ref, s32[4]{0:T(128)} %compare_select_fusion.column_ref, s32[32,16]{1,0:T(8,128)} %fusion.flags_ref, s32[4,128]{1,0:T(4,128)} %convert_reduce_fusion.marks_ref, bf16[4,43,128,128]{3,2,1,0:T(8,128)(2,1)} %bitcast.52, ...), custom_call_target="tpu_custom_call" | custom-call | flops 999999995904 | bytes 1 | tf_op jit(solution)/shard_map/multiply/pallas_call | solution.py:346
  155.4 1.4 collective-permute-start.16
  159.2 2.4 collective-permute-done.10.refs_2_
  162.1 5.7 %unpack_b.14 = (bf16[8192,768]{1,0:T(8,128)(2,1)}, s32[1]{0:T(128)}) custom-call(s32[1]{0:T(128)} %bitcast.8.shard_ref, s32[16,16]{1,0:T(8,128)} %bitcast_convert_fusion.flags_ref, bf16[96,128,128]{2,1,0:T(8,128)(2,1)} %copy-done.1, bf16[25,128,128]{2,1,0:T(8,128)(2,1)} %collective-permute-done.7.refs_1_, ...), custom_call_target="tpu_custom_call", output_to_operand_aliasing={{0}: (5, {})} | custom-call | flops 1 | bytes 1 | tf_op jit(solution)/shard_map/unpack_b/pallas_call | solution.py:200
  168.7 5.7 %unpack_b.15 = (bf16[8192,768]{1,0:T(8,128)(2,1)}, s32[1]{0:T(128)}) custom-call(s32[1]{0:T(128)} %bitcast.2.shard_ref, s32[16,16]{1,0:T(8,128)} %fusion.1.flags_ref, bf16[96,128,128]{2,1,0:T(8,128)(2,1)} %collective-permute-done.5.refs_0_, bf16[25,128,128]{2,1,0:T(8,128)(2,1)} %copy-done.3, ...), custom_call_target="tpu_custom_call", output_to_operand_aliasing={{0}: (5, {})} | custom-call | flops 1 | bytes 1 | tf_op jit(solution)/shard_map/unpack_b/pallas_call | solution.py:200
  174.4 16.6 %multiply.5 = (s16[512,768]{1,0:T(8,128)(2,1)}, f32[4,1,768]{2,1,0:T(1,128)}) custom-call(s32[1]{0:T(128)} %bitcast.turn_ref, s32[4]{0:T(128)} %compare_select_fusion.column_ref, s32[32,16]{1,0:T(8,128)} %fusion.flags_ref, s32[4,128]{1,0:T(4,128)} %convert_reduce_fusion.marks_ref, bf16[4,43,128,128]{3,2,1,0:T(8,128)(2,1)} %bitcast.53, ...), custom_call_target="tpu_custom_call" | custom-call | flops 1 | bytes 1 | tf_op jit(solution)/shard_map/multiply/pallas_call | solution.py:346
  191.1 1.8 collective-permute-start.11
  192.8 1.9 collective-permute-done.11
  194.8 1.5 collective-permute-start.21
  198.1 1.5 collective-permute-start.20
  199.6 4.6 %collective-permute-start.13 = (bf16[8,128,128]{2,1,0:T(8,128)(2,1)}, bf16[8,128,128]{2,1,0:T(8,128)(2,1)}, u32[]{:S(2)}, u32[]{:S(2)}) collective-permute-start(bf16[8,128,128]{2,1,0:T(8,128)(2,1)} %get-tuple-element.88.refs_2_), channel_id=1, source_target_pairs={{0,2},{2,4},{4,6},{6,0},{1,3},{3,5},{5,7},{7,1},{8,10},{10,12},{12... | collective-permute-start | bytes 786440 | tf_op jit(solution)/shard_map/ppermute | solution.py:458
  204.2 3.2 %collective-permute-start.15 = (bf16[8,128,128]{2,1,0:T(8,128)(2,1)}, bf16[8,128,128]{2,1,0:T(8,128)(2,1)}, u32[]{:S(2)}, u32[]{:S(2)}) collective-permute-start(bf16[8,128,128]{2,1,0:T(8,128)(2,1)} %get-tuple-element.88.refs_2_), channel_id=1, source_target_pairs={{0,4},{2,6},{4,0},{6,2},{1,5},{3,7},{5,1},{7,3},{8,12},{10,14},{12... | collective-permute-start | bytes 786440 | tf_op jit(solution)/shard_map/ppermute | solution.py:458
  207.5 25.4 %multiply.6.refs_15_ = f32[512,2048]{1,0:T(8,128)} custom-call(s32[1]{0:T(128)} %bitcast.turn_ref, s32[4]{0:T(128)} %compare_select_fusion.column_ref, s32[32,16]{1,0:T(8,128)} %fusion.flags_ref, s32[4,128]{1,0:T(4,128)} %convert_reduce_fusion.marks_ref, bf16[4,43,128,128]{3,2,1,0:T(8,128)(2,1)} %bitcast.54, ...), custom_call_target="tpu_custom_call" | custom-call | flops 999999995904 | bytes 1 | tf_op jit(solution)/shard_map/multiply/pallas_call | solution.py:346
  233.0 11.0 %collective-permute-done.20.refs_13_ = s16[512,768]{1,0:T(8,128)(2,1)} collective-permute-done((s16[512,768]{1,0:T(8,128)(2,1)}, s16[512,768]{1,0:T(8,128)(2,1)}, u32[]{:S(2)}, u32[]{:S(2)}) %collective-permute-start.20) | collective-permute-done | bytes 786464 | tf_op jit(solution)/shard_map/ppermute | solution.py:488
  243.9 15.0 %multiply.7 = f32[512,2048]{1,0:T(8,128)} custom-call(s32[1]{0:T(128)} %bitcast.turn_ref, s32[4]{0:T(128)} %compare_select_fusion.column_ref, s32[32,16]{1,0:T(8,128)} %fusion.flags_ref, s32[4,128]{1,0:T(4,128)} %convert_reduce_fusion.marks_ref, bf16[4,43,128,128]{3,2,1,0:T(8,128)(2,1)} %bitcast.55, bf16[26,128,128]{2,1,0:T(8,128)(2,1)} %get-tuple-element.85.refs_1_, ...), custom_call_target="tpu_custom_call" | custom-call | flops 1 | bytes 1 | tf_op jit(solution)/shard_map/multiply/pallas_call | solution.py:346
  (69 shorter events, 14.0 us)
Async XLA Ops:
  6.5 8.5 %copy-start.5 = (s32[16,16]{1,0:T(8,128)S(1)}, s32[16,16]{1,0:T(8,128)}, u32[]{:S(2)}) copy-start(s32[16,16]{1,0:T(8,128)} %other_ref.3) | copy-start | bytes 3076
  6.5 116.5 %all-gather.9.cloned.1.call-start = ((), (), s32[]{:S(2)}) async-start(), calls=%async_computation.4 | async-start | bytes 7045120 | tf_op jit(solution)/shard_map/all_gather | solution.py:412
  23.4 10.7 %collective-permute-start.2 = (bf16[96,128,128]{2,1,0:T(8,128)(2,1)}, bf16[96,128,128]{2,1,0:T(8,128)(2,1)}, u32[]{:S(2)}, u32[]{:S(2)}) collective-permute-start(bf16[96,128,128]{2,1,0:T(8,128)(2,1)} %get-tuple-element.57.refs_0_), channel_id=1, source_target_pairs={{0,8},{8,0},{16,24},{24,16},{1,9},{9,1},{17,25},{25,17},{2,10},{10... | collective-permute-start | bytes 9437192 | tf_op jit(solution)/shard_map/ppermute | solution.py:438
  23.9 71.5 %collective-permute-start.1 = (bf16[96,128,128]{2,1,0:T(8,128)(2,1)}, bf16[96,128,128]{2,1,0:T(8,128)(2,1)S(1)}, u32[]{:S(2)}, u32[]{:S(2)}) collective-permute-start(bf16[96,128,128]{2,1,0:T(8,128)(2,1)} %get-tuple-element.57.refs_0_), channel_id=1, source_target_pairs={{0,16},{8,24},{16,0},{24,8},{1,17},{9,25},{17,1},{25,9},{2,18},{10... | collective-permute-start | bytes 9437192 | tf_op jit(solution)/shard_map/ppermute | solution.py:431
  26.5 8.9 %collective-permute-start.3 = (bf16[25,128,128]{2,1,0:T(8,128)(2,1)}, bf16[25,128,128]{2,1,0:T(8,128)(2,1)}, u32[]{:S(2)}, u32[]{:S(2)}) collective-permute-start(bf16[25,128,128]{2,1,0:T(8,128)(2,1)} %get-tuple-element.72.refs_1_), channel_id=1, source_target_pairs={{0,8},{8,0},{16,24},{24,16},{1,9},{9,1},{17,25},{25,17},{2,10},{10... | collective-permute-start | bytes 2457608 | tf_op jit(solution)/shard_map/ppermute | solution.py:438
  26.6 8.7 %collective-permute-start.4 = (bf16[24,128,128]{2,1,0:T(8,128)(2,1)}, bf16[24,128,128]{2,1,0:T(8,128)(2,1)}, u32[]{:S(2)}, u32[]{:S(2)}) collective-permute-start(bf16[24,128,128]{2,1,0:T(8,128)(2,1)} %get-tuple-element.74.refs_2_), channel_id=1, source_target_pairs={{0,8},{8,0},{16,24},{24,16},{1,9},{9,1},{17,25},{25,17},{2,10},{10... | collective-permute-start | bytes 2359304 | tf_op jit(solution)/shard_map/ppermute | solution.py:438
  95.4 14.4 %copy-start.1 = (bf16[96,128,128]{2,1,0:T(8,128)(2,1)}, bf16[96,128,128]{2,1,0:T(8,128)(2,1)S(1)}, u32[]{:S(2)}) copy-start(bf16[96,128,128]{2,1,0:T(8,128)(2,1)S(1)} %collective-permute-done.1.refs_0_) | copy-start | bytes 9437188
  95.4 20.7 %collective-permute-start.5 = (bf16[96,128,128]{2,1,0:T(8,128)(2,1)S(1)}, bf16[96,128,128]{2,1,0:T(8,128)(2,1)}, u32[]{:S(2)}, u32[]{:S(2)}) collective-permute-start(bf16[96,128,128]{2,1,0:T(8,128)(2,1)S(1)} %collective-permute-done.1.refs_0_), channel_id=1, source_target_pairs={{0,8},{8,0},{16,24},{24,16},{1,9},{9,1},{17,25},{25,17},{2,10},{10... | collective-permute-start | bytes 9437192 | tf_op jit(solution)/shard_map/ppermute | solution.py:445
  101.9 55.5 %collective-permute-start.9 = (bf16[24,128,128]{2,1,0:T(8,128)(2,1)}, bf16[24,128,128]{2,1,0:T(8,128)(2,1)}, u32[]{:S(2)}, u32[]{:S(2)}) collective-permute-start(bf16[24,128,128]{2,1,0:T(8,128)(2,1)} %get-tuple-element.74.refs_2_), channel_id=1, source_target_pairs={{0,16},{8,24},{16,0},{24,8},{1,17},{9,25},{17,1},{25,9},{2,18},{10... | collective-permute-start | bytes 2359304 | tf_op jit(solution)/shard_map/ppermute | solution.py:431
  103.7 51.7 %collective-permute-start.7 = (bf16[25,128,128]{2,1,0:T(8,128)(2,1)}, bf16[25,128,128]{2,1,0:T(8,128)(2,1)}, u32[]{:S(2)}, u32[]{:S(2)}) collective-permute-start(bf16[25,128,128]{2,1,0:T(8,128)(2,1)} %get-tuple-element.72.refs_1_), channel_id=1, source_target_pairs={{0,16},{8,24},{16,0},{24,8},{1,17},{9,25},{17,1},{25,9},{2,18},{10... | collective-permute-start | bytes 2457608 | tf_op jit(solution)/shard_map/ppermute | solution.py:431
  126.0 71.5 %collective-permute-start.12 = (bf16[26,128,128]{2,1,0:T(8,128)(2,1)}, bf16[26,128,128]{2,1,0:T(8,128)(2,1)}, u32[]{:S(2)}, u32[]{:S(2)}) collective-permute-start(bf16[26,128,128]{2,1,0:T(8,128)(2,1)} %get-tuple-element.85.refs_1_), channel_id=1, source_target_pairs={{0,2},{2,4},{4,6},{6,0},{1,3},{3,5},{5,7},{7,1},{8,10},{10,12},{12... | collective-permute-start | bytes 2555912 | tf_op jit(solution)/shard_map/ppermute | solution.py:458
  127.8 70.3 %collective-permute-start.14 = (bf16[26,128,128]{2,1,0:T(8,128)(2,1)}, bf16[26,128,128]{2,1,0:T(8,128)(2,1)}, u32[]{:S(2)}, u32[]{:S(2)}) collective-permute-start(bf16[26,128,128]{2,1,0:T(8,128)(2,1)} %get-tuple-element.85.refs_1_), channel_id=1, source_target_pairs={{0,4},{2,6},{4,0},{6,2},{1,5},{3,7},{5,1},{7,3},{8,12},{10,14},{12... | collective-permute-start | bytes 2555912 | tf_op jit(solution)/shard_map/ppermute | solution.py:458
  132.3 24.5 %collective-permute-start = (f32[8,128]{1,0:T(8,128)}, f32[8,128]{1,0:T(8,128)}, u32[]{:S(2)}, u32[]{:S(2)}) collective-permute-start(f32[8,128]{1,0:T(8,128)} %reduce_max.15), channel_id=1, source_target_pairs={{0,1},{1,0},{2,3},{3,2},{4,5},{5,4},{6,7},{7,6},{8,9},{9,8},{10,11... | collective-permute-start | bytes 12296 | tf_op jit(solution)/shard_map/ppermute | solution.py:368
  133.8 23.0 %copy-start.10 = (bf16[8,128]{1,0:T(8,128)(2,1)S(1)}, bf16[8,128]{1,0:T(8,128)(2,1)}, u32[]{:S(2)}) copy-start(bf16[8,128]{1,0:T(8,128)(2,1)} %copy-done.9) | copy-start | bytes 6148
  155.4 44.3 %collective-permute-start.16 = (bf16[26,128,128]{2,1,0:T(8,128)(2,1)}, bf16[26,128,128]{2,1,0:T(8,128)(2,1)S(1)}, u32[]{:S(2)}, u32[]{:S(2)}) collective-permute-start(bf16[26,128,128]{2,1,0:T(8,128)(2,1)} %get-tuple-element.85.refs_1_), channel_id=1, source_target_pairs={{0,6},{2,0},{4,2},{6,4},{1,7},{3,1},{5,3},{7,5},{8,14},{10,8},{12,... | collective-permute-start | bytes 2555912 | tf_op jit(solution)/shard_map/ppermute | solution.py:458
  156.8 11.0 %collective-permute-start.8 = (bf16[25,128,128]{2,1,0:T(8,128)(2,1)}, bf16[25,128,128]{2,1,0:T(8,128)(2,1)S(1)}, u32[]{:S(2)}, u32[]{:S(2)}) collective-permute-start(bf16[25,128,128]{2,1,0:T(8,128)(2,1)} %collective-permute-done.7.refs_1_), channel_id=1, source_target_pairs={{0,8},{8,0},{16,24},{24,16},{1,9},{9,1},{17,25},{25,17},{2,10},{10... | collective-permute-start | bytes 2457608 | tf_op jit(solution)/shard_map/ppermute | solution.py:479
  157.5 1.6 collective-permute-start.6
  159.1 2.5 collective-permute-start.10
  161.6 6.2 %copy-start.4 = (bf16[24,128,128]{2,1,0:T(8,128)(2,1)}, bf16[24,128,128]{2,1,0:T(8,128)(2,1)S(1)}, u32[]{:S(2)}) copy-start(bf16[24,128,128]{2,1,0:T(8,128)(2,1)S(1)} %collective-permute-done.10.refs_2_) | copy-start | bytes 2359300
  161.6 42.6 %collective-permute-start.19 = (f32[4,1,1280]{2,1,0:T(1,128)}, f32[4,1,1280]{2,1,0:T(1,128)S(1)}, u32[]{:S(2)}, u32[]{:S(2)}) collective-permute-start(f32[4,1,1280]{2,1,0:T(1,128)} %get-tuple-element.70), channel_id=1, source_target_pairs={{0,1},{1,0},{2,3},{3,2},{4,5},{5,4},{6,7},{7,6},{8,9},{9,8},{10,11... | collective-permute-start | bytes 61448 | tf_op jit(solution)/shard_map/ppermute | solution.py:488
  191.1 3.7 %collective-permute-start.11 = (f32[8,128]{1,0:T(8,128)S(1)}, f32[8,128]{1,0:T(8,128)S(1)}, u32[]{:S(2)}, u32[]{:S(2)}) collective-permute-start(f32[8,128]{1,0:T(8,128)S(1)} %max.10), channel_id=1, source_target_pairs={{0,16},{8,24},{16,0},{24,8},{1,17},{9,25},{17,1},{25,9},{2,18},{10... | collective-permute-start | bytes 12296 | tf_op jit(solution)/shard_map/ppermute | solution.py:368
  194.8 12.7 %collective-permute-start.21 = (f32[4,1,768]{2,1,0:T(1,128)}, f32[4,1,768]{2,1,0:T(1,128)S(1)}, u32[]{:S(2)}, u32[]{:S(2)}) collective-permute-start(f32[4,1,768]{2,1,0:T(1,128)} %get-tuple-element.80), channel_id=1, source_target_pairs={{0,1},{1,0},{2,3},{3,2},{4,5},{5,4},{6,7},{7,6},{8,9},{9,8},{10,11... | collective-permute-start | bytes 36872 | tf_op jit(solution)/shard_map/ppermute | solution.py:488
  197.5 35.5 %collective-permute-start.18 = (s16[512,1280]{1,0:T(8,128)(2,1)}, s16[512,1280]{1,0:T(8,128)(2,1)}, u32[]{:S(2)}, u32[]{:S(2)}) collective-permute-start(s16[512,1280]{1,0:T(8,128)(2,1)} %get-tuple-element.89), channel_id=1, source_target_pairs={{0,1},{1,0},{2,3},{3,2},{4,5},{5,4},{6,7},{7,6},{8,9},{9,8},{10,11... | collective-permute-start | bytes 3932168 | tf_op jit(solution)/shard_map/ppermute | solution.py:488
  198.1 45.8 %collective-permute-start.20 = (s16[512,768]{1,0:T(8,128)(2,1)}, s16[512,768]{1,0:T(8,128)(2,1)}, u32[]{:S(2)}, u32[]{:S(2)}) collective-permute-start(s16[512,768]{1,0:T(8,128)(2,1)} %get-tuple-element.90), channel_id=1, source_target_pairs={{0,1},{1,0},{2,3},{3,2},{4,5},{5,4},{6,7},{7,6},{8,9},{9,8},{10,11... | collective-permute-start | bytes 2359304 | tf_op jit(solution)/shard_map/ppermute | solution.py:488
  199.6 7.9 %copy-start.2 = (bf16[26,128,128]{2,1,0:T(8,128)(2,1)}, bf16[26,128,128]{2,1,0:T(8,128)(2,1)S(1)}, u32[]{:S(2)}) copy-start(bf16[26,128,128]{2,1,0:T(8,128)(2,1)S(1)} %collective-permute-done.16.refs_4_.refs_7_) | copy-start | bytes 2555908
  199.6 33.3 %collective-permute-start.13 = (bf16[8,128,128]{2,1,0:T(8,128)(2,1)}, bf16[8,128,128]{2,1,0:T(8,128)(2,1)}, u32[]{:S(2)}, u32[]{:S(2)}) collective-permute-start(bf16[8,128,128]{2,1,0:T(8,128)(2,1)} %get-tuple-element.88.refs_2_), channel_id=1, source_target_pairs={{0,2},{2,4},{4,6},{6,0},{1,3},{3,5},{5,7},{7,1},{8,10},{10,12},{12... | collective-permute-start | bytes 786440 | tf_op jit(solution)/shard_map/ppermute | solution.py:458
  204.2 28.7 %copy-start.8 = (f32[4,1,1280]{2,1,0:T(1,128)}, f32[4,1,1280]{2,1,0:T(1,128)S(1)}, u32[]{:S(2)}) copy-start(f32[4,1,1280]{2,1,0:T(1,128)S(1)} %collective-permute-done.19.refs_12_) | copy-start | bytes 61444
  204.2 28.7 %collective-permute-start.15 = (bf16[8,128,128]{2,1,0:T(8,128)(2,1)}, bf16[8,128,128]{2,1,0:T(8,128)(2,1)}, u32[]{:S(2)}, u32[]{:S(2)}) collective-permute-start(bf16[8,128,128]{2,1,0:T(8,128)(2,1)} %get-tuple-element.88.refs_2_), channel_id=1, source_target_pairs={{0,4},{2,6},{4,0},{6,2},{1,5},{3,7},{5,1},{7,3},{8,12},{10,14},{12... | collective-permute-start | bytes 786440 | tf_op jit(solution)/shard_map/ppermute | solution.py:458
  207.5 25.4 %copy-start.11 = (f32[4,1,768]{2,1,0:T(1,128)}, f32[4,1,768]{2,1,0:T(1,128)S(1)}, u32[]{:S(2)}) copy-start(f32[4,1,768]{2,1,0:T(1,128)S(1)} %collective-permute-done.21.refs_14_) | copy-start | bytes 36868
  207.5 25.5 %collective-permute-start.17 = (bf16[8,128,128]{2,1,0:T(8,128)(2,1)}, bf16[8,128,128]{2,1,0:T(8,128)(2,1)}, u32[]{:S(2)}, u32[]{:S(2)}) collective-permute-start(bf16[8,128,128]{2,1,0:T(8,128)(2,1)} %get-tuple-element.88.refs_2_), channel_id=1, source_target_pairs={{0,6},{2,0},{4,2},{6,4},{1,7},{3,1},{5,3},{7,5},{8,14},{10,8},{12,... | collective-permute-start | bytes 786440 | tf_op jit(solution)/shard_map/ppermute | solution.py:458
  232.9 26.0 %copy-start.6 = (s32[16,16]{1,0:T(8,128)S(1)}, s32[16,16]{1,0:T(8,128)}, u32[]{:S(2)}) copy-start(s32[16,16]{1,0:T(8,128)} %other_ref.3) | copy-start | bytes 3076
  232.9 26.0 %copy-start.7 = (s32[8,16]{1,0:T(8,128)S(1)}, s32[8,16]{1,0:T(8,128)}, u32[]{:S(2)}) copy-start(s32[8,16]{1,0:T(8,128)} %flags_ref.2) | copy-start | bytes 1540
  (2 other events, 1.4 us)
Sparse Core Ops, SparseCore 0:
  15.1 107.2 all-gather.8

commit v3 on v2

--- a/solution.py
+++ b/solution.py
@@ -222,17 +222,15 @@
 
 
 def multiply_kernel(plan, turn_ref, column_ref, flags_ref, marks_ref, *refs):
-    place, stages, blocks, cuts, shards, halves, given, carried, final, starts, ends = plan
+    place, stages, blocks, cuts, shards, halves, given, carried, pieces, starts, ends = plan
     stage = stages[-1]
     rows, wide = stage.rows, stage.wide
-    n = len(cuts) - 2
-    gathered_ref, refs = refs[0], refs[1:]
-    lists = [refs[s * n : (s + 1) * n] for s in range(shards)]
-    refs = refs[shards * n :]
+    n = len(cuts) - 1
+    gathered_refs, refs = refs[:n], refs[n:]
     b_refs, refs = refs[:halves], refs[halves:]
-    codes_in, refs = refs[: 2 * halves * given], refs[2 * halves * given :]
+    codes_in, refs = refs[: halves * given], refs[halves * given :]
     before, refs = refs[:carried], refs[carried:]
-    outs, (dense, sem, total) = refs[:-3], refs[-3:]
+    over_ref, out_ref, dense, sem, total = refs[-5:]
     turn = turn_ref[0]
 
     def fill():
@@ -240,7 +238,7 @@
         started = jnp.int32(0)
         for s in range(shards):
             column = column_ref[s]
-            parts = [gathered_ref.at[column], *lists[s]]
+            parts = [ref.at[column] for ref in gathered_refs]
 
             def flag_of(stage, u):
                 row, k = place(stage, u, turn)
@@ -265,30 +263,37 @@
             started += jnp.minimum(end, cuts[-1]) - jnp.minimum(slot, cuts[-1])
 
         def settle(t, _):
-            pltpu.make_async_copy(gathered_ref.at[0, 0], dense.at[:BLOCK, :BLOCK], sem).wait()
+            pltpu.make_async_copy(gathered_refs[0].at[0, 0], dense.at[:BLOCK, :BLOCK], sem).wait()
             return 0
 
         lax.fori_loop(0, started, settle, 0)
 
     pl.when(pl.program_id(0) == 0)(fill)
 
+    def code(value):
+        share = rows // pieces
+        for q in range(pieces):
+            base = q * (share * BLOCK + 16)
+            powers = []
+            for r in range(share):
+                some = value[(q * share + r) * BLOCK : (q * share + r + 1) * BLOCK]
+                top = jnp.max(jnp.abs(some), axis=0, keepdims=True)
+                power = jnp.clip(jnp.ceil(jnp.log2(top)), -60.0, 60.0)
+                some = jnp.clip(jnp.round(some * jnp.exp2(15.0 - power)), -32767.0, 32767.0)
+                out_ref[base + r * BLOCK : base + (r + 1) * BLOCK] = some.astype(jnp.int32).astype(jnp.int16)
+                powers.append(power)
+            flag = jnp.broadcast_to(over_ref[0:1, 0:1], powers[0].shape)
+            notes = jnp.concatenate(powers + [flag] * (16 - share), axis=0)
+            out_ref[base + share * BLOCK : base + share * BLOCK + 16] = notes.astype(jnp.int32).astype(jnp.int16)
+
     def finish(value, h):
-        if not final:
-            codes_ref, factors_ref = outs
-            for r in range(rows):
-                span = slice(r * BLOCK, (r + 1) * BLOCK)
-                top = jnp.max(jnp.abs(value[span]), axis=0, keepdims=True)
-                factor = jnp.where(top > 0, 32767.0 / top, 0.0)
-                codes_ref[span] = jnp.round(value[span] * factor).astype(jnp.int32).astype(jnp.int16)
-                factors_ref[r] = top * (1.0 / 32767.0)
-            return
-        (out_ref,) = outs
         for r in range(rows):
             span = slice(r * BLOCK, (r + 1) * BLOCK)
             some = value[span]
             for q in range(given):
-                codes, factors = codes_in[2 * (q * halves + h) : 2 * (q * halves + h) + 2]
-                some += codes[span].astype(jnp.int32).astype(jnp.float32) * factors[r]
+                codes = codes_in[q * halves + h]
+                notes = codes[rows * BLOCK : rows * BLOCK + 16].astype(jnp.int32).astype(jnp.float32)
+                some += codes[span].astype(jnp.int32).astype(jnp.float32) * jnp.exp2(notes[r : r + 1] - 15.0)
             for earlier in before:
                 some += earlier[span]
             out_ref[span] = some
@@ -299,13 +304,16 @@
         def _():
             b_here = b_ref[...].reshape(-1, b_ref.shape[-1])
             total[...] = jnp.dot(dense[...], b_here, preferred_element_type=jnp.float32)
-            finish(total, h)
-
-
-def multiply(gathered, lists, flags, marks, turn, columns, place, stages, k_blocks, cuts, b_halves, final, cost, received=(), before=()):
-    shards, halves = len(lists), len(b_halves)
+            if pieces:
+                code(total)
+            else:
+                finish(total, h)
+
+
+def multiply(parts, flags, marks, turn, columns, place, stages, k_blocks, cuts, b_halves, over, pieces=0, received=(), before=()):
+    shards, halves = parts[0].shape[0], len(b_halves)
     stage = stages[-1]
-    n = len(cuts) - 2
+    n = len(cuts) - 1
     widths = [b_half.shape[1] for b_half in b_halves]
     shared = math.gcd(*widths)
     tile = max(t for t in (BLOCK, 256, 512) if shared % t == 0 and t * stage.wide <= TILE_ROOM)
@@ -320,45 +328,37 @@
     def at(h, *fixed):
         return lambda j, *_: (*fixed, jnp.clip(j - starts[h], 0, ends[h] - starts[h] - 1))
 
-    in_specs = [whole] * (1 + shards * n)
-    operands = [gathered] + [p for parts in lists for p in parts[:n]]
+    in_specs = [whole] * n
+    operands = [*parts[:n]]
     for h, b_half in enumerate(b_halves):
         in_specs.append(pl.BlockSpec((shards, layers, deep * BLOCK, tile), at(h, 0, skip // layers, 0)))
         operands.append(b_half.reshape(shards, k_blocks // deep, deep * BLOCK, widths[h]))
     for pairs in received:
-        for h, (codes, factors) in enumerate(pairs):
-            in_specs.append(pl.BlockSpec((tall, tile), at(h, 0)))
-            in_specs.append(pl.BlockSpec((stage.rows, 1, tile), at(h, 0, 0)))
-            operands += [codes, factors]
+        for h, codes in enumerate(pairs):
+            in_specs.append(pl.BlockSpec((tall + 16, tile), at(h, 0)))
+            operands.append(codes)
     in_specs += [pl.BlockSpec((tall, tile), lambda j, *_: (0, j))] * len(before)
     operands += [*before]
-    out_specs = [pl.BlockSpec((tall, tile), lambda j, *_: (0, j))]
-    if final:
-        out_shape = [jax.ShapeDtypeStruct((tall, sum(widths)), jnp.float32)]
-    else:
-        out_specs.append(pl.BlockSpec((stage.rows, 1, tile), lambda j, *_: (0, 0, j)))
-        out_shape = [
-            jax.ShapeDtypeStruct((tall, sum(widths)), jnp.int16),
-            jax.ShapeDtypeStruct((stage.rows, 1, sum(widths)), jnp.float32),
-        ]
-    blocks = flags.shape[0] // shards
-    plan = (place, stages, blocks, cuts, shards, halves, len(received), len(before), final, starts, ends)
+    in_specs.append(pl.BlockSpec(memory_space=pltpu.VMEM))
+    operands.append(over)
+    high = tall + 16 * pieces
+    plan = (place, stages, flags.shape[0] // shards, cuts, shards, halves, len(received), len(before), pieces, starts, ends)
     return pl.pallas_call(
         functools.partial(multiply_kernel, plan),
         grid_spec=pltpu.PrefetchScalarGridSpec(
             num_scalar_prefetch=4,
             grid=(ends[-1],),
             in_specs=in_specs,
-            out_specs=out_specs,
+            out_specs=pl.BlockSpec((high, tile), lambda j, *_: (0, j)),
             scratch_shapes=[
                 pltpu.VMEM((tall, shards * stage.wide * BLOCK), b_halves[0].dtype),
                 pltpu.SemaphoreType.DMA,
                 pltpu.VMEM((tall, tile), jnp.float32),
             ],
         ),
-        out_shape=out_shape,
+        out_shape=jax.ShapeDtypeStruct((high, sum(widths)), jnp.int16 if pieces else jnp.float32),
         compiler_params=pltpu.CompilerParams(vmem_limit_bytes=VMEM_LIMIT),
-        cost_estimate=cost,
+        cost_estimate=SMALL,
         name="multiply",
     )(turn, columns, flags, marks, *operands)
 
@@ -409,7 +409,8 @@
     a_parts, done = pack(
         a_tiles, a_occupancy, turn, a_place, a_stages, a_cuts, a_cuts, b_occupancy, (b_place, b_stages, b_ends)
     )
-    gathered = lax.all_gather(a_parts[0], "col", axis=0)
+    joint = [lax.all_gather(part, "col", axis=0) for part in a_parts]
+    gathered = joint[0]
     b_parts, done = pack(
         b_tiles, b_occupancy, after(turn, done), b_place, b_stages, b_ends, b_cuts, b_occupancy, None
     )
@@ -449,28 +450,20 @@
         for hop in hops:
             done = unpack(0, shards[hop] ^ side, sides[hop][side], done)
 
-    a_lists = [[] for _ in range(cols)]
-    waits = [done] * cols
-    for part in a_parts[1:]:
-        a_lists[0].append(part)
-        for hop in range(1, cols):
-            there = [(c, (c + hop) % cols) for c in range(cols)]
-            waits[hop] = lax.ppermute(after(part, waits[hop], gathered), "col", there)
-            a_lists[hop].append(waits[hop])
-    a_columns = lax.rem(me_col - jnp.arange(cols, dtype=jnp.int32) + cols, cols)
+    a_columns = jnp.arange(cols, dtype=jnp.int32)
     a_flags = gathered[:, 0, :a_rows, :a_k].astype(jnp.int32).reshape(cols * a_rows, a_k)
 
     a_marks = gathered[:, 0, :, 0].astype(jnp.int32)
+
+    over = jnp.max(gathered[:, 0, mark_row(0) : mark_row(0) + 8].astype(jnp.float32), axis=0)
 
     def product_of(g, halves, done, **more):
         return multiply(
-            gathered, a_lists, a_flags, a_marks, after(turn, done), a_columns, a_place, a_stages[: g + 1], a_k, a_cuts[: g + 2],
+            joint, a_flags, a_marks, after(turn, done), a_columns, a_place, a_stages[: g + 1], a_k, a_cuts[: g + 2],
             halves, **more
         )
 
-    over = jnp.max(gathered[:, 0, mark_row(0) : mark_row(0) + 8].astype(jnp.float32), axis=0)
-    over = largest_over(over, "layer", layers)
-
+    high = piece * BLOCK + 16
     received = [[] for _ in range(layers - 1)]
     for h in range(len(b_stages)):
         if h:
@@ -479,22 +472,24 @@
                 there = [lax.ppermute(part, "row", swap) for part in here]
                 for side, more in zip(range(pair), (here, there)):
                     done = unpack(h, shards[hop] ^ side, sides[hop][side] + more, done)
-        codes, factors = product_of(0, [b_dense[h]], done, final=False, cost=SMALL if h else LARGE)
-        done = factors
-        over = largest_over(after(over, done), "row", rows, 1 << h, 2 << h if h + 1 < len(b_stages) else rows)
+            over = largest_over(after(over, codes[-16:, :BLOCK]), "row", rows, 2)
+        codes = product_of(0, [b_dense[h]], done, over=over, pieces=layers - 1)
+        if not h:
+            over = largest_over(over, "row", rows, 1, 2)
+        done = codes[-16:, :BLOCK]
         for q in range(layers - 1):
             there = [(i, (i + 1 + q) % layers) for i in range(layers)]
-            own = codes[q * piece * BLOCK : (q + 1) * piece * BLOCK], factors[q * piece : (q + 1) * piece]
-            received[q].append(tuple(lax.ppermute(x, "layer", there) for x in own))
-
-    (product,) = product_of(1, b_dense, done, final=True, cost=LARGE)
+            received[q].append(lax.ppermute(codes[q * high : (q + 1) * high], "layer", there))
+
+    product = product_of(1, b_dense, done, over=over)
     for g in range(2, len(a_stages)):
         last = g == len(a_stages) - 1
-        (product,) = product_of(
-            g, b_dense, done, final=True, cost=SMALL, received=received if last else (), before=(product,)
-        )
+        product = product_of(g, b_dense, done, over=over, received=received if last else (), before=(product,))
+    over = over[0, 0]
+    for pairs in received:
+        over = jnp.maximum(over, pairs[-1][-1, 0].astype(jnp.float32))
     return lax.cond(
-        over[0, 0] > 0,
+        over > 0,
         lambda: whole_slab(a_tiles, a_occupancy, b_tiles, b_occupancy),
         lambda: product,
     )

time: 268 us -> 244 us (0.910)
  starting transfers between devices: 27.3 us -> 10.3 us
  waiting for transfers between devices: 70.7 us -> 59 us
  local copies, waits for them, and re-layouts: 3.28 us -> 6.94 us
    ppermute x10 -> x2, starting transfers between devices: 17.8 us -> 2.34 us  [per_device(): lax.ppermute(codes[q * high:(q + 1) * high], 'layer', there)]
    ppermute x10 -> x2, waiting for transfers between devices: 11 us -> 0.01 us  [per_device(): lax.ppermute(codes[q * high:(q + 1) * high], 'layer', there)]
    all_gather x1 -> x3, waiting for transfers between devices: 0.02 us -> 3.46 us  [per_device(): joint = [lax.all_gather(part, 'col', axis=0) for part in a_parts]]
  transfers between devices with their start and end apart: 23 -> 16, of which waited for: 5 -> 4; matrix products, arithmetic and copies ran while one was open for 4% -> 6% of each run, Pallas kernels for 44% -> 49%
where the time goes in v3:
time: 244 us; the launch traced here: 241 us
  Pallas kernels  141 us (58%)
  waiting for transfers between devices  59 us (24%)
  between operations  14.6 us (6%)
  starting transfers between devices  10.3 us (4%)
  other arithmetic  9.91 us (4%)
  local copies, waits for them, and re-layouts  6.94 us (3%)
    pallas_call x4, Pallas kernels, multiply(): pl.pallas_call(functools.partial(multiply_kernel, plan), grid_spec=pltpu....  79.7 us
    ppermute x3, waiting for transfers between devices, across(): lax.ppermute(part, 'row', [(r, (r + pair * hop) % rows) for r in range(ro...  54.3 us
    pallas_call x8, Pallas kernels, unpack_b(): pl.pallas_call(functools.partial(unpack_b_kernel, k_blocks, first, stop,...  46 us
    pallas_call x2, Pallas kernels, pack(): pl.pallas_call(functools.partial(pack_kernel, place, stages, ends, cuts,...  14.9 us
  transfers between devices with their start and end apart: 16, of which 4 were waited for; matrix products, arithmetic and copies ran while one was open for 6% of the time, Pallas kernels for 49%

profile of v3, /device:TPU:0, one launch (start us, length us, event | category | flops | bytes accessed | tf_op | source)
XLA Modules:
  0.0 241.4 jit_solution(11677403197188474787)
XLA Ops:
  6.5 0.7 convert_element_type.63
  7.2 0.6 pad.8.header_ref
  7.9 7.1 %pack.2 = (bf16[43,128,128]{2,1,0:T(8,128)(2,1)}, bf16[26,128,128]{2,1,0:T(8,128)(2,1)}, bf16[8,128,128]{2,1,0:T(8,128)(2,1)}, s32[1]{0:T(128)}) custom-call(s32[1]{0:T(128)} %bitcast.turn_ref, s32[8,16]{1,0:T(8,128)} %flags_ref.2, s32[16,16]{1,0:T(8,128)} %other_ref.3, bf16[128,128]{1,0:T(8,128)(2,1)} %pad.8.header_ref, bf16[1024,2048]{1,0:T(8,128)(2,1)} %values_ref.2), custom_call_target="tpu_custom_call" | custom-call | flops 1 | bytes 1 | tf_op jit(solution)/shard_map/pack/pallas_call | solution.py:131
  15.7 7.8 %pack.3 = (bf16[96,128,128]{2,1,0:T(8,128)(2,1)}, bf16[25,128,128]{2,1,0:T(8,128)(2,1)}, bf16[24,128,128]{2,1,0:T(8,128)(2,1)}, s32[1]{0:T(128)}) custom-call(s32[1]{0:T(128)} %bitcast.turn_ref, s32[16,16]{1,0:T(8,128)S(1)} %copy-done.6, s32[16,16]{1,0:T(8,128)S(1)} %copy-done.6, bf16[128,128]{1,0:T(8,128)(2,1)} %pad.9.header_ref, bf16[2048,2048]{1,0:T(8,128)(2,1)} %values_ref.3), custom_call_target="tpu_custom_call" | custom-call | flops 1 | bytes 1 | tf_op jit(solution)/shard_map/pack/pallas_call | solution.py:131
  24.0 2.6 %collective-permute-start.1 = (bf16[96,128,128]{2,1,0:T(8,128)(2,1)}, bf16[96,128,128]{2,1,0:T(8,128)(2,1)S(1)}, u32[]{:S(2)}, u32[]{:S(2)}) collective-permute-start(bf16[96,128,128]{2,1,0:T(8,128)(2,1)} %get-tuple-element.45.refs_0_), channel_id=1, source_target_pairs={{0,16},{8,24},{16,0},{24,8},{1,17},{9,25},{17,1},{25,9},{2,18},{10... | collective-permute-start | bytes 9437192 | tf_op jit(solution)/shard_map/ppermute | solution.py:432
  27.2 1.3 bitcast_convert_fusion.1.flags_ref
  28.5 5.7 %unpack_b.8 = (bf16[8192,768]{1,0:T(8,128)(2,1)}, s32[1]{0:T(128)}) custom-call(s32[1]{0:T(128)} %bitcast.6.shard_ref, s32[16,16]{1,0:T(8,128)} %bitcast_convert_fusion.1.flags_ref, bf16[96,128,128]{2,1,0:T(8,128)(2,1)} %get-tuple-element.45.refs_0_, bf16[25,128,128]{2,1,0:T(8,128)(2,1)} %get-tuple-element.57.refs_1_, ...), custom_call_target="tpu_custom_call" | custom-call | flops 1 | bytes 1 | tf_op jit(solution)/shard_map/unpack_b/pallas_call | solution.py:200
  34.2 1.3 fusion.2.flags_ref
  35.5 5.7 %unpack_b.9 = (bf16[8192,768]{1,0:T(8,128)(2,1)}, s32[1]{0:T(128)}) custom-call(s32[1]{0:T(128)} %bitcast.4.shard_ref, s32[16,16]{1,0:T(8,128)} %fusion.2.flags_ref, bf16[96,128,128]{2,1,0:T(8,128)(2,1)} %collective-permute-done.2.refs_0_, bf16[25,128,128]{2,1,0:T(8,128)(2,1)} %collective-permute-done.3.refs_1_, ...), custom_call_target="tpu_custom_call", output_to_operand_aliasing={{0}: (5, {})} | custom-call | flops 1 | bytes 1 | tf_op jit(solution)/shard_map/unpack_b/pallas_call | solution.py:200
  41.2 54.3 %collective-permute-done.1.refs_0_ = bf16[96,128,128]{2,1,0:T(8,128)(2,1)S(1)} collective-permute-done((bf16[96,128,128]{2,1,0:T(8,128)(2,1)}, bf16[96,128,128]{2,1,0:T(8,128)(2,1)S(1)}, u32[]{:S(2)}, u32[]{:S(2)}) %collective-permute-start.1) | collective-permute-done | bytes 3145760 | tf_op jit(solution)/shard_map/ppermute | solution.py:432
  95.4 6.0 %unpack_b.10 = (bf16[8192,1280]{1,0:T(8,128)(2,1)}, s32[1]{0:T(128)}) custom-call(s32[1]{0:T(128)} %bitcast.6.shard_ref, s32[16,16]{1,0:T(8,128)} %bitcast_convert_fusion.1.flags_ref, bf16[96,128,128]{2,1,0:T(8,128)(2,1)} %get-tuple-element.45.refs_0_), custom_call_target="tpu_custom_call" | custom-call | flops 1 | bytes 1 | tf_op jit(solution)/shard_map/unpack_b/pallas_call | solution.py:200
  101.5 1.8 collective-permute-start.9
  104.2 5.7 %unpack_b.11 = (bf16[8192,1280]{1,0:T(8,128)(2,1)}, s32[1]{0:T(128)}) custom-call(s32[1]{0:T(128)} %bitcast.4.shard_ref, s32[16,16]{1,0:T(8,128)} %fusion.2.flags_ref, bf16[96,128,128]{2,1,0:T(8,128)(2,1)} %collective-permute-done.2.refs_0_, bf16[8192,1280]{1,0:T(8,128)(2,1)} %get-tuple-element.52.refs_1_), custom_call_target="tpu_custom_call", output_to_operand_aliasing={{0}: (3, {})} | custom-call | flops 1 | bytes 1 | tf_op jit(solution)/shard_map/unpack_b/pallas_call | solution.py:200
  109.9 5.7 %unpack_b.12 = (bf16[8192,1280]{1,0:T(8,128)(2,1)}, s32[1]{0:T(128)}) custom-call(s32[1]{0:T(128)} %bitcast.9.shard_ref, s32[16,16]{1,0:T(8,128)} %bitcast_convert_fusion.flags_ref, bf16[96,128,128]{2,1,0:T(8,128)(2,1)} %copy-done.1, bf16[8192,1280]{1,0:T(8,128)(2,1)} %get-tuple-element.53.refs_1_), custom_call_target="tpu_custom_call", output_to_operand_aliasing={{0}: (3, {})} | custom-call | flops 1 | bytes 1 | tf_op jit(solution)/shard_map/unpack_b/pallas_call | solution.py:200
  115.6 1.3 fusion.1.flags_ref
  116.9 5.7 %unpack_b.13 = (bf16[8192,1280]{1,0:T(8,128)(2,1)}, s32[1]{0:T(128)}) custom-call(s32[1]{0:T(128)} %bitcast.3.shard_ref, s32[16,16]{1,0:T(8,128)} %fusion.1.flags_ref, bf16[96,128,128]{2,1,0:T(8,128)(2,1)} %collective-permute-done.5.refs_0_, bf16[8192,1280]{1,0:T(8,128)(2,1)} %get-tuple-element.54.refs_1_), custom_call_target="tpu_custom_call", output_to_operand_aliasing={{0}: (3, {})} | custom-call | flops 1 | bytes 1 | tf_op jit(solution)/shard_map/unpack_b/pallas_call | solution.py:200
  122.7 0.7 slice_reduce_fusion
  124.0 1.6 convert_reduce_fusion.marks_ref
  125.5 1.3 fusion.flags_ref
  127.4 22.1 %multiply.4 = s16[528,1280]{1,0:T(8,128)(2,1)} custom-call(s32[1]{0:T(128)} %bitcast.turn_ref, s32[4]{0:T(128)} %iota.9.column_ref, s32[32,16]{1,0:T(8,128)} %fusion.flags_ref, s32[4,128]{1,0:T(4,128)} %convert_reduce_fusion.marks_ref, bf16[4,43,128,128]{3,2,1,0:T(8,128)(2,1)} %bitcast.53, bf16[4,1,2048,1280]{3,2,1,0:T(8,128)(2,1)} %bitcast.44, ...), custom_call_target="tpu_custom_call" | custom-call | flops 1 | bytes 1 | tf_op jit(solution)/shard_map/multiply/pallas_call | solution.py:346
  150.1 1.9 collective-permute-start.12
  152.0 1.2 collective-permute-done
  153.2 1.6 collective-permute-start.6
  154.8 5.7 %unpack_b.14 = (bf16[8192,768]{1,0:T(8,128)(2,1)}, s32[1]{0:T(128)}) custom-call(s32[1]{0:T(128)} %bitcast.9.shard_ref, s32[16,16]{1,0:T(8,128)} %bitcast_convert_fusion.flags_ref, bf16[96,128,128]{2,1,0:T(8,128)(2,1)} %copy-done.1, bf16[25,128,128]{2,1,0:T(8,128)(2,1)} %collective-permute-done.7.refs_1_, ...), custom_call_target="tpu_custom_call", output_to_operand_aliasing={{0}: (5, {})} | custom-call | flops 1 | bytes 1 | tf_op jit(solution)/shard_map/unpack_b/pallas_call | solution.py:200
  161.1 0.9 copy-done.5
  162.3 5.7 %unpack_b.15 = (bf16[8192,768]{1,0:T(8,128)(2,1)}, s32[1]{0:T(128)}) custom-call(s32[1]{0:T(128)} %bitcast.3.shard_ref, s32[16,16]{1,0:T(8,128)} %fusion.1.flags_ref, bf16[96,128,128]{2,1,0:T(8,128)(2,1)} %collective-permute-done.5.refs_0_, bf16[25,128,128]{2,1,0:T(8,128)(2,1)} %copy-done.3, ...), custom_call_target="tpu_custom_call", output_to_operand_aliasing={{0}: (5, {})} | custom-call | flops 1 | bytes 1 | tf_op jit(solution)/shard_map/unpack_b/pallas_call | solution.py:200
  168.6 16.9 %multiply.5 = s16[528,768]{1,0:T(8,128)(2,1)} custom-call(s32[1]{0:T(128)} %bitcast.turn_ref, s32[4]{0:T(128)} %iota.10.column_ref, s32[32,16]{1,0:T(8,128)} %fusion.flags_ref, s32[4,128]{1,0:T(4,128)} %convert_reduce_fusion.marks_ref, bf16[4,43,128,128]{3,2,1,0:T(8,128)(2,1)} %bitcast.54, bf16[4,1,2048,768]{3,2,1,0:T(8,128)(2,1)} %bitcast.47, ...), custom_call_target="tpu_custom_call" | custom-call | flops 1 | bytes 1 | tf_op jit(solution)/shard_map/multiply/pallas_call | solution.py:346
  185.9 1.2 slice.44
  187.1 3.1 %all-gather.15.cloned.1.call-done = bf16[104,128,128]{2,1,0:T(8,128)(2,1)} async-done(((bf16[26,128,128]{2,1,0:T(8,128)(2,1)}), bf16[104,128,128]{2,1,0:T(8,128)(2,1)}) %all-gather.15.cloned.1.call-update) | async-done | bytes 3407888 | tf_op jit(solution)/shard_map/all_gather | solution.py:412
  190.8 25.5 %multiply.6.refs_7_ = f32[512,2048]{1,0:T(8,128)} custom-call(s32[1]{0:T(128)} %bitcast.turn_ref, s32[4]{0:T(128)} %iota.12.column_ref, s32[32,16]{1,0:T(8,128)} %fusion.flags_ref, s32[4,128]{1,0:T(4,128)} %convert_reduce_fusion.marks_ref, bf16[4,43,128,128]{3,2,1,0:T(8,128)(2,1)} %bitcast.55, bf16[4,26,128,128]{3,2,1,0:T(8,128)(2,1)} %bitcast.59, ...), custom_call_target="tpu_custom_call" | custom-call | flops 1 | bytes 1 | tf_op jit(solution)/shard_map/multiply/pallas_call | solution.py:346
  216.3 0.6 slice.52
  219.6 15.3 %multiply.7 = f32[512,2048]{1,0:T(8,128)} custom-call(s32[1]{0:T(128)} %bitcast.turn_ref, s32[4]{0:T(128)} %iota.11.column_ref, s32[32,16]{1,0:T(8,128)} %fusion.flags_ref, s32[4,128]{1,0:T(4,128)} %convert_reduce_fusion.marks_ref, bf16[4,43,128,128]{3,2,1,0:T(8,128)(2,1)} %bitcast.56, bf16[4,26,128,128]{3,2,1,0:T(8,128)(2,1)} %bitcast.60, ...), custom_call_target="tpu_custom_call" | custom-call | flops 1 | bytes 1 | tf_op jit(solution)/shard_map/multiply/pallas_call | solution.py:346
  (54 shorter events, 8.3 us)
Async XLA Ops:
  6.5 8.5 %copy-start.6 = (s32[16,16]{1,0:T(8,128)S(1)}, s32[16,16]{1,0:T(8,128)}, u32[]{:S(2)}) copy-start(s32[16,16]{1,0:T(8,128)} %other_ref.3) | copy-start | bytes 3076
  6.5 116.1 %all-gather.13.cloned.1.call-start = ((), (), s32[]{:S(2)}) async-start(), calls=%async_computation.4 | async-start | bytes 7045120 | tf_op jit(solution)/shard_map/all_gather | solution.py:412
  15.0 175.2 %all-gather.15.cloned.1.call-start = ((), (), s32[]{:S(2)}) async-start(), calls=%async_computation.5 | async-start | bytes 4259840 | tf_op jit(solution)/shard_map/all_gather | solution.py:412
  23.5 10.7 %collective-permute-start.2 = (bf16[96,128,128]{2,1,0:T(8,128)(2,1)}, bf16[96,128,128]{2,1,0:T(8,128)(2,1)}, u32[]{:S(2)}, u32[]{:S(2)}) collective-permute-start(bf16[96,128,128]{2,1,0:T(8,128)(2,1)} %get-tuple-element.45.refs_0_), channel_id=1, source_target_pairs={{0,8},{8,0},{16,24},{24,16},{1,9},{9,1},{17,25},{25,17},{2,10},{10... | collective-permute-start | bytes 9437192 | tf_op jit(solution)/shard_map/ppermute | solution.py:439
  24.0 71.5 %collective-permute-start.1 = (bf16[96,128,128]{2,1,0:T(8,128)(2,1)}, bf16[96,128,128]{2,1,0:T(8,128)(2,1)S(1)}, u32[]{:S(2)}, u32[]{:S(2)}) collective-permute-start(bf16[96,128,128]{2,1,0:T(8,128)(2,1)} %get-tuple-element.45.refs_0_), channel_id=1, source_target_pairs={{0,16},{8,24},{16,0},{24,8},{1,17},{9,25},{17,1},{25,9},{2,18},{10... | collective-permute-start | bytes 9437192 | tf_op jit(solution)/shard_map/ppermute | solution.py:432
  26.6 191.9 %all-gather.17.cloned.1.call-start = ((), (), s32[]{:S(2)}) async-start(), calls=%async_computation.6 | async-start | bytes 1310720 | tf_op jit(solution)/shard_map/all_gather | solution.py:412
  26.6 8.8 %collective-permute-start.3 = (bf16[25,128,128]{2,1,0:T(8,128)(2,1)}, bf16[25,128,128]{2,1,0:T(8,128)(2,1)}, u32[]{:S(2)}, u32[]{:S(2)}) collective-permute-start(bf16[25,128,128]{2,1,0:T(8,128)(2,1)} %get-tuple-element.57.refs_1_), channel_id=1, source_target_pairs={{0,8},{8,0},{16,24},{24,16},{1,9},{9,1},{17,25},{25,17},{2,10},{10... | collective-permute-start | bytes 2457608 | tf_op jit(solution)/shard_map/ppermute | solution.py:439
  26.8 8.6 %collective-permute-start.4 = (bf16[24,128,128]{2,1,0:T(8,128)(2,1)}, bf16[24,128,128]{2,1,0:T(8,128)(2,1)}, u32[]{:S(2)}, u32[]{:S(2)}) collective-permute-start(bf16[24,128,128]{2,1,0:T(8,128)(2,1)} %get-tuple-element.59.refs_2_), channel_id=1, source_target_pairs={{0,8},{8,0},{16,24},{24,16},{1,9},{9,1},{17,25},{25,17},{2,10},{10... | collective-permute-start | bytes 2359304 | tf_op jit(solution)/shard_map/ppermute | solution.py:439
  95.4 14.5 %copy-start.1 = (bf16[96,128,128]{2,1,0:T(8,128)(2,1)}, bf16[96,128,128]{2,1,0:T(8,128)(2,1)S(1)}, u32[]{:S(2)}) copy-start(bf16[96,128,128]{2,1,0:T(8,128)(2,1)S(1)} %collective-permute-done.1.refs_0_) | copy-start | bytes 9437188
  95.4 20.2 %collective-permute-start.5 = (bf16[96,128,128]{2,1,0:T(8,128)(2,1)S(1)}, bf16[96,128,128]{2,1,0:T(8,128)(2,1)}, u32[]{:S(2)}, u32[]{:S(2)}) collective-permute-start(bf16[96,128,128]{2,1,0:T(8,128)(2,1)S(1)} %collective-permute-done.1.refs_0_), channel_id=1, source_target_pairs={{0,8},{8,0},{16,24},{24,16},{1,9},{9,1},{17,25},{25,17},{2,10},{10... | collective-permute-start | bytes 9437192 | tf_op jit(solution)/shard_map/ppermute | solution.py:446
  101.5 48.1 %collective-permute-start.9 = (bf16[24,128,128]{2,1,0:T(8,128)(2,1)}, bf16[24,128,128]{2,1,0:T(8,128)(2,1)}, u32[]{:S(2)}, u32[]{:S(2)}) collective-permute-start(bf16[24,128,128]{2,1,0:T(8,128)(2,1)} %get-tuple-element.59.refs_2_), channel_id=1, source_target_pairs={{0,16},{8,24},{16,0},{24,8},{1,17},{9,25},{17,1},{25,9},{2,18},{10... | collective-permute-start | bytes 2359304 | tf_op jit(solution)/shard_map/ppermute | solution.py:432
  103.3 46.3 %collective-permute-start.7 = (bf16[25,128,128]{2,1,0:T(8,128)(2,1)}, bf16[25,128,128]{2,1,0:T(8,128)(2,1)}, u32[]{:S(2)}, u32[]{:S(2)}) collective-permute-start(bf16[25,128,128]{2,1,0:T(8,128)(2,1)} %get-tuple-element.57.refs_1_), channel_id=1, source_target_pairs={{0,16},{8,24},{16,0},{24,8},{1,17},{9,25},{17,1},{25,9},{2,18},{10... | collective-permute-start | bytes 2457608 | tf_op jit(solution)/shard_map/ppermute | solution.py:432
  127.4 24.6 %copy-start.8 = (f32[8,128]{1,0:T(8,128)S(1)}, f32[8,128]{1,0:T(8,128)}, u32[]{:S(2)}) copy-start(f32[8,128]{1,0:T(8,128)} %reduce_max.15.refs_2_) | copy-start | bytes 12292
  149.5 11.6 %collective-permute-start.8 = (bf16[25,128,128]{2,1,0:T(8,128)(2,1)}, bf16[25,128,128]{2,1,0:T(8,128)(2,1)S(1)}, u32[]{:S(2)}, u32[]{:S(2)}) collective-permute-start(bf16[25,128,128]{2,1,0:T(8,128)(2,1)} %collective-permute-done.7.refs_1_), channel_id=1, source_target_pairs={{0,8},{8,0},{16,24},{24,16},{1,9},{9,1},{17,25},{25,17},{2,10},{10... | collective-permute-start | bytes 2457608 | tf_op jit(solution)/shard_map/ppermute | solution.py:472
  149.6 11.5 %collective-permute-start.10 = (bf16[24,128,128]{2,1,0:T(8,128)(2,1)}, bf16[24,128,128]{2,1,0:T(8,128)(2,1)S(1)}, u32[]{:S(2)}, u32[]{:S(2)}) collective-permute-start(bf16[24,128,128]{2,1,0:T(8,128)(2,1)} %collective-permute-done.9.refs_2_), channel_id=1, source_target_pairs={{0,8},{8,0},{16,24},{24,16},{1,9},{9,1},{17,25},{25,17},{2,10},{10... | collective-permute-start | bytes 2359304 | tf_op jit(solution)/shard_map/ppermute | solution.py:472
  150.1 68.4 %collective-permute-start.12 = (s16[528,1280]{1,0:T(8,128)(2,1)}, s16[528,1280]{1,0:T(8,128)(2,1)S(1)}, u32[]{:S(2)}, u32[]{:S(2)}) collective-permute-start(s16[528,1280]{1,0:T(8,128)(2,1)} %multiply.4), channel_id=1, source_target_pairs={{0,1},{1,0},{2,3},{3,2},{4,5},{5,4},{6,7},{7,6},{8,9},{9,8},{10,11... | collective-permute-start | bytes 4055048 | tf_op jit(solution)/shard_map/ppermute | solution.py:482
  152.0 1.2 collective-permute-start
  153.2 7.3 %collective-permute-start.6 = (f32[8,128]{1,0:T(8,128)S(1)}, f32[8,128]{1,0:T(8,128)S(1)}, u32[]{:S(2)}, u32[]{:S(2)}) collective-permute-start(f32[8,128]{1,0:T(8,128)S(1)} %convert_maximum_fusion), channel_id=1, source_target_pairs={{0,16},{8,24},{16,0},{24,8},{1,17},{9,25},{17,1},{25,9},{2,18},{10... | collective-permute-start | bytes 12296 | tf_op jit(solution)/shard_map/ppermute | solution.py:368
  161.1 0.9 copy-start.5
  161.1 1.2 copy-start.3
  185.4 30.9 %collective-permute-start.11 = (s16[528,768]{1,0:T(8,128)(2,1)}, s16[528,768]{1,0:T(8,128)(2,1)S(1)}, u32[]{:S(2)}, u32[]{:S(2)}) collective-permute-start(s16[528,768]{1,0:T(8,128)(2,1)} %multiply.5), channel_id=1, source_target_pairs={{0,1},{1,0},{2,3},{3,2},{4,5},{5,4},{6,7},{7,6},{8,9},{9,8},{10,11... | collective-permute-start | bytes 2433032 | tf_op jit(solution)/shard_map/ppermute | solution.py:482
  216.3 2.8 %copy-start.4 = (s16[528,768]{1,0:T(8,128)(2,1)}, s16[528,768]{1,0:T(8,128)(2,1)S(1)}, u32[]{:S(2)}) copy-start(s16[528,768]{1,0:T(8,128)(2,1)S(1)} %collective-permute-done.11.refs_6_) | copy-start | bytes 2433028
  218.5 1.1 copy-start.2
  219.6 15.3 %copy-start.7 = (s32[8,16]{1,0:T(8,128)S(1)}, s32[8,16]{1,0:T(8,128)}, u32[]{:S(2)}) copy-start(s32[8,16]{1,0:T(8,128)} %flags_ref.2) | copy-start | bytes 1540
Sparse Core Ops, SparseCore 0:
  15.1 107.2 all-gather.12
  124.1 66.1 all-gather.14
  191.9 26.5 all-gather.16

commit v4 on v3

v4 whole, which is shorter than its diff:
```python
import functools
import math
import typing

import jax
import jax.numpy as jnp
from jax import lax
from jax.experimental import pallas as pl
from jax.experimental.pallas import tpu as pltpu
from jax.sharding import PartitionSpec as P

BLOCK = 128
VMEM_LIMIT = 56 * 1024 * 1024
TILE_ROOM = 256 * 16
SMALL = pl.CostEstimate(flops=1, bytes_accessed=1, transcendentals=0)
LARGE = pl.CostEstimate(flops=10**12, bytes_accessed=1, transcendentals=0)


def keep_blocks(values, occupancy):
    height, breadth = values.shape
    tiled = values.reshape(height // BLOCK, BLOCK, breadth // BLOCK, BLOCK)
    flags = occupancy.astype(values.dtype)
    return (tiled * flags[:, None, :, None]).reshape(height, breadth)


def along(part, axis, size, dim):
    me, length = lax.axis_index(axis), part.shape[dim]
    shape = list(part.shape)
    shape[dim] *= size
    whole = lax.dynamic_update_slice_in_dim(jnp.zeros(shape, part.dtype), part, me * length, dim)
    for hop in range(1, size):
        came = lax.ppermute(part, axis, [(i, (i + hop) % size) for i in range(size)])
        whole = lax.dynamic_update_slice_in_dim(whole, came, (me - hop + size) % size * length, dim)
    return whole


def whole_slab(sizes, a_tiles, a_occupancy, b_tiles, b_occupancy):
    rows, cols, layers = sizes
    a_slab = along(keep_blocks(a_tiles, a_occupancy), "col", cols, 1)
    b_kept = keep_blocks(b_tiles, b_occupancy)
    partial_value = jnp.zeros((a_slab.shape[0], b_kept.shape[1]), jnp.float32)
    for hop in range(rows):
        part = lax.ppermute(b_kept, "row", [(i, (i + hop) % rows) for i in range(rows)]) if hop else b_kept
        at = (lax.axis_index("row") - hop + rows) % rows * part.shape[0]
        beside = lax.dynamic_slice_in_dim(a_slab, at, part.shape[0], 1)
        partial_value += jnp.dot(beside, part, preferred_element_type=jnp.float32)
    me, length = lax.axis_index("layer"), partial_value.shape[0] // layers
    total = lax.dynamic_slice_in_dim(partial_value, me * length, length)
    for hop in range(1, layers):
        given = lax.dynamic_slice_in_dim(partial_value, (me + hop) % layers * length, length)
        total += lax.ppermute(given, "layer", [(i, (i + hop) % layers) for i in range(layers)])
    return total


def slots_for(blocks, spread):
    if blocks < 16:
        return blocks + 1
    room = (blocks * 7 + 15) // 16 + int(round(spread * blocks**0.5))
    return min(blocks, room) + 1


def cuts_for(stages, spread):
    cuts, blocks = [0], 0
    for stage in stages:
        blocks += stage.rows * stage.wide
        cuts.append(max(slots_for(blocks, spread), cuts[-1] + 1))
    return cuts


class Stage(typing.NamedTuple):
    row: int
    rows: int
    first: int
    wide: int


def header_of(occupancy):
    rows, columns = occupancy.shape
    flags = occupancy.astype(jnp.bfloat16)
    return jnp.pad(flags, ((0, BLOCK - rows), (0, BLOCK - columns)))


MARKS, OVER = BLOCK - 8, BLOCK - 1


def pack_kernel(place, stages, ends, cuts, other, columns, turn_ref, flags_ref, other_ref, header_ref, values_ref, *refs):
    n = len(cuts) - 1
    parts, (whole, held, sem, out_sems) = refs[:n], refs[-4:]
    header = pltpu.make_async_copy(header_ref.at[:BLOCK, :BLOCK], held.at[0], sem)
    if other is None:
        header.start()
    else:
        held[0] = jnp.zeros_like(held[0])
    lane = lax.broadcasted_iota(jnp.int32, (16, BLOCK), 1)

    def step_of(stage):
        def step(u, carry):
            slot, notes = carry
            row, column = place(stage, u, turn_ref[0])
            flag = flags_ref[row, column]

            @pl.when(flag > 0)
            def _():
                pltpu.make_async_copy(
                    values_ref.at[
                        pl.ds(pl.multiple_of(row * BLOCK, BLOCK), BLOCK),
                        pl.ds(pl.multiple_of(column * BLOCK, BLOCK), BLOCK),
                    ],
                    held.at[jnp.minimum(slot, cuts[-1])],
                    sem,
                ).start()

            if other is not None:
                code = (stage.row + u // stage.wide) * columns + stage.first + u % stage.wide
                notes = jnp.where(lane == jnp.where(flag > 0, slot, BLOCK), code.astype(jnp.float32), notes)
            return slot + flag, notes

        return step

    slot, over, marks = jnp.int32(1), jnp.int32(0), []
    notes = jnp.zeros((16, BLOCK), jnp.float32)
    for stage, cut in zip(stages, ends[1:]):
        marks.append(slot)
        slot, notes = lax.fori_loop(0, stage.rows * stage.wide, step_of(stage), (slot, notes), unroll=4)
        over = jnp.maximum(over, jnp.where(slot > cut, 1, 0))
    marks.append(slot)
    if other is not None:
        other_place, other_stages, other_ends = other
        spent = jnp.int32(1)
        for stage, cut in zip(other_stages, other_ends[1:]):

            def count(u, spent):
                row, column = other_place(stage, u, turn_ref[0])
                return spent + other_ref[row, column]

            spent = lax.fori_loop(0, stage.rows * stage.wide, count, spent, unroll=16)
            over = jnp.maximum(over, jnp.where(spent > cut, 1, 0))

    def settle(t, _):
        header.wait()
        return 0

    lax.fori_loop(0, slot if other is None else slot - 1, settle, 0)
    if other is not None:
        notes = jnp.where(lane >= MARKS, over.astype(jnp.float32), notes)
        for i, mark in enumerate(marks):
            notes = jnp.where(lane == MARKS + i, mark.astype(jnp.float32), notes)
        held[0, :16, :] = notes.astype(held.dtype)
    copies = [
        pltpu.make_async_copy(held.at[pl.ds(lo, hi - lo)], part, out_sems.at[i])
        for i, (part, lo, hi) in enumerate(zip(parts, cuts[:-1], cuts[1:]))
    ]
    if other is None:
        copies.append(pltpu.make_async_copy(held.at[pl.ds(0, cuts[-1])], whole, out_sems.at[n]))
    for copy in copies:
        copy.start()
    for copy in copies:
        copy.wait()


def pack(values, occupancy, turn, place, stages, ends, cuts, other_flags, other):
    n = len(cuts) - 1
    sizes = [hi - lo for lo, hi in zip(cuts[:-1], cuts[1:])] + [cuts[-1] if other is None else 1]
    if other is None:
        header = header_of(occupancy)
    else:
        header = values
        assert cuts[-1] <= MARKS and len(stages) < OVER - MARKS and occupancy.size <= 256
    *parts, whole = pl.pallas_call(
        functools.partial(pack_kernel, place, stages, ends, cuts, other, occupancy.shape[1]),
        grid_spec=pltpu.PrefetchScalarGridSpec(
            num_scalar_prefetch=3,
            grid=(),
            in_specs=[pl.BlockSpec(memory_space=pl.ANY)] * 2,
            out_specs=[pl.BlockSpec(memory_space=pl.ANY)] * (n + 1),
            scratch_shapes=[
                pltpu.VMEM((cuts[-1] + 1, BLOCK, BLOCK), values.dtype),
                pltpu.SemaphoreType.DMA,
                pltpu.SemaphoreType.DMA((n + 1,)),
            ],
        ),
        out_shape=[jax.ShapeDtypeStruct((size, BLOCK, BLOCK), values.dtype) for size in sizes],
        compiler_params=pltpu.CompilerParams(vmem_limit_bytes=VMEM_LIMIT),
        cost_estimate=SMALL,
        name="pack",
    )(turn, occupancy, other_flags, header, values)
    return parts, whole


def after(values, others):
    k = len(values)
    whole = pl.BlockSpec(memory_space=pl.ANY)
    return pl.pallas_call(
        lambda *refs: None,
        in_specs=[whole] * (k + len(others)),
        out_specs=[whole] * k,
        out_shape=[jax.ShapeDtypeStruct(value.shape, value.dtype) for value in values],
        input_output_aliases={i: i for i in range(k)},
        cost_estimate=SMALL,
        name="after",
    )(*values, *others)


def load_list(parts, cuts, held, sems):
    return [
        pltpu.make_async_copy(part, held.at[pl.ds(lo, hi - lo)], sems.at[i])
        for i, (part, lo, hi) in enumerate(zip(parts, cuts[:-1], cuts[1:]))
    ]


def unpack_b_kernel(k_blocks, first, stop, cuts, shard_ref, flags_ref, *refs):
    parts, (out_ref, done_ref, held, sems, sem) = refs[: len(cuts) - 1], refs[-5:]
    done_ref[0] = 0
    nothing = cuts[-1]
    copies = load_list(parts, cuts, held, sems)
    for copy in copies:
        copy.start()
    held[nothing] = jnp.zeros_like(held[nothing])

    def flag_of(t):
        return flags_ref[t % k_blocks, t // k_blocks]

    slot = lax.fori_loop(0, first * k_blocks, lambda t, slot: slot + flag_of(t), jnp.int32(1), unroll=8)
    for copy in copies:
        copy.wait()
    base = shard_ref[0] * k_blocks

    def step(t, slot):
        flag = flag_of(first * k_blocks + t)
        pltpu.make_async_copy(
            held.at[jnp.where(flag > 0, jnp.minimum(slot, nothing), nothing)],
            out_ref.at[
                pl.ds(pl.multiple_of((base + t % k_blocks) * BLOCK, BLOCK), BLOCK),
                pl.ds(pl.multiple_of(t // k_blocks * BLOCK, BLOCK), BLOCK),
            ],
            sem,
        ).start()
        return slot + flag

    lax.fori_loop(0, (stop - first) * k_blocks, step, slot, unroll=8)
    written = out_ref.at[pl.ds(pl.multiple_of(base * BLOCK, BLOCK), k_blocks * BLOCK)]
    pltpu.make_async_copy(written, written, sem).wait()


def unpack_b(parts, flags, shard, shards, first, stop, k_blocks, cuts, into, token):
    n = len(parts)
    operands = [*parts, token] + ([] if into is None else [into])
    return pl.pallas_call(
        functools.partial(unpack_b_kernel, k_blocks, first, stop, cuts),
        grid_spec=pltpu.PrefetchScalarGridSpec(
            num_scalar_prefetch=2,
            grid=(),
            in_specs=[pl.BlockSpec(memory_space=pl.ANY)] * len(operands),
            out_specs=[pl.BlockSpec(memory_space=pl.ANY), pl.BlockSpec(memory_space=pltpu.SMEM)],
            scratch_shapes=[
                pltpu.VMEM((cuts[-1] + 1, BLOCK, BLOCK), parts[0].dtype),
                pltpu.SemaphoreType.DMA((n,)),
                pltpu.SemaphoreType.DMA,
            ],
        ),
        out_shape=[
            jax.ShapeDtypeStruct((shards * k_blocks * BLOCK, (stop - first) * BLOCK), parts[0].dtype),
            jax.ShapeDtypeStruct((1,), jnp.int32),
        ],
        input_output_aliases={} if into is None else {3 + n: 0},
        compiler_params=pltpu.CompilerParams(vmem_limit_bytes=VMEM_LIMIT),
        cost_estimate=SMALL,
        name="unpack_b",
    )(shard, flags, *operands)


def multiply_kernel(plan, notes_ref, *refs):
    stages, k_blocks, cuts, shards, halves, given, carried, tokens, pieces, starts, ends = plan
    stage, g = stages[-1], len(stages) - 1
    rows, wide = stage.rows, stage.wide
    n = len(cuts) - 1
    parts, refs = refs[:n], refs[n:]
    b_refs, refs = refs[:halves], refs[halves:]
    codes_in, refs = refs[: halves * given], refs[halves * given :]
    before, refs = refs[:carried], refs[carried + tokens :]
    over_ref, out_ref, dense, sem, total = refs

    def fill():
        dense[...] = jnp.zeros_like(dense)
        started = jnp.int32(0)
        for s in range(shards):
            base = s * wide - stage.first

            for part, lo, hi in zip(parts, cuts[:-1], cuts[1:]):

                def put(slot, _):
                    code = notes_ref[s, slot]
                    row, k = lax.div(code, k_blocks), lax.rem(code, k_blocks)
                    pltpu.make_async_copy(
                        part.at[s, slot - lo],
                        dense.at[
                            pl.ds(pl.multiple_of((row - stage.row) * BLOCK, BLOCK), BLOCK),
                            pl.ds(pl.multiple_of((base + k) * BLOCK, BLOCK), BLOCK),
                        ],
                        sem,
                    ).start()
                    return 0

                first = jnp.maximum(notes_ref[s, MARKS + g], lo)
                stop = jnp.maximum(jnp.minimum(notes_ref[s, MARKS + g + 1], hi), first)
                lax.fori_loop(first, stop, put, 0)
                started += stop - first

        def settle(t, _):
            pltpu.make_async_copy(parts[0].at[0, 0], dense.at[:BLOCK, :BLOCK], sem).wait()
            return 0

        lax.fori_loop(0, started, settle, 0)

    pl.when(pl.program_id(0) == 0)(fill)

    def code(value):
        share = rows // pieces
        for q in range(pieces):
            base = q * (share * BLOCK + 16)
            powers = []
            for r in range(share):
                some = value[(q * share + r) * BLOCK : (q * share + r + 1) * BLOCK]
                top = jnp.max(jnp.abs(some), axis=0, keepdims=True)
                power = jnp.clip(jnp.ceil(jnp.log2(top)), -60.0, 60.0)
                some = jnp.clip(jnp.round(some * jnp.exp2(15.0 - power)), -32767.0, 32767.0)
                out_ref[base + r * BLOCK : base + (r + 1) * BLOCK] = some.astype(jnp.int32).astype(jnp.int16)
                powers.append(power)
            flag = jnp.broadcast_to(over_ref[0:1, 0:1], powers[0].shape)
            notes = jnp.concatenate(powers + [flag] * (16 - share), axis=0)
            out_ref[base + share * BLOCK : base + share * BLOCK + 16] = notes.astype(jnp.int32).astype(jnp.int16)

    def finish(value, h):
        for r in range(rows):
            span = slice(r * BLOCK, (r + 1) * BLOCK)
            some = value[span]
            for q in range(given):
                codes = codes_in[q * halves + h]
                notes = codes[rows * BLOCK : rows * BLOCK + 16].astype(jnp.int32).astype(jnp.float32)
                some += codes[span].astype(jnp.int32).astype(jnp.float32) * jnp.exp2(notes[r : r + 1] - 15.0)
            for earlier in before:
                some += earlier[span]
            out_ref[span] = some

    for h, b_ref in enumerate(b_refs):

        @pl.when((pl.program_id(0) >= starts[h]) & (pl.program_id(0) < ends[h]))
        def _():
            b_here = b_ref[...].reshape(-1, b_ref.shape[-1])
            total[...] = jnp.dot(dense[...], b_here, preferred_element_type=jnp.float32)
            if pieces:
                code(total)
            else:
                finish(total, h)


def multiply(
    parts, notes, stages, k_blocks, cuts, b_halves, over, pieces=0, received=(), before=(), tokens=()
):
    shards, halves = parts[0].shape[0], len(b_halves)
    stage = stages[-1]
    n = len(cuts) - 1
    widths = [b_half.shape[1] for b_half in b_halves]
    shared = math.gcd(*widths)
    tile = max(t for t in (BLOCK, 256, 512) if shared % t == 0 and t * stage.wide <= TILE_ROOM)
    ends = [sum(widths[: h + 1]) // tile for h in range(halves)]
    starts = [0] + ends[:-1]
    deep = math.gcd(math.gcd(stage.first, stage.wide), k_blocks)
    layers, skip = stage.wide // deep, stage.first // deep
    assert skip % layers == 0
    tall = stage.rows * BLOCK
    whole = pl.BlockSpec(memory_space=pl.ANY)

    def at(h, *fixed):
        return lambda j, *_: (*fixed, jnp.clip(j - starts[h], 0, ends[h] - starts[h] - 1))

    in_specs = [whole] * n
    operands = [*parts[:n]]
    for h, b_half in enumerate(b_halves):
        in_specs.append(pl.BlockSpec((shards, layers, deep * BLOCK, tile), at(h, 0, skip // layers, 0)))
        operands.append(b_half.reshape(shards, k_blocks // deep, deep * BLOCK, widths[h]))
    for pairs in received:
        for h, codes in enumerate(pairs):
            in_specs.append(pl.BlockSpec((tall + 16, tile), at(h, 0)))
            operands.append(codes)
    in_specs += [pl.BlockSpec((tall, tile), lambda j, *_: (0, j))] * len(before)
    operands += [*before]
    in_specs += [whole] * len(tokens) + [pl.BlockSpec(memory_space=pltpu.VMEM)]
    operands += [*tokens, over]
    high = tall + 16 * pieces
    plan = (stages, k_blocks, cuts, shards, halves, len(received), len(before), len(tokens), pieces, starts, ends)
    return pl.pallas_call(
        functools.partial(multiply_kernel, plan),
        grid_spec=pltpu.PrefetchScalarGridSpec(
            num_scalar_prefetch=1,
            grid=(ends[-1],),
            in_specs=in_specs,
            out_specs=pl.BlockSpec((high, tile), lambda j, *_: (0, j)),
            scratch_shapes=[
                pltpu.VMEM((tall, shards * stage.wide * BLOCK), b_halves[0].dtype),
                pltpu.SemaphoreType.DMA,
                pltpu.VMEM((tall, tile), jnp.float32),
            ],
        ),
        out_shape=jax.ShapeDtypeStruct((high, sum(widths)), jnp.int16 if pieces else jnp.float32),
        compiler_params=pltpu.CompilerParams(vmem_limit_bytes=VMEM_LIMIT),
        cost_estimate=SMALL,
        name="multiply",
    )(notes, *operands)


def largest_over(value, axis, size):
    step = 1
    while step < size:
        value = jnp.maximum(value, lax.ppermute(value, axis, [(i, i ^ step) for i in range(size)]))
        step *= 2
    return value


def per_device(sizes, a_tiles, a_occupancy, b_tiles, b_occupancy):
    rows, cols, layers = sizes
    me_row, me_col, me_layer = (lax.axis_index(axis).astype(jnp.int32) for axis in ("row", "col", "layer"))
    a_rows, a_k = a_occupancy.shape
    b_k, b_columns = b_occupancy.shape
    piece = a_rows // layers
    given = a_rows - piece
    turn = me_layer.reshape(1)

    def a_place(stage, u, layer):
        row, k = stage.row + u // stage.wide, stage.first + u % stage.wide
        return lax.rem(row + (layer + 1) * piece, a_rows), k

    def b_place(stage, u, _):
        return stage.first + u % stage.wide, stage.row + u // stage.wide

    early = a_k * 3 // 4
    a_stages = [Stage(0, given, 0, a_k), Stage(given, piece, 0, early), Stage(given, piece, early, a_k - early)]
    half = b_columns * 5 // 8
    b_stages = [Stage(0, half, 0, b_k), Stage(half, b_columns - half, 0, b_k)]
    a_cuts, b_cuts = cuts_for(a_stages, 1.77), cuts_for(b_stages, 2.0)

    a_parts, _ = pack(a_tiles, a_occupancy, turn, a_place, a_stages, a_cuts, a_cuts, b_occupancy, (b_place, b_stages, b_cuts))
    a_parts = [lax.all_gather(part, "col", axis=0) for part in a_parts]
    b_parts, b_whole = pack(b_tiles, b_occupancy, turn, b_place, b_stages, b_cuts, b_cuts, b_occupancy, None)

    pair = 2 if rows % 2 == 0 else 1
    swap = [(r, r ^ 1) for r in range(rows)]
    hops = range(1, rows // pair)
    shards = [lax.rem(me_row - pair * hop + rows, rows) for hop in range(rows // pair)]
    b_dense = [None] * len(b_stages)

    def across(part, hop):
        return lax.ppermute(part, "row", [(r, (r + pair * hop) % rows) for r in range(rows)])

    def unpack(h, shard, parts, cuts, token):
        stage = b_stages[h]
        flags = parts[0][0, :b_k, :b_columns].astype(jnp.int32)
        b_dense[h], token = unpack_b(
            parts, flags, shard.reshape(1), rows, stage.row, stage.row + stage.rows, b_k, cuts, b_dense[h], token
        )
        return token

    came = [across(b_parts[0], hop) for hop in hops]
    cut = [0, b_cuts[-1]]
    token = turn
    for h in range(2):
        token = unpack(h, shards[0], [b_whole], cut, token)
    if pair == 2:
        other = lax.ppermute(b_whole, "row", swap)
        for h in range(2):
            token = unpack(h, shards[0] ^ 1, [other], cut, token)

    *came, b_second = after([*came, b_parts[1]], [token])
    sides = [[part] for part in came]
    if pair == 2:
        sides += [[lax.ppermute(part, "row", swap)] for part in came]
    came = [across(b_second, hop) for hop in hops]
    places = [shards[hop] ^ side for side in range(pair) for hop in hops]
    for place, parts in zip(places, sides):
        token = unpack(0, place, parts, b_cuts[:2], token)
    notes = a_parts[0][:, 0, 0].astype(jnp.int32)
    over = jnp.max(a_parts[0][:, 0, :8, MARKS:].astype(jnp.float32), axis=0)[:, OVER - MARKS :]
    over = jnp.broadcast_to(over, (8, BLOCK))

    def product_of(g, halves, over, **more):
        return multiply(a_parts, notes, a_stages[: g + 1], a_k, a_cuts[: g + 2], halves, over, **more)

    high = piece * BLOCK + 16

    def exchange(codes):
        out = []
        for q in range(layers - 1):
            there = [(i, (i + 1 + q) % layers) for i in range(layers)]
            out.append(lax.ppermute(codes[q * high : (q + 1) * high], "layer", there))
        return out

    codes = product_of(0, b_dense[:1], over, pieces=layers - 1, tokens=[token])

    came = after(came, [codes])
    first = exchange(codes)
    more = [*came]
    if pair == 2:
        more += [lax.ppermute(part, "row", swap) for part in came]
    for place, parts, part in zip(places, sides, more):
        token = unpack(1, place, [*parts, part], b_cuts, token)
    over = largest_over(over, "row", rows)
    codes = product_of(0, b_dense[1:], over, pieces=layers - 1, tokens=[token])

    second = exchange(codes)
    product = product_of(1, b_dense, over, tokens=[codes])

    received = [*zip(first, second)]
    product = product_of(2, b_dense, over, received=received, before=(product,))
    over = over[0, 0]
    for codes in second:
        over = jnp.maximum(over, codes[-1, 0].astype(jnp.float32))
    return lax.cond(
        over > 0,
        lambda: whole_slab(sizes, a_tiles, a_occupancy, b_tiles, b_occupancy),
        lambda: product,
    )


def solution(mesh):
    sizes = tuple(mesh.shape[axis] for axis in ("row", "col", "layer"))
    in_specs = (
        P("row", ("layer", "col")),
        P("row", ("layer", "col")),
        P(("layer", "row"), "col"),
        P(("layer", "row"), "col"),
    )
    out_specs = P(("row", "layer"), "col")
    return jax.shard_map(
        functools.partial(per_device, sizes), mesh=mesh, in_specs=in_specs, out_specs=out_specs, check_vma=False
    )
```

time: 244 us -> 242 us (level)
  Pallas kernels: 141 us -> 137 us
  local copies, waits for them, and re-layouts: 6.94 us -> 10 us
  other arithmetic: 9.91 us -> 7.43 us
    all_gather x3, waiting for transfers between devices: 3.46 us -> 18.4 us  [per_device(): a_parts = [lax.all_gather(part, 'col', axis=0) for part in a_parts]]
    ppermute x3 -> x2, waiting for transfers between devices: 54.3 us -> 40.5 us  [across(): lax.ppermute(part, 'row', [(r, (r + pair * hop) % rows) for r in range(ro...]
    pallas_call x4, Pallas kernels: 79.7 us -> 69.2 us  [multiply(): pl.pallas_call(functools.partial(multiply_kernel, plan), grid_spec=pltpu....]
    unnamed x16 -> x18, local copies, waits for them, and re-layouts: 1.69 us -> 6.91 us
    pallas_call x8, Pallas kernels: 46 us -> 51.1 us  [unpack_b(): pl.pallas_call(functools.partial(unpack_b_kernel, k_blocks, first, stop,...]
    convert_element_type x6 -> x5, other arithmetic: 7.31 us -> 5.73 us  [the longest x4 4.47 us: unpack(): flags = parts[0][0, :b_k, :b_columns].astype(jnp.int32)]
  transfers between devices with their start and end apart: 16 -> 12, of which waited for: 4 -> 5; matrix products, arithmetic and copies ran while one was open for 6% -> 4% of each run, Pallas kernels for 49% -> 49%
where the time goes in v4:
time: 242 us; the launch traced here: 240 us
  Pallas kernels  137 us (57%)
  waiting for transfers between devices  60.6 us (25%)
  between operations  14.7 us (6%)
  local copies, waits for them, and re-layouts  10 us (4%)
  starting transfers between devices  9.98 us (4%)
  other arithmetic  7.43 us (3%)
    pallas_call x4, Pallas kernels, multiply(): pl.pallas_call(functools.partial(multiply_kernel, plan), grid_spec=pltpu....  69.2 us
    pallas_call x8, Pallas kernels, unpack_b(): pl.pallas_call(functools.partial(unpack_b_kernel, k_blocks, first, stop,...  51.1 us
    ppermute x2, waiting for transfers between devices, across(): lax.ppermute(part, 'row', [(r, (r + pair * hop) % rows) for r in range(ro...  40.5 us
    all_gather x3, waiting for transfers between devices, per_device(): a_parts = [lax.all_gather(part, 'col', axis=0) for part in a_parts]  18.4 us
    pallas_call x2, Pallas kernels, pack(): pl.pallas_call(functools.partial(pack_kernel, place, stages, ends, cuts,...  15.7 us
    unnamed x18, local copies, waits for them, and re-layouts  6.91 us
  transfers between devices with their start and end apart: 12, of which 5 were waited for; matrix products, arithmetic and copies ran while one was open for 4% of the time, Pallas kernels for 49%

profile of v4, /device:TPU:0, one launch (start us, length us, event | category | flops | bytes accessed | tf_op | source)
XLA Modules:
  0.0 239.7 jit_solution(10293070084577648372)
XLA Ops:
  6.5 6.9 %pack.2 = (bf16[43,128,128]{2,1,0:T(8,128)(2,1)}, bf16[26,128,128]{2,1,0:T(8,128)(2,1)}, bf16[8,128,128]{2,1,0:T(8,128)(2,1)}, bf16[1,128,128]{2,1,0:T(8,128)(2,1)}) custom-call(s32[1]{0:T(128)} %bitcast.turn_ref.refs_1_, s32[8,16]{1,0:T(8,128)} %flags_ref.2, s32[16,16]{1,0:T(8,128)} %other_ref.3, bf16[1024,2048]{1,0:T(8,128)(2,1)} %values_ref.2, ...), custom_call_target="tpu_custom_call" | custom-call | flops 1 | bytes 1 | tf_op jit(solution)/shard_map/pack/pallas_call | solution.py:169
  14.2 8.8 %pack.3 = (bf16[96,128,128]{2,1,0:T(8,128)(2,1)}, bf16[49,128,128]{2,1,0:T(8,128)(2,1)}, bf16[145,128,128]{2,1,0:T(8,128)(2,1)}) custom-call(s32[1]{0:T(128)} %bitcast.turn_ref.refs_1_, s32[16,16]{1,0:T(8,128)S(1)} %copy-done.8, s32[16,16]{1,0:T(8,128)S(1)} %copy-done.8, bf16[128,128]{1,0:T(8,128)(2,1)} %pad.4.header_ref, bf16[2048,2048]{1,0:T(8,128)(2,1)} %values_ref.3), custom_call_target="tpu_custom_call" | custom-call | flops 1 | bytes 1 | tf_op jit(solution)/shard_map/pack/pallas_call | solution.py:169
  23.4 2.8 %collective-permute-start.9 = (bf16[96,128,128]{2,1,0:T(8,128)(2,1)}, bf16[96,128,128]{2,1,0:T(8,128)(2,1)S(1)}, u32[]{:S(2)}, u32[]{:S(2)}) collective-permute-start(bf16[96,128,128]{2,1,0:T(8,128)(2,1)} %get-tuple-element.46), channel_id=1, source_target_pairs={{0,16},{8,24},{16,0},{24,8},{1,17},{9,25},{17,1},{25,9},{2,18},{10... | collective-permute-start | bytes 9437192 | tf_op jit(solution)/shard_map/ppermute | solution.py:453
  26.2 1.3 bitcast_convert_fusion.1.flags_ref
  27.5 6.2 %unpack_b.8 = (bf16[8192,1280]{1,0:T(8,128)(2,1)}, s32[1]{0:T(128)}) custom-call(s32[1]{0:T(128)} %bitcast.7.shard_ref, s32[16,16]{1,0:T(8,128)} %bitcast_convert_fusion.1.flags_ref, bf16[145,128,128]{2,1,0:T(8,128)(2,1)} %get-tuple-element.48.refs_0_, s32[1]{0:T(128)} %bitcast.turn_ref.refs_1_), custom_call_target="tpu_custom_call" | custom-call | flops 1 | bytes 1 | tf_op jit(solution)/shard_map/unpack_b/pallas_call | solution.py:248
  33.6 6.4 %unpack_b.9 = (bf16[8192,768]{1,0:T(8,128)(2,1)}, s32[1]{0:T(128)}) custom-call(s32[1]{0:T(128)} %bitcast.7.shard_ref, s32[16,16]{1,0:T(8,128)} %bitcast_convert_fusion.1.flags_ref, bf16[145,128,128]{2,1,0:T(8,128)(2,1)} %get-tuple-element.48.refs_0_, s32[1]{0:T(128)} %get-tuple-element.49.refs_1_), custom_call_target="tpu_custom_call" | custom-call | flops 1 | bytes 1 | tf_op jit(solution)/shard_map/unpack_b/pallas_call | solution.py:248
  40.0 1.3 fusion.15.flags_ref
  41.3 6.8 %unpack_b.10 = (bf16[8192,1280]{1,0:T(8,128)(2,1)}, s32[1]{0:T(128)}) custom-call(s32[1]{0:T(128)} %bitcast.4.shard_ref, s32[16,16]{1,0:T(8,128)} %fusion.15.flags_ref, bf16[145,128,128]{2,1,0:T(8,128)(2,1)} %collective-permute-done.10.refs_0_, s32[1]{0:T(128)} %get-tuple-element.50.refs_1_, ...), custom_call_target="tpu_custom_call", output_to_operand_aliasing={{0}: (4, {})} | custom-call | flops 1 | bytes 1 | tf_op jit(solution)/shard_map/unpack_b/pallas_call | solution.py:248
  48.1 6.4 %unpack_b.11 = (bf16[8192,768]{1,0:T(8,128)(2,1)}, s32[1]{0:T(128)}) custom-call(s32[1]{0:T(128)} %bitcast.4.shard_ref, s32[16,16]{1,0:T(8,128)} %fusion.15.flags_ref, bf16[145,128,128]{2,1,0:T(8,128)(2,1)} %collective-permute-done.10.refs_0_, s32[1]{0:T(128)} %get-tuple-element.52.refs_1_, ...), custom_call_target="tpu_custom_call", output_to_operand_aliasing={{0}: (4, {})} | custom-call | flops 1 | bytes 1 | tf_op jit(solution)/shard_map/unpack_b/pallas_call | solution.py:248
  54.5 40.5 %collective-permute-done.9.refs_0_ = bf16[96,128,128]{2,1,0:T(8,128)(2,1)S(1)} collective-permute-done((bf16[96,128,128]{2,1,0:T(8,128)(2,1)}, bf16[96,128,128]{2,1,0:T(8,128)(2,1)S(1)}, u32[]{:S(2)}, u32[]{:S(2)}) %collective-permute-start.9) | collective-permute-done | bytes 3145760 | tf_op jit(solution)/shard_map/ppermute | solution.py:453
  95.0 1.7 copy-done.1
  97.3 1.8 collective-permute-start.12
  99.2 1.3 bitcast_convert_fusion.flags_ref
  100.4 6.2 %unpack_b.12 = (bf16[8192,1280]{1,0:T(8,128)(2,1)}, s32[1]{0:T(128)}) custom-call(s32[1]{0:T(128)} %bitcast.12.shard_ref, s32[16,16]{1,0:T(8,128)} %bitcast_convert_fusion.flags_ref, bf16[96,128,128]{2,1,0:T(8,128)(2,1)} %get-tuple-element.55.refs_0_, s32[1]{0:T(128)} %get-tuple-element.54.refs_2_.refs_1_, ...), custom_call_target="tpu_custom_call", output_to_operand_aliasing={{0}: (4, {})} | custom-call | flops 1 | bytes 1 | tf_op jit(solution)/shard_map/unpack_b/pallas_call | solution.py:248
  108.3 6.4 %unpack_b.13 = (bf16[8192,1280]{1,0:T(8,128)(2,1)}, s32[1]{0:T(128)}) custom-call(s32[1]{0:T(128)} %bitcast.3.shard_ref, s32[16,16]{1,0:T(8,128)} %fusion.14.flags_ref, bf16[96,128,128]{2,1,0:T(8,128)(2,1)} %copy-done.3, s32[1]{0:T(128)} %get-tuple-element.58.refs_1_, bf16[8192,1280]{1,0:T(8,128)(2,1)} %get-tuple-element.59.refs_2_), custom_call_target="tpu_custom_call", output_to_operand_aliasing={{0}: (4, {})} | custom-call | flops 1 | bytes 1 | tf_op jit(solution)/shard_map/unpack_b/pallas_call | solution.py:248
  114.8 6.1 %all-gather.7.cloned.1.call-done = bf16[172,128,128]{2,1,0:T(8,128)(2,1)} async-done(((bf16[43,128,128]{2,1,0:T(8,128)(2,1)}), bf16[172,128,128]{2,1,0:T(8,128)(2,1)}) %all-gather.7.cloned.1.call-update) | async-done | bytes 5636112 | tf_op jit(solution)/shard_map/all_gather | solution.py:443
  121.9 1.3 slice_convert_fusion
  123.8 19.4 %multiply.4.refs_1_ = s16[528,1280]{1,0:T(8,128)(2,1)} custom-call(s32[4,128]{1,0:T(4,128)} %bitcast.62, bf16[4,43,128,128]{3,2,1,0:T(8,128)(2,1)} %bitcast.51, bf16[4,1,2048,1280]{3,2,1,0:T(8,128)(2,1)} %bitcast.43, s32[1]{0:T(128)} %get-tuple-element.61.refs_2_, f32[8,128]{1,0:T(8,128)} %broadcast_in_dim.14.refs_3_), custom_call_target="tpu_custom_call" | custom-call | flops 1 | bytes 1 | tf_op jit(solution)/shard_map/multiply/pallas_call | solution.py:392
  143.3 1.5 collective-permute-start.15
  145.0 1.7 collective-permute-done.7
  146.8 1.5 collective-permute-start.8
  148.3 6.3 %unpack_b.14 = (bf16[8192,768]{1,0:T(8,128)(2,1)}, s32[1]{0:T(128)}) custom-call(s32[1]{0:T(128)} %bitcast.12.shard_ref, s32[16,16]{1,0:T(8,128)} %bitcast_convert_fusion.flags_ref, bf16[96,128,128]{2,1,0:T(8,128)(2,1)} %get-tuple-element.55.refs_0_, bf16[49,128,128]{2,1,0:T(8,128)(2,1)} %after.3.refs_1_, ...), custom_call_target="tpu_custom_call", output_to_operand_aliasing={{0}: (5, {})} | custom-call | flops 1 | bytes 1 | tf_op jit(solution)/shard_map/unpack_b/pallas_call | solution.py:248
  155.3 1.2 copy-done.5
  156.4 6.5 %unpack_b.15 = (bf16[8192,768]{1,0:T(8,128)(2,1)}, s32[1]{0:T(128)}) custom-call(s32[1]{0:T(128)} %bitcast.3.shard_ref, s32[16,16]{1,0:T(8,128)} %fusion.14.flags_ref, bf16[96,128,128]{2,1,0:T(8,128)(2,1)} %copy-done.3, bf16[49,128,128]{2,1,0:T(8,128)(2,1)} %copy-done.5, s32[1]{0:T(128)} %get-tuple-element.63.refs_2_, ...), custom_call_target="tpu_custom_call", output_to_operand_aliasing={{0}: (5, {})} | custom-call | flops 1 | bytes 1 | tf_op jit(solution)/shard_map/unpack_b/pallas_call | solution.py:248
  162.9 14.5 %multiply.5.refs_4_ = s16[528,768]{1,0:T(8,128)(2,1)} custom-call(s32[4,128]{1,0:T(4,128)} %bitcast.63, bf16[4,43,128,128]{3,2,1,0:T(8,128)(2,1)} %bitcast.52, bf16[4,1,2048,768]{3,2,1,0:T(8,128)(2,1)} %bitcast.46, s32[1]{0:T(128)} %get-tuple-element.66.refs_2_, f32[8,128]{1,0:T(8,128)} %fusion.20.refs_3_.refs_5_.refs_8_), custom_call_target="tpu_custom_call" | custom-call | flops 1 | bytes 1 | tf_op jit(solution)/shard_map/multiply/pallas_call | solution.py:392
  177.4 1.6 collective-permute-start.14
  179.0 1.2 slice.34
  180.1 8.5 %all-gather.9.cloned.1.call-done = bf16[104,128,128]{2,1,0:T(8,128)(2,1)} async-done(((bf16[26,128,128]{2,1,0:T(8,128)(2,1)}), bf16[104,128,128]{2,1,0:T(8,128)(2,1)}) %all-gather.9.cloned.1.call-update) | async-done | bytes 3407888 | tf_op jit(solution)/shard_map/all_gather | solution.py:443
  188.7 22.4 %multiply.6.refs_7_ = f32[512,2048]{1,0:T(8,128)} custom-call(s32[4,128]{1,0:T(4,128)} %bitcast.64, bf16[4,43,128,128]{3,2,1,0:T(8,128)(2,1)} %bitcast.53, bf16[4,26,128,128]{3,2,1,0:T(8,128)(2,1)} %bitcast.59, bf16[4,4,512,1280]{3,2,1,0:T(8,128)(2,1)} %bitcast.44, bf16[4,4,512,768]{3,2,1,0:T(8,128)(2,1)} %bitcast.47, s16[528,768]{1,0:T(8,128)(2,1)} %multiply.5.refs_4_, ...), custom_call_target="tpu_custom_call" | custom-call | flops 1 | bytes 1 | tf_op jit(solution)/shard_map/multiply/pallas_call | solution.py:392
  213.1 3.7 %all-gather.11.cloned.1.call-done = bf16[32,128,128]{2,1,0:T(8,128)(2,1)} async-done(((bf16[8,128,128]{2,1,0:T(8,128)(2,1)}), bf16[32,128,128]{2,1,0:T(8,128)(2,1)}) %all-gather.11.cloned.1.call-update) | async-done | bytes 1048592 | tf_op jit(solution)/shard_map/all_gather | solution.py:443
  217.9 12.9 %multiply.7 = f32[512,2048]{1,0:T(8,128)S(1)} custom-call(s32[4,128]{1,0:T(4,128)} %bitcast.65, bf16[4,43,128,128]{3,2,1,0:T(8,128)(2,1)} %bitcast.54, bf16[4,26,128,128]{3,2,1,0:T(8,128)(2,1)} %bitcast.60, bf16[4,8,128,128]{3,2,1,0:T(8,128)(2,1)} %bitcast.61, bf16[4,4,512,1280]{3,2,1,0:T(8,128)(2,1)} %bitcast.45, bf16[4,4,512,768]{3,2,1,0:T(8,128)(2,1)} %bitcast.48, ...), custom_call_target="tpu_custom_call" | custom-call | flops 1 | bytes 1 | tf_op jit(solution)/shard_map/multiply/pallas_call | solution.py:392
  231.1 2.0 copy-done.4
  (44 shorter events, 8.1 us)
Async XLA Ops:
  6.5 7.0 %copy-start.8 = (s32[16,16]{1,0:T(8,128)S(1)}, s32[16,16]{1,0:T(8,128)}, u32[]{:S(2)}) copy-start(s32[16,16]{1,0:T(8,128)} %other_ref.3) | copy-start | bytes 3076
  6.5 114.4 %all-gather.7.cloned.1.call-start = ((), (), s32[]{:S(2)}) async-start(), calls=%async_computation | async-start | bytes 7045120 | tf_op jit(solution)/shard_map/all_gather | solution.py:443
  13.5 175.2 %all-gather.9.cloned.1.call-start = ((), (), s32[]{:S(2)}) async-start(), calls=%async_computation.1 | async-start | bytes 4259840 | tf_op jit(solution)/shard_map/all_gather | solution.py:443
  23.0 17.1 %collective-permute-start.10 = (bf16[145,128,128]{2,1,0:T(8,128)(2,1)}, bf16[145,128,128]{2,1,0:T(8,128)(2,1)}, u32[]{:S(2)}, u32[]{:S(2)}) collective-permute-start(bf16[145,128,128]{2,1,0:T(8,128)(2,1)} %get-tuple-element.48.refs_0_), channel_id=1, source_target_pairs={{0,8},{8,0},{16,24},{24,16},{1,9},{9,1},{17,25},{25,17},{2,10},{10... | collective-permute-start | bytes 14254088 | tf_op jit(solution)/shard_map/ppermute | solution.py:469
  23.4 71.7 %collective-permute-start.9 = (bf16[96,128,128]{2,1,0:T(8,128)(2,1)}, bf16[96,128,128]{2,1,0:T(8,128)(2,1)S(1)}, u32[]{:S(2)}, u32[]{:S(2)}) collective-permute-start(bf16[96,128,128]{2,1,0:T(8,128)(2,1)} %get-tuple-element.46), channel_id=1, source_target_pairs={{0,16},{8,24},{16,0},{24,8},{1,17},{9,25},{17,1},{25,9},{2,18},{10... | collective-permute-start | bytes 9437192 | tf_op jit(solution)/shard_map/ppermute | solution.py:453
  26.1 190.7 %all-gather.11.cloned.1.call-start = ((), (), s32[]{:S(2)}) async-start(), calls=%async_computation.2 | async-start | bytes 1310720 | tf_op jit(solution)/shard_map/all_gather | solution.py:443
  95.0 1.7 copy-start.1
  97.3 9.4 %collective-permute-start.11 = (bf16[96,128,128]{2,1,0:T(8,128)(2,1)}, bf16[96,128,128]{2,1,0:T(8,128)(2,1)S(1)}, u32[]{:S(2)}, u32[]{:S(2)}) collective-permute-start(bf16[96,128,128]{2,1,0:T(8,128)(2,1)} %get-tuple-element.55.refs_0_), channel_id=1, source_target_pairs={{0,8},{8,0},{16,24},{24,16},{1,9},{9,1},{17,25},{25,17},{2,10},{10... | collective-permute-start | bytes 9437192 | tf_op jit(solution)/shard_map/ppermute | solution.py:476
  97.3 45.8 %collective-permute-start.12 = (bf16[49,128,128]{2,1,0:T(8,128)(2,1)}, bf16[49,128,128]{2,1,0:T(8,128)(2,1)}, u32[]{:S(2)}, u32[]{:S(2)}) collective-permute-start(bf16[49,128,128]{2,1,0:T(8,128)(2,1)} %get-tuple-element.56), channel_id=1, source_target_pairs={{0,16},{8,24},{16,0},{24,8},{1,17},{9,25},{17,1},{25,9},{2,18},{10... | collective-permute-start | bytes 4816904 | tf_op jit(solution)/shard_map/ppermute | solution.py:453
  106.7 1.7 copy-start.3
  123.8 21.0 %copy-start.10 = (f32[8,128]{1,0:T(8,128)S(1)}, f32[8,128]{1,0:T(8,128)}, u32[]{:S(2)}) copy-start(f32[8,128]{1,0:T(8,128)} %broadcast_in_dim.14.refs_3_) | copy-start | bytes 12292
  143.2 12.1 %collective-permute-start.13 = (bf16[49,128,128]{2,1,0:T(8,128)(2,1)}, bf16[49,128,128]{2,1,0:T(8,128)(2,1)S(1)}, u32[]{:S(2)}, u32[]{:S(2)}) collective-permute-start(bf16[49,128,128]{2,1,0:T(8,128)(2,1)} %after.3.refs_1_), channel_id=1, source_target_pairs={{0,8},{8,0},{16,24},{24,16},{1,9},{9,1},{17,25},{25,17},{2,10},{10... | collective-permute-start | bytes 4816904 | tf_op jit(solution)/shard_map/ppermute | solution.py:503
  143.3 73.5 %collective-permute-start.15 = (s16[528,1280]{1,0:T(8,128)(2,1)}, s16[528,1280]{1,0:T(8,128)(2,1)S(1)}, u32[]{:S(2)}, u32[]{:S(2)}) collective-permute-start(s16[528,1280]{1,0:T(8,128)(2,1)} %multiply.4.refs_1_), channel_id=1, source_target_pairs={{0,1},{1,0},{2,3},{3,2},{4,5},{5,4},{6,7},{7,6},{8,9},{9,8},{10,11... | collective-permute-start | bytes 4055048 | tf_op jit(solution)/shard_map/ppermute | solution.py:494
  144.8 1.9 collective-permute-start.7
  146.8 7.8 %collective-permute-start.8 = (f32[8,128]{1,0:T(8,128)S(1)}, f32[8,128]{1,0:T(8,128)S(1)}, u32[]{:S(2)}, u32[]{:S(2)}) collective-permute-start(f32[8,128]{1,0:T(8,128)S(1)} %broadcast_maximum_fusion), channel_id=1, source_target_pairs={{0,16},{8,24},{16,0},{24,8},{1,17},{9,25},{17,1},{25,9},{2,18},{10... | collective-permute-start | bytes 12296 | tf_op jit(solution)/shard_map/ppermute | solution.py:415
  155.3 1.2 copy-start.5
  177.4 33.7 %collective-permute-start.14 = (s16[528,768]{1,0:T(8,128)(2,1)}, s16[528,768]{1,0:T(8,128)(2,1)S(1)}, u32[]{:S(2)}, u32[]{:S(2)}) collective-permute-start(s16[528,768]{1,0:T(8,128)(2,1)} %multiply.5.refs_4_), channel_id=1, source_target_pairs={{0,1},{1,0},{2,3},{3,2},{4,5},{5,4},{6,7},{7,6},{8,9},{9,8},{10,11... | collective-permute-start | bytes 2433032 | tf_op jit(solution)/shard_map/ppermute | solution.py:494
  211.1 5.7 %copy-start.7 = (s16[528,768]{1,0:T(8,128)(2,1)}, s16[528,768]{1,0:T(8,128)(2,1)S(1)}, u32[]{:S(2)}) copy-start(s16[528,768]{1,0:T(8,128)(2,1)S(1)} %collective-permute-done.14.refs_6_) | copy-start | bytes 2433028
  216.8 1.1 copy-start.6
  217.9 12.9 %copy-start.9 = (s32[8,16]{1,0:T(8,128)S(1)}, s32[8,16]{1,0:T(8,128)}, u32[]{:S(2)}) copy-start(s32[8,16]{1,0:T(8,128)} %flags_ref.2) | copy-start | bytes 1540
  231.1 2.0 copy-start.4
Sparse Core Ops, SparseCore 0:
  13.6 107.2 all-gather.6
  122.5 66.1 all-gather.8
  190.2 26.5 all-gather.10

commit v5 on v4

--- a/solution.py
+++ b/solution.py
@@ -10,7 +10,7 @@
 from jax.sharding import PartitionSpec as P
 
 BLOCK = 128
-VMEM_LIMIT = 56 * 1024 * 1024
+VMEM_LIMIT = 63 * 1024 * 1024
 TILE_ROOM = 256 * 16
 SMALL = pl.CostEstimate(flops=1, bytes_accessed=1, transcendentals=0)
 LARGE = pl.CostEstimate(flops=10**12, bytes_accessed=1, transcendentals=0)
@@ -44,6 +44,7 @@
         at = (lax.axis_index("row") - hop + rows) % rows * part.shape[0]
         beside = lax.dynamic_slice_in_dim(a_slab, at, part.shape[0], 1)
         partial_value += jnp.dot(beside, part, preferred_element_type=jnp.float32)
+        partial_value, b_kept = lax.optimization_barrier((partial_value, b_kept))
     me, length = lax.axis_index("layer"), partial_value.shape[0] // layers
     total = lax.dynamic_slice_in_dim(partial_value, me * length, length)
     for hop in range(1, layers):
@@ -242,9 +243,9 @@
     pltpu.make_async_copy(written, written, sem).wait()
 
 
-def unpack_b(parts, flags, shard, shards, first, stop, k_blocks, cuts, into, token):
+def unpack_b(parts, flags, shard, shards, first, stop, k_blocks, cuts, into, tokens):
     n = len(parts)
-    operands = [*parts, token] + ([] if into is None else [into])
+    operands = [*parts, *tokens] + ([] if into is None else [into])
     return pl.pallas_call(
         functools.partial(unpack_b_kernel, k_blocks, first, stop, cuts),
         grid_spec=pltpu.PrefetchScalarGridSpec(
@@ -262,15 +263,15 @@
             jax.ShapeDtypeStruct((shards * k_blocks * BLOCK, (stop - first) * BLOCK), parts[0].dtype),
             jax.ShapeDtypeStruct((1,), jnp.int32),
         ],
-        input_output_aliases={} if into is None else {3 + n: 0},
+        input_output_aliases={} if into is None else {2 + n + len(tokens): 0},
         compiler_params=pltpu.CompilerParams(vmem_limit_bytes=VMEM_LIMIT),
         cost_estimate=SMALL,
         name="unpack_b",
     )(shard, flags, *operands)
 
 
-def multiply_kernel(plan, notes_ref, *refs):
-    stages, k_blocks, cuts, shards, halves, given, carried, tokens, pieces, starts, ends = plan
+def multiply_kernel(plan, notes_ref, hop_ref, *refs):
+    stages, k_blocks, cuts, shards, halves, given, carried, tokens, pieces, remarks, starts, ends = plan
     stage, g = stages[-1], len(stages) - 1
     rows, wide = stage.rows, stage.wide
     n = len(cuts) - 1
@@ -284,15 +285,15 @@
         dense[...] = jnp.zeros_like(dense)
         started = jnp.int32(0)
         for s in range(shards):
-            base = s * wide - stage.first
-
-            for part, lo, hi in zip(parts, cuts[:-1], cuts[1:]):
+            base, hop = s * wide - stage.first, hop_ref[s]
+
+            for part, at, lo, hi in zip(parts, [hop] + [s] * (n - 1), cuts[:-1], cuts[1:]):
 
                 def put(slot, _):
-                    code = notes_ref[s, slot]
+                    code = notes_ref[hop, slot]
                     row, k = lax.div(code, k_blocks), lax.rem(code, k_blocks)
                     pltpu.make_async_copy(
-                        part.at[s, slot - lo],
+                        part.at[at, slot - lo],
                         dense.at[
                             pl.ds(pl.multiple_of((row - stage.row) * BLOCK, BLOCK), BLOCK),
                             pl.ds(pl.multiple_of((base + k) * BLOCK, BLOCK), BLOCK),
@@ -301,8 +302,8 @@
                     ).start()
                     return 0
 
-                first = jnp.maximum(notes_ref[s, MARKS + g], lo)
-                stop = jnp.maximum(jnp.minimum(notes_ref[s, MARKS + g + 1], hi), first)
+                first = jnp.maximum(notes_ref[hop, MARKS + g], lo)
+                stop = jnp.maximum(jnp.minimum(notes_ref[hop, MARKS + g + 1], hi), first)
                 lax.fori_loop(first, stop, put, 0)
                 started += stop - first
 
@@ -317,7 +318,7 @@
     def code(value):
         share = rows // pieces
         for q in range(pieces):
-            base = q * (share * BLOCK + 16)
+            base = q * (share * BLOCK + remarks)
             powers = []
             for r in range(share):
                 some = value[(q * share + r) * BLOCK : (q * share + r + 1) * BLOCK]
@@ -327,8 +328,8 @@
                 out_ref[base + r * BLOCK : base + (r + 1) * BLOCK] = some.astype(jnp.int32).astype(jnp.int16)
                 powers.append(power)
             flag = jnp.broadcast_to(over_ref[0:1, 0:1], powers[0].shape)
-            notes = jnp.concatenate(powers + [flag] * (16 - share), axis=0)
-            out_ref[base + share * BLOCK : base + share * BLOCK + 16] = notes.astype(jnp.int32).astype(jnp.int16)
+            notes = jnp.concatenate(powers + [flag] * (remarks - share), axis=0)
+            out_ref[base + share * BLOCK : base + share * BLOCK + remarks] = notes.astype(jnp.int32).astype(jnp.int16)
 
     def finish(value, h):
         for r in range(rows):
@@ -355,7 +356,7 @@
 
 
 def multiply(
-    parts, notes, stages, k_blocks, cuts, b_halves, over, pieces=0, received=(), before=(), tokens=()
+    parts, notes, hops, stages, k_blocks, cuts, b_halves, over, pieces=0, remarks=16, received=(), before=(), tokens=()
 ):
     shards, halves = parts[0].shape[0], len(b_halves)
     stage = stages[-1]
@@ -381,18 +382,18 @@
         operands.append(b_half.reshape(shards, k_blocks // deep, deep * BLOCK, widths[h]))
     for pairs in received:
         for h, codes in enumerate(pairs):
-            in_specs.append(pl.BlockSpec((tall + 16, tile), at(h, 0)))
+            in_specs.append(pl.BlockSpec((codes.shape[0], tile), at(h, 0)))
             operands.append(codes)
     in_specs += [pl.BlockSpec((tall, tile), lambda j, *_: (0, j))] * len(before)
     operands += [*before]
     in_specs += [whole] * len(tokens) + [pl.BlockSpec(memory_space=pltpu.VMEM)]
     operands += [*tokens, over]
-    high = tall + 16 * pieces
-    plan = (stages, k_blocks, cuts, shards, halves, len(received), len(before), len(tokens), pieces, starts, ends)
+    high = tall + remarks * pieces
+    plan = (stages, k_blocks, cuts, shards, halves, len(received), len(before), len(tokens), pieces, remarks, starts, ends)
     return pl.pallas_call(
         functools.partial(multiply_kernel, plan),
         grid_spec=pltpu.PrefetchScalarGridSpec(
-            num_scalar_prefetch=1,
+            num_scalar_prefetch=2,
             grid=(ends[-1],),
             in_specs=in_specs,
             out_specs=pl.BlockSpec((high, tile), lambda j, *_: (0, j)),
@@ -406,15 +407,7 @@
         compiler_params=pltpu.CompilerParams(vmem_limit_bytes=VMEM_LIMIT),
         cost_estimate=SMALL,
         name="multiply",
-    )(notes, *operands)
-
-
-def largest_over(value, axis, size):
-    step = 1
-    while step < size:
-        value = jnp.maximum(value, lax.ppermute(value, axis, [(i, i ^ step) for i in range(size)]))
-        step *= 2
-    return value
+    )(notes, hops, *operands)
 
 
 def per_device(sizes, a_tiles, a_occupancy, b_tiles, b_occupancy):
@@ -435,13 +428,25 @@
 
     early = a_k * 3 // 4
     a_stages = [Stage(0, given, 0, a_k), Stage(given, piece, 0, early), Stage(given, piece, early, a_k - early)]
-    half = b_columns * 5 // 8
+    half = b_columns // 2
     b_stages = [Stage(0, half, 0, b_k), Stage(half, b_columns - half, 0, b_k)]
-    a_cuts, b_cuts = cuts_for(a_stages, 1.77), cuts_for(b_stages, 2.0)
-
-    a_parts, _ = pack(a_tiles, a_occupancy, turn, a_place, a_stages, a_cuts, a_cuts, b_occupancy, (b_place, b_stages, b_cuts))
-    a_parts = [lax.all_gather(part, "col", axis=0) for part in a_parts]
+    a_ends, b_cuts = cuts_for(a_stages, 1.77), cuts_for(b_stages, 2.0)
+    a_cuts = sorted({0, max(a_ends[1] // 14, 1), *a_ends})
+    a_counts = [a_cuts.index(end) for end in a_ends[1:]]
+
+    a_parts, _ = pack(a_tiles, a_occupancy, turn, a_place, a_stages, a_ends, a_cuts, b_occupancy, (b_place, b_stages, b_cuts))
+    heads = [a_parts[0]]
+    for hop in range(1, cols):
+        heads.append(lax.ppermute(a_parts[0], "col", [(c, (c + hop) % cols) for c in range(cols)]))
+    a_parts = [lax.all_gather(part, "col", axis=0) for part in a_parts[1:]]
     b_parts, b_whole = pack(b_tiles, b_occupancy, turn, b_place, b_stages, b_cuts, b_cuts, b_occupancy, None)
+    b_first, b_whole = after([b_parts[0], b_whole], heads[1:])
+    a_parts = [jnp.stack(heads), *a_parts]
+
+    notes = a_parts[0][:, 0, 0].astype(jnp.int32)
+    places_of = lax.rem(me_col - jnp.arange(cols, dtype=jnp.int32) + cols, cols)
+    over = jnp.max(a_parts[0][:, 0, :8, MARKS:].astype(jnp.float32), axis=0)[:, OVER - MARKS :]
+    over = jnp.broadcast_to(over, (8, BLOCK))
 
     pair = 2 if rows % 2 == 0 else 1
     swap = [(r, r ^ 1) for r in range(rows)]
@@ -452,25 +457,31 @@
     def across(part, hop):
         return lax.ppermute(part, "row", [(r, (r + pair * hop) % rows) for r in range(rows)])
 
-    def unpack(h, shard, parts, cuts, token):
+    def unpack(h, shard, parts, cuts, *tokens):
         stage = b_stages[h]
         flags = parts[0][0, :b_k, :b_columns].astype(jnp.int32)
         b_dense[h], token = unpack_b(
-            parts, flags, shard.reshape(1), rows, stage.row, stage.row + stage.rows, b_k, cuts, b_dense[h], token
+            parts, flags, shard.reshape(1), rows, stage.row, stage.row + stage.rows, b_k, cuts, b_dense[h], tokens
         )
         return token
 
-    came = [across(b_parts[0], hop) for hop in hops]
+    came = [across(b_first, hop) for hop in hops]
     cut = [0, b_cuts[-1]]
     token = turn
     for h in range(2):
         token = unpack(h, shards[0], [b_whole], cut, token)
     if pair == 2:
         other = lax.ppermute(b_whole, "row", swap)
+        over = jnp.maximum(over, lax.ppermute(over, "row", swap))
         for h in range(2):
-            token = unpack(h, shards[0] ^ 1, [other], cut, token)
-
-    *came, b_second = after([*came, b_parts[1]], [token])
+            token = unpack(h, shards[0] ^ 1, [other], cut, token, *[over] * h)
+
+    step = pair
+    (over,) = after([over], [token])
+    while step < rows:
+        over = jnp.maximum(over, lax.ppermute(over, "row", [(r, r ^ step) for r in range(rows)]))
+        step *= 2
+    *came, b_second = after([*came, b_parts[1]], [token, over])
     sides = [[part] for part in came]
     if pair == 2:
         sides += [[lax.ppermute(part, "row", swap)] for part in came]
@@ -478,23 +489,19 @@
     places = [shards[hop] ^ side for side in range(pair) for hop in hops]
     for place, parts in zip(places, sides):
         token = unpack(0, place, parts, b_cuts[:2], token)
-    notes = a_parts[0][:, 0, 0].astype(jnp.int32)
-    over = jnp.max(a_parts[0][:, 0, :8, MARKS:].astype(jnp.float32), axis=0)[:, OVER - MARKS :]
-    over = jnp.broadcast_to(over, (8, BLOCK))
-
     def product_of(g, halves, over, **more):
-        return multiply(a_parts, notes, a_stages[: g + 1], a_k, a_cuts[: g + 2], halves, over, **more)
-
-    high = piece * BLOCK + 16
+        return multiply(
+            a_parts, notes, places_of, a_stages[: g + 1], a_k, a_cuts[: a_counts[g] + 1], halves, over, **more
+        )
 
     def exchange(codes):
-        out = []
+        out, high = [], codes.shape[0] // (layers - 1)
         for q in range(layers - 1):
             there = [(i, (i + 1 + q) % layers) for i in range(layers)]
             out.append(lax.ppermute(codes[q * high : (q + 1) * high], "layer", there))
         return out
 
-    codes = product_of(0, b_dense[:1], over, pieces=layers - 1, tokens=[token])
+    codes = product_of(0, b_dense[:1], over, pieces=layers - 1, remarks=32, tokens=[token])
 
     came = after(came, [codes])
     first = exchange(codes)
@@ -503,7 +510,6 @@
         more += [lax.ppermute(part, "row", swap) for part in came]
     for place, parts, part in zip(places, sides, more):
         token = unpack(1, place, [*parts, part], b_cuts, token)
-    over = largest_over(over, "row", rows)
     codes = product_of(0, b_dense[1:], over, pieces=layers - 1, tokens=[token])
 
     second = exchange(codes)

time: 242 us -> 232 us (0.959)
  waiting for transfers between devices: 60.6 us -> 51.4 us
  local copies, waits for them, and re-layouts: 10 us -> 3.79 us
  starting transfers between devices: 9.98 us -> 13.4 us
    ppermute x2, waiting for transfers between devices: 40.5 us -> 10.2 us  [across(): lax.ppermute(part, 'row', [(r, (r + pair * hop) % rows) for r in range(ro...]
    ppermute x2 -> x5, waiting for transfers between devices: 1.72 us -> 26.3 us  [the longest x1 26.2 us: per_device(): lax.ppermute(over, 'row', [(r, r ^ step) for r in range(rows)])]
    unnamed x18 -> x14, local copies, waits for them, and re-layouts: 6.91 us -> 0.69 us
    ppermute x2 -> x5, starting transfers between devices: 1.65 us -> 7.83 us  [the longest x3 7.05 us: per_device(): lax.ppermute(a_parts[0], 'col', [(c, (c + hop) % cols) for c in range(col...]
    all_gather x3, waiting for transfers between devices: 18.4 us -> 14.9 us  [per_device(): a_parts = [lax.all_gather(part, 'col', axis=0) for part in a_parts[1:]]]
  transfers between devices with their start and end apart: 12 -> 15, of which waited for: 5 -> 5; matrix products, arithmetic and copies ran while one was open for 4% -> 5% of each run, Pallas kernels for 49% -> 51%
where the time goes in v5:
time: 232 us; the launch traced here: 230 us
  Pallas kernels  137 us (59%)
  waiting for transfers between devices  51.4 us (22%)
  between operations  14.6 us (6%)
  starting transfers between devices  13.4 us (6%)
  other arithmetic  9.39 us (4%)
  local copies, waits for them, and re-layouts  3.79 us (2%)
    pallas_call x4, Pallas kernels, multiply(): pl.pallas_call(functools.partial(multiply_kernel, plan), grid_spec=pltpu....  69.3 us
    pallas_call x8, Pallas kernels, unpack_b(): pl.pallas_call(functools.partial(unpack_b_kernel, k_blocks, first, stop,...  51 us
    ppermute x1, waiting for transfers between devices, per_device(): lax.ppermute(over, 'row', [(r, r ^ step) for r in range(rows)])  26.2 us
    pallas_call x2, Pallas kernels, pack(): pl.pallas_call(functools.partial(pack_kernel, place, stages, ends, cuts,...  15.8 us
    all_gather x3, waiting for transfers between devices, per_device(): a_parts = [lax.all_gather(part, 'col', axis=0) for part in a_parts[1:]]  14.9 us
    ppermute x2, waiting for transfers between devices, across(): lax.ppermute(part, 'row', [(r, (r + pair * hop) % rows) for r in range(ro...  10.2 us
    ppermute x3, starting transfers between devices, per_device(): lax.ppermute(a_parts[0], 'col', [(c, (c + hop) % cols) for c in range(col...  7.05 us
    convert_element_type x4, other arithmetic, unpack(): flags = parts[0][0, :b_k, :b_columns].astype(jnp.int32)  5.07 us
  transfers between devices with their start and end apart: 15, of which 5 were waited for; matrix products, arithmetic and copies ran while one was open for 5% of the time, Pallas kernels for 51%

profile of v5, /device:TPU:0, one launch (start us, length us, event | category | flops | bytes accessed | tf_op | source)
XLA Modules:
  0.0 230.1 jit_solution(12453995137814016265)
XLA Ops:
  6.5 7.0 %pack.2 = (bf16[3,128,128]{2,1,0:T(8,128)(2,1)}, bf16[40,128,128]{2,1,0:T(8,128)(2,1)}, bf16[26,128,128]{2,1,0:T(8,128)(2,1)}, bf16[8,128,128]{2,1,0:T(8,128)(2,1)}, bf16[1,128,128]{2,1,0:T(8,128)(2,1)}) custom-call(s32[1]{0:T(128)} %bitcast.turn_ref.refs_1_, s32[8,16]{1,0:T(8,128)} %flags_ref.2, s32[16,16]{1,0:T(8,128)} %other_ref.3, ...), custom_call_target="tpu_custom_call" | custom-call | flops 1 | bytes 1 | tf_op jit(solution)/shard_map/pack/pallas_call | solution.py:170
  13.6 3.1 %collective-permute-start.7 = (bf16[3,128,128]{2,1,0:T(8,128)(2,1)}, bf16[3,128,128]{2,1,0:T(8,128)(2,1)S(1)}, u32[]{:S(2)}, u32[]{:S(2)}) collective-permute-start(bf16[3,128,128]{2,1,0:T(8,128)(2,1)} %get-tuple-element.55), channel_id=1, source_target_pairs={{0,2},{2,4},{4,6},{6,0},{1,3},{3,5},{5,7},{7,1},{8,10},{10,12},{12... | collective-permute-start | bytes 294920 | tf_op jit(solution)/shard_map/ppermute | solution.py:440
  16.7 2.6 %collective-permute-start.8 = (bf16[3,128,128]{2,1,0:T(8,128)(2,1)}, bf16[3,128,128]{2,1,0:T(8,128)(2,1)S(1)}, u32[]{:S(2)}, u32[]{:S(2)}) collective-permute-start(bf16[3,128,128]{2,1,0:T(8,128)(2,1)} %get-tuple-element.55), channel_id=1, source_target_pairs={{0,4},{2,6},{4,0},{6,2},{1,5},{3,7},{5,1},{7,3},{8,12},{10,14},{12... | collective-permute-start | bytes 294920 | tf_op jit(solution)/shard_map/ppermute | solution.py:440
  19.3 1.3 collective-permute-start.9
  21.3 8.9 %pack.3 = (bf16[80,128,128]{2,1,0:T(8,128)(2,1)}, bf16[65,128,128]{2,1,0:T(8,128)(2,1)}, bf16[145,128,128]{2,1,0:T(8,128)(2,1)}) custom-call(s32[1]{0:T(128)} %bitcast.turn_ref.refs_1_, s32[16,16]{1,0:T(8,128)S(1)} %copy-done.6, s32[16,16]{1,0:T(8,128)S(1)} %copy-done.6, bf16[128,128]{1,0:T(8,128)(2,1)} %pad.4.header_ref, bf16[2048,2048]{1,0:T(8,128)(2,1)} %values_ref.3), custom_call_target="tpu_custom_call" | custom-call | flops 1 | bytes 1 | tf_op jit(solution)/shard_map/pack/pallas_call | solution.py:170
  30.9 1.5 collective-permute-start.13
  34.1 1.3 bitcast_convert_fusion.1.flags_ref
  35.4 5.7 %unpack_b.8 = (bf16[8192,1024]{1,0:T(8,128)(2,1)}, s32[1]{0:T(128)}) custom-call(s32[1]{0:T(128)} %bitcast.8.shard_ref, s32[16,16]{1,0:T(8,128)} %bitcast_convert_fusion.1.flags_ref, bf16[145,128,128]{2,1,0:T(8,128)(2,1)} %get-tuple-element.58.refs_0_, s32[1]{0:T(128)} %bitcast.turn_ref.refs_1_), custom_call_target="tpu_custom_call" | custom-call | flops 1 | bytes 1 | tf_op jit(solution)/shard_map/unpack_b/pallas_call | solution.py:249
  41.1 6.9 %unpack_b.9 = (bf16[8192,1024]{1,0:T(8,128)(2,1)}, s32[1]{0:T(128)}) custom-call(s32[1]{0:T(128)} %bitcast.8.shard_ref, s32[16,16]{1,0:T(8,128)} %bitcast_convert_fusion.1.flags_ref, bf16[145,128,128]{2,1,0:T(8,128)(2,1)} %get-tuple-element.58.refs_0_, s32[1]{0:T(128)} %get-tuple-element.59.refs_1_), custom_call_target="tpu_custom_call" | custom-call | flops 1 | bytes 1 | tf_op jit(solution)/shard_map/unpack_b/pallas_call | solution.py:249
  48.7 1.3 fusion.13.flags_ref
  49.9 6.4 %unpack_b.10 = (bf16[8192,1024]{1,0:T(8,128)(2,1)}, s32[1]{0:T(128)}) custom-call(s32[1]{0:T(128)} %bitcast.5.shard_ref, s32[16,16]{1,0:T(8,128)} %fusion.13.flags_ref, bf16[145,128,128]{2,1,0:T(8,128)(2,1)} %collective-permute-done.11.refs_0_, s32[1]{0:T(128)} %get-tuple-element.60.refs_1_, ...), custom_call_target="tpu_custom_call", output_to_operand_aliasing={{0}: (4, {})} | custom-call | flops 1 | bytes 1 | tf_op jit(solution)/shard_map/unpack_b/pallas_call | solution.py:249
  56.3 6.8 %unpack_b.11 = (bf16[8192,1024]{1,0:T(8,128)(2,1)}, s32[1]{0:T(128)}) custom-call(s32[1]{0:T(128)} %bitcast.5.shard_ref, s32[16,16]{1,0:T(8,128)} %fusion.13.flags_ref, bf16[145,128,128]{2,1,0:T(8,128)(2,1)} %collective-permute-done.11.refs_0_, s32[1]{0:T(128)} %get-tuple-element.62.refs_1_, ...), custom_call_target="tpu_custom_call", output_to_operand_aliasing={{0}: (5, {})} | custom-call | flops 1 | bytes 1 | tf_op jit(solution)/shard_map/unpack_b/pallas_call | solution.py:249
  64.3 26.2 %collective-permute-done.12 = f32[8,128]{1,0:T(8,128)S(1)} collective-permute-done((f32[8,128]{1,0:T(8,128)}, f32[8,128]{1,0:T(8,128)S(1)}, u32[]{:S(2)}, u32[]{:S(2)}) %collective-permute-start.12) | collective-permute-done | bytes 4128 | tf_op jit(solution)/shard_map/ppermute | solution.py:482
  90.5 1.3 max.11.refs_3_.refs_4_.refs_6_.refs_9_
  92.4 1.6 collective-permute-start.15
  95.1 1.3 bitcast_convert_fusion.flags_ref
  96.4 5.6 %unpack_b.12 = (bf16[8192,1024]{1,0:T(8,128)(2,1)}, s32[1]{0:T(128)}) custom-call(s32[1]{0:T(128)} %bitcast.16.shard_ref, s32[16,16]{1,0:T(8,128)} %bitcast_convert_fusion.flags_ref, bf16[80,128,128]{2,1,0:T(8,128)(2,1)} %get-tuple-element.68.refs_0_, s32[1]{0:T(128)} %get-tuple-element.64.refs_1_.refs_2_, ...), custom_call_target="tpu_custom_call", output_to_operand_aliasing={{0}: (4, {})} | custom-call | flops 1 | bytes 1 | tf_op jit(solution)/shard_map/unpack_b/pallas_call | solution.py:249
  102.0 1.3 fusion.12.flags_ref
  103.3 5.9 %unpack_b.13 = (bf16[8192,1024]{1,0:T(8,128)(2,1)}, s32[1]{0:T(128)}) custom-call(s32[1]{0:T(128)} %bitcast.13.shard_ref, s32[16,16]{1,0:T(8,128)} %fusion.12.flags_ref, bf16[80,128,128]{2,1,0:T(8,128)(2,1)} %collective-permute-done.14.refs_0_, s32[1]{0:T(128)} %get-tuple-element.71.refs_1_, ...), custom_call_target="tpu_custom_call", output_to_operand_aliasing={{0}: (4, {})} | custom-call | flops 1 | bytes 1 | tf_op jit(solution)/shard_map/unpack_b/pallas_call | solution.py:249
  109.1 5.3 %all-gather.7.cloned.1.call-done = bf16[160,128,128]{2,1,0:T(8,128)(2,1)} async-done(((bf16[40,128,128]{2,1,0:T(8,128)(2,1)}), bf16[160,128,128]{2,1,0:T(8,128)(2,1)}) %all-gather.7.cloned.1.call-update) | async-done | bytes 5242896 | tf_op jit(solution)/shard_map/all_gather | solution.py:441
  114.4 16.8 %multiply.4.refs_1_ = s16[544,1024]{1,0:T(8,128)(2,1)} custom-call(s32[4,128]{1,0:T(4,128)} %bitcast.66, s32[4]{0:T(128)} %compare_select_fusion.hop_ref, bf16[4,3,128,128]{3,2,1,0:T(8,128)(2,1)} %copy-done.2, bf16[4,40,128,128]{3,2,1,0:T(8,128)(2,1)} %bitcast.53, bf16[4,1,2048,1024]{3,2,1,0:T(8,128)(2,1)} %bitcast.50, s32[1]{0:T(128)} %get-tuple-element.74.refs_3_.refs_2_, ...), custom_call_target="tpu_custom_call" | custom-call | flops 1 | bytes 1 | tf_op jit(solution)/shard_map/multiply/pallas_call | solution.py:393
  131.3 10.2 %collective-permute-done.15.refs_0_ = bf16[65,128,128]{2,1,0:T(8,128)(2,1)} collective-permute-done((bf16[65,128,128]{2,1,0:T(8,128)(2,1)}, bf16[65,128,128]{2,1,0:T(8,128)(2,1)}, u32[]{:S(2)}, u32[]{:S(2)}) %collective-permute-start.15) | collective-permute-done | bytes 2129952 | tf_op jit(solution)/shard_map/ppermute | solution.py:458
  141.5 1.6 collective-permute-start.18
  143.1 6.8 %unpack_b.14 = (bf16[8192,1024]{1,0:T(8,128)(2,1)}, s32[1]{0:T(128)}) custom-call(s32[1]{0:T(128)} %bitcast.16.shard_ref, s32[16,16]{1,0:T(8,128)} %bitcast_convert_fusion.flags_ref, bf16[80,128,128]{2,1,0:T(8,128)(2,1)} %get-tuple-element.68.refs_0_, bf16[65,128,128]{2,1,0:T(8,128)(2,1)} %after.7.refs_1_, ...), custom_call_target="tpu_custom_call", output_to_operand_aliasing={{0}: (5, {})} | custom-call | flops 1 | bytes 1 | tf_op jit(solution)/shard_map/unpack_b/pallas_call | solution.py:249
  149.9 6.9 %unpack_b.15 = (bf16[8192,1024]{1,0:T(8,128)(2,1)}, s32[1]{0:T(128)}) custom-call(s32[1]{0:T(128)} %bitcast.13.shard_ref, s32[16,16]{1,0:T(8,128)} %fusion.12.flags_ref, bf16[80,128,128]{2,1,0:T(8,128)(2,1)} %collective-permute-done.14.refs_0_, bf16[65,128,128]{2,1,0:T(8,128)(2,1)} %collective-permute-done.16.refs_1_, ...), custom_call_target="tpu_custom_call", output_to_operand_aliasing={{0}: (5, {})} | custom-call | flops 1 | bytes 1 | tf_op jit(solution)/shard_map/unpack_b/pallas_call | solution.py:249
  156.8 16.9 %multiply.5.refs_5_ = s16[528,1024]{1,0:T(8,128)(2,1)} custom-call(s32[4,128]{1,0:T(4,128)} %bitcast.67, s32[4]{0:T(128)} %compare_select_fusion.hop_ref, bf16[4,3,128,128]{3,2,1,0:T(8,128)(2,1)} %copy-done.2, bf16[4,40,128,128]{3,2,1,0:T(8,128)(2,1)} %bitcast.54, bf16[4,1,2048,1024]{3,2,1,0:T(8,128)(2,1)} %bitcast.47, s32[1]{0:T(128)} %get-tuple-element.79.refs_3_, ...), custom_call_target="tpu_custom_call" | custom-call | flops 1 | bytes 1 | tf_op jit(solution)/shard_map/multiply/pallas_call | solution.py:393
  174.5 1.2 slice.36
  175.7 6.5 %all-gather.9.cloned.1.call-done = bf16[104,128,128]{2,1,0:T(8,128)(2,1)} async-done(((bf16[26,128,128]{2,1,0:T(8,128)(2,1)}), bf16[104,128,128]{2,1,0:T(8,128)(2,1)}) %all-gather.9.cloned.1.call-update) | async-done | bytes 3407888 | tf_op jit(solution)/shard_map/all_gather | solution.py:441
  182.2 22.7 %multiply.6.refs_8_ = f32[512,2048]{1,0:T(8,128)} custom-call(s32[4,128]{1,0:T(4,128)} %bitcast.68, s32[4]{0:T(128)} %compare_select_fusion.hop_ref, bf16[4,3,128,128]{3,2,1,0:T(8,128)(2,1)} %copy-done.2, bf16[4,40,128,128]{3,2,1,0:T(8,128)(2,1)} %bitcast.55, bf16[4,26,128,128]{3,2,1,0:T(8,128)(2,1)} %bitcast.59, bf16[4,4,512,1024]{3,2,1,0:T(8,128)(2,1)} %bitcast.51, ...), custom_call_target="tpu_custom_call" | custom-call | flops 1 | bytes 1 | tf_op jit(solution)/shard_map/multiply/pallas_call | solution.py:393
  205.0 1.2 slice.45
  207.3 3.0 %all-gather.11.cloned.1.call-done = bf16[32,128,128]{2,1,0:T(8,128)(2,1)} async-done(((bf16[8,128,128]{2,1,0:T(8,128)(2,1)}), bf16[32,128,128]{2,1,0:T(8,128)(2,1)}) %all-gather.11.cloned.1.call-update) | async-done | bytes 1048592 | tf_op jit(solution)/shard_map/all_gather | solution.py:441
  210.4 12.8 %multiply.7 = f32[512,2048]{1,0:T(8,128)} custom-call(s32[4,128]{1,0:T(4,128)} %bitcast.69, s32[4]{0:T(128)} %compare_select_fusion.hop_ref, bf16[4,3,128,128]{3,2,1,0:T(8,128)(2,1)} %copy-done.2, bf16[4,40,128,128]{3,2,1,0:T(8,128)(2,1)} %bitcast.56, bf16[4,26,128,128]{3,2,1,0:T(8,128)(2,1)} %bitcast.60, bf16[4,8,128,128]{3,2,1,0:T(8,128)(2,1)} %bitcast.61, ...), custom_call_target="tpu_custom_call" | custom-call | flops 1 | bytes 1 | tf_op jit(solution)/shard_map/multiply/pallas_call | solution.py:393
  (50 shorter events, 7.5 us)
Async XLA Ops:
  6.5 14.1 %copy-start.6 = (s32[16,16]{1,0:T(8,128)S(1)}, s32[16,16]{1,0:T(8,128)}, u32[]{:S(2)}) copy-start(s32[16,16]{1,0:T(8,128)} %other_ref.3) | copy-start | bytes 3076
  6.5 107.9 %all-gather.7.cloned.1.call-start = ((), (), s32[]{:S(2)}) async-start(), calls=%async_computation | async-start | bytes 6553600 | tf_op jit(solution)/shard_map/all_gather | solution.py:441
  13.5 168.7 %all-gather.9.cloned.1.call-start = ((), (), s32[]{:S(2)}) async-start(), calls=%async_computation.1 | async-start | bytes 4259840 | tf_op jit(solution)/shard_map/all_gather | solution.py:441
  13.6 16.5 %collective-permute-start.7 = (bf16[3,128,128]{2,1,0:T(8,128)(2,1)}, bf16[3,128,128]{2,1,0:T(8,128)(2,1)S(1)}, u32[]{:S(2)}, u32[]{:S(2)}) collective-permute-start(bf16[3,128,128]{2,1,0:T(8,128)(2,1)} %get-tuple-element.55), channel_id=1, source_target_pairs={{0,2},{2,4},{4,6},{6,0},{1,3},{3,5},{5,7},{7,1},{8,10},{10,12},{12... | collective-permute-start | bytes 294920 | tf_op jit(solution)/shard_map/ppermute | solution.py:440
  16.7 13.4 %collective-permute-start.8 = (bf16[3,128,128]{2,1,0:T(8,128)(2,1)}, bf16[3,128,128]{2,1,0:T(8,128)(2,1)S(1)}, u32[]{:S(2)}, u32[]{:S(2)}) collective-permute-start(bf16[3,128,128]{2,1,0:T(8,128)(2,1)} %get-tuple-element.55), channel_id=1, source_target_pairs={{0,4},{2,6},{4,0},{6,2},{1,5},{3,7},{5,1},{7,3},{8,12},{10,14},{12... | collective-permute-start | bytes 294920 | tf_op jit(solution)/shard_map/ppermute | solution.py:440
  19.3 10.9 %collective-permute-start.9 = (bf16[3,128,128]{2,1,0:T(8,128)(2,1)}, bf16[3,128,128]{2,1,0:T(8,128)(2,1)S(1)}, u32[]{:S(2)}, u32[]{:S(2)}) collective-permute-start(bf16[3,128,128]{2,1,0:T(8,128)(2,1)} %get-tuple-element.55), channel_id=1, source_target_pairs={{0,6},{2,0},{4,2},{6,4},{1,7},{3,1},{5,3},{7,5},{8,14},{10,8},{12,... | collective-permute-start | bytes 294920 | tf_op jit(solution)/shard_map/ppermute | solution.py:440
  21.3 11.2 %copy-start.7 = (bf16[3,128,128]{2,1,0:T(8,128)(2,1)S(1)}, bf16[3,128,128]{2,1,0:T(8,128)(2,1)}, u32[]{:S(2)}) copy-start(bf16[3,128,128]{2,1,0:T(8,128)(2,1)} %get-tuple-element.55) | copy-start | bytes 294916
  30.1 0.6 copy-start.3
  30.2 0.7 copy-start.4
  30.2 0.7 copy-start.5
  30.9 17.8 %collective-permute-start.11 = (bf16[145,128,128]{2,1,0:T(8,128)(2,1)}, bf16[145,128,128]{2,1,0:T(8,128)(2,1)}, u32[]{:S(2)}, u32[]{:S(2)}) collective-permute-start(bf16[145,128,128]{2,1,0:T(8,128)(2,1)} %get-tuple-element.58.refs_0_), channel_id=1, source_target_pairs={{0,8},{8,0},{16,24},{24,16},{1,9},{9,1},{17,25},{25,17},{2,10},{10... | collective-permute-start | bytes 14254088 | tf_op jit(solution)/shard_map/ppermute | solution.py:474
  30.9 60.9 %collective-permute-start.13 = (bf16[80,128,128]{2,1,0:T(8,128)(2,1)}, bf16[80,128,128]{2,1,0:T(8,128)(2,1)}, u32[]{:S(2)}, u32[]{:S(2)}) collective-permute-start(bf16[80,128,128]{2,1,0:T(8,128)(2,1)} %get-tuple-element.66), channel_id=1, source_target_pairs={{0,16},{8,24},{16,0},{24,8},{1,17},{9,25},{17,1},{25,9},{2,18},{10... | collective-permute-start | bytes 7864328 | tf_op jit(solution)/shard_map/ppermute | solution.py:458
  32.4 178.0 %all-gather.11.cloned.1.call-start = ((), (), s32[]{:S(2)}) async-start(), calls=%async_computation.2 | async-start | bytes 1310720 | tf_op jit(solution)/shard_map/all_gather | solution.py:441
  33.5 61.0 %copy-start.2 = (bf16[4,3,128,128]{3,2,1,0:T(8,128)(2,1)}, bf16[4,3,128,128]{3,2,1,0:T(8,128)(2,1)S(1)}, u32[]{:S(2)}) copy-start(bf16[4,3,128,128]{3,2,1,0:T(8,128)(2,1)S(1)} %pad_maximum_fusion.refs_0_) | copy-start | bytes 1179652
  33.9 14.1 %collective-permute-start.10 = (f32[8,128]{1,0:T(8,128)S(1)}, f32[8,128]{1,0:T(8,128)S(1)}, u32[]{:S(2)}, u32[]{:S(2)}) collective-permute-start(f32[8,128]{1,0:T(8,128)S(1)} %broadcast_in_dim.14), channel_id=1, source_target_pairs={{0,8},{8,0},{16,24},{24,16},{1,9},{9,1},{17,25},{25,17},{2,10},{10... | collective-permute-start | bytes 12296 | tf_op jit(solution)/shard_map/ppermute | solution.py:475
  63.7 26.8 %collective-permute-start.12 = (f32[8,128]{1,0:T(8,128)}, f32[8,128]{1,0:T(8,128)S(1)}, u32[]{:S(2)}, u32[]{:S(2)}) collective-permute-start(f32[8,128]{1,0:T(8,128)} %after.5), channel_id=1, source_target_pairs={{0,16},{8,24},{16,0},{24,8},{1,17},{9,25},{17,1},{25,9},{2,18},{10... | collective-permute-start | bytes 12296 | tf_op jit(solution)/shard_map/ppermute | solution.py:482
  92.3 9.7 %collective-permute-start.14 = (bf16[80,128,128]{2,1,0:T(8,128)(2,1)}, bf16[80,128,128]{2,1,0:T(8,128)(2,1)}, u32[]{:S(2)}, u32[]{:S(2)}) collective-permute-start(bf16[80,128,128]{2,1,0:T(8,128)(2,1)} %get-tuple-element.68.refs_0_), channel_id=1, source_target_pairs={{0,8},{8,0},{16,24},{24,16},{1,9},{9,1},{17,25},{25,17},{2,10},{10... | collective-permute-start | bytes 7864328 | tf_op jit(solution)/shard_map/ppermute | solution.py:487
  92.4 49.1 %collective-permute-start.15 = (bf16[65,128,128]{2,1,0:T(8,128)(2,1)}, bf16[65,128,128]{2,1,0:T(8,128)(2,1)}, u32[]{:S(2)}, u32[]{:S(2)}) collective-permute-start(bf16[65,128,128]{2,1,0:T(8,128)(2,1)} %get-tuple-element.69), channel_id=1, source_target_pairs={{0,16},{8,24},{16,0},{24,8},{1,17},{9,25},{17,1},{25,9},{2,18},{10... | collective-permute-start | bytes 6389768 | tf_op jit(solution)/shard_map/ppermute | solution.py:458
  141.5 8.5 %collective-permute-start.16 = (bf16[65,128,128]{2,1,0:T(8,128)(2,1)}, bf16[65,128,128]{2,1,0:T(8,128)(2,1)}, u32[]{:S(2)}, u32[]{:S(2)}) collective-permute-start(bf16[65,128,128]{2,1,0:T(8,128)(2,1)} %after.7.refs_1_), channel_id=1, source_target_pairs={{0,8},{8,0},{16,24},{24,16},{1,9},{9,1},{17,25},{25,17},{2,10},{10... | collective-permute-start | bytes 6389768 | tf_op jit(solution)/shard_map/ppermute | solution.py:510
  141.5 68.9 %collective-permute-start.18 = (s16[544,1024]{1,0:T(8,128)(2,1)}, s16[544,1024]{1,0:T(8,128)(2,1)}, u32[]{:S(2)}, u32[]{:S(2)}) collective-permute-start(s16[544,1024]{1,0:T(8,128)(2,1)} %multiply.4.refs_1_), channel_id=1, source_target_pairs={{0,1},{1,0},{2,3},{3,2},{4,5},{5,4},{6,7},{7,6},{8,9},{9,8},{10,11... | collective-permute-start | bytes 3342344 | tf_op jit(solution)/shard_map/ppermute | solution.py:501
  173.8 31.2 %collective-permute-start.17 = (s16[528,1024]{1,0:T(8,128)(2,1)}, s16[528,1024]{1,0:T(8,128)(2,1)}, u32[]{:S(2)}, u32[]{:S(2)}) collective-permute-start(s16[528,1024]{1,0:T(8,128)(2,1)} %multiply.5.refs_5_), channel_id=1, source_target_pairs={{0,1},{1,0},{2,3},{3,2},{4,5},{5,4},{6,7},{7,6},{8,9},{9,8},{10,11... | collective-permute-start | bytes 3244040 | tf_op jit(solution)/shard_map/ppermute | solution.py:501
  210.4 12.8 %copy-start.8 = (s32[8,16]{1,0:T(8,128)S(1)}, s32[8,16]{1,0:T(8,128)}, u32[]{:S(2)}) copy-start(s32[8,16]{1,0:T(8,128)} %flags_ref.2) | copy-start | bytes 1540
Sparse Core Ops, SparseCore 0:
  13.7 100.7 all-gather.6
  116.0 66.1 all-gather.8
  183.8 26.5 all-gather.10

commit v6 on v5

--- a/solution.py
+++ b/solution.py
@@ -84,12 +84,22 @@
 MARKS, OVER = BLOCK - 8, BLOCK - 1
 
 
+def settle(count, most, held, sem):
+    some = 1 << (most.bit_length() - 1)
+    while some:
+
+        @pl.when(lax.rem(lax.div(count, some), 2) == 1)
+        def _(some=some):
+            pltpu.make_async_copy(held.at[pl.ds(0, some)], held.at[pl.ds(0, some)], sem).wait()
+
+        some //= 2
+
+
 def pack_kernel(place, stages, ends, cuts, other, columns, turn_ref, flags_ref, other_ref, header_ref, values_ref, *refs):
     n = len(cuts) - 1
     parts, (whole, held, sem, out_sems) = refs[:n], refs[-4:]
-    header = pltpu.make_async_copy(header_ref.at[:BLOCK, :BLOCK], held.at[0], sem)
     if other is None:
-        header.start()
+        pltpu.make_async_copy(header_ref.at[:BLOCK, :BLOCK], held.at[0], sem).start()
     else:
         held[0] = jnp.zeros_like(held[0])
     lane = lax.broadcasted_iota(jnp.int32, (16, BLOCK), 1)
@@ -122,26 +132,18 @@
     notes = jnp.zeros((16, BLOCK), jnp.float32)
     for stage, cut in zip(stages, ends[1:]):
         marks.append(slot)
-        slot, notes = lax.fori_loop(0, stage.rows * stage.wide, step_of(stage), (slot, notes), unroll=4)
+        slot, notes = lax.fori_loop(0, stage.rows * stage.wide, step_of(stage), (slot, notes), unroll=8)
         over = jnp.maximum(over, jnp.where(slot > cut, 1, 0))
     marks.append(slot)
     if other is not None:
-        other_place, other_stages, other_ends = other
-        spent = jnp.int32(1)
+        other_stages, other_ends = other
+        present = other_ref[...]
+        column = lax.broadcasted_iota(jnp.int32, present.shape, 1)
         for stage, cut in zip(other_stages, other_ends[1:]):
-
-            def count(u, spent):
-                row, column = other_place(stage, u, turn_ref[0])
-                return spent + other_ref[row, column]
-
-            spent = lax.fori_loop(0, stage.rows * stage.wide, count, spent, unroll=16)
+            spent = 1 + jnp.sum(jnp.where(column < stage.row + stage.rows, present, 0))
             over = jnp.maximum(over, jnp.where(spent > cut, 1, 0))
 
-    def settle(t, _):
-        header.wait()
-        return 0
-
-    lax.fori_loop(0, slot if other is None else slot - 1, settle, 0)
+    settle(slot if other is None else slot - 1, sum(stage.rows * stage.wide for stage in stages) + 1, held, sem)
     if other is not None:
         notes = jnp.where(lane >= MARKS, over.astype(jnp.float32), notes)
         for i, mark in enumerate(marks):
@@ -170,12 +172,12 @@
     *parts, whole = pl.pallas_call(
         functools.partial(pack_kernel, place, stages, ends, cuts, other, occupancy.shape[1]),
         grid_spec=pltpu.PrefetchScalarGridSpec(
-            num_scalar_prefetch=3,
+            num_scalar_prefetch=2,
             grid=(),
-            in_specs=[pl.BlockSpec(memory_space=pl.ANY)] * 2,
+            in_specs=[pl.BlockSpec(memory_space=pltpu.VMEM)] + [pl.BlockSpec(memory_space=pl.ANY)] * 2,
             out_specs=[pl.BlockSpec(memory_space=pl.ANY)] * (n + 1),
             scratch_shapes=[
-                pltpu.VMEM((cuts[-1] + 1, BLOCK, BLOCK), values.dtype),
+                pltpu.VMEM((max(cuts[-1], 1 << occupancy.size.bit_length()) + 1, BLOCK, BLOCK), values.dtype),
                 pltpu.SemaphoreType.DMA,
                 pltpu.SemaphoreType.DMA((n + 1,)),
             ],
@@ -271,7 +273,7 @@
 
 
 def multiply_kernel(plan, notes_ref, hop_ref, *refs):
-    stages, k_blocks, cuts, shards, halves, given, carried, tokens, pieces, remarks, starts, ends = plan
+    stages, k_blocks, cuts, shards, halves, given, carried, tokens, pieces, remarks, starts, ends, by_hop = plan
     stage, g = stages[-1], len(stages) - 1
     rows, wide = stage.rows, stage.wide
     n = len(cuts) - 1
@@ -279,7 +281,7 @@
     b_refs, refs = refs[:halves], refs[halves:]
     codes_in, refs = refs[: halves * given], refs[halves * given :]
     before, refs = refs[:carried], refs[carried + tokens :]
-    over_ref, out_ref, dense, sem, total = refs
+    over_ref, out_ref, *word_ref, dense, sem, total = refs
 
     def fill():
         dense[...] = jnp.zeros_like(dense)
@@ -287,7 +289,9 @@
         for s in range(shards):
             base, hop = s * wide - stage.first, hop_ref[s]
 
-            for part, at, lo, hi in zip(parts, [hop] + [s] * (n - 1), cuts[:-1], cuts[1:]):
+            for i, (part, lo, hi) in enumerate(zip(parts, cuts[:-1], cuts[1:])):
+                at = hop if i in by_hop else s
+
 
                 def put(slot, _):
                     code = notes_ref[hop, slot]
@@ -315,48 +319,57 @@
 
     pl.when(pl.program_id(0) == 0)(fill)
 
-    def code(value):
+    def code(here):
         share = rows // pieces
         for q in range(pieces):
             base = q * (share * BLOCK + remarks)
             powers = []
             for r in range(share):
-                some = value[(q * share + r) * BLOCK : (q * share + r + 1) * BLOCK]
+                some = total[(q * share + r) * BLOCK : (q * share + r + 1) * BLOCK, here]
                 top = jnp.max(jnp.abs(some), axis=0, keepdims=True)
                 power = jnp.clip(jnp.ceil(jnp.log2(top)), -60.0, 60.0)
                 some = jnp.clip(jnp.round(some * jnp.exp2(15.0 - power)), -32767.0, 32767.0)
-                out_ref[base + r * BLOCK : base + (r + 1) * BLOCK] = some.astype(jnp.int32).astype(jnp.int16)
+                out_ref[base + r * BLOCK : base + (r + 1) * BLOCK, here] = some.astype(jnp.int32).astype(jnp.int16)
                 powers.append(power)
             flag = jnp.broadcast_to(over_ref[0:1, 0:1], powers[0].shape)
             notes = jnp.concatenate(powers + [flag] * (remarks - share), axis=0)
-            out_ref[base + share * BLOCK : base + share * BLOCK + remarks] = notes.astype(jnp.int32).astype(jnp.int16)
-
-    def finish(value, h):
+            out_ref[base + share * BLOCK : base + share * BLOCK + remarks, here] = notes.astype(jnp.int32).astype(jnp.int16)
+
+    def finish(here, h):
         for r in range(rows):
             span = slice(r * BLOCK, (r + 1) * BLOCK)
-            some = value[span]
+            some = total[span, here]
             for q in range(given):
                 codes = codes_in[q * halves + h]
-                notes = codes[rows * BLOCK : rows * BLOCK + 16].astype(jnp.int32).astype(jnp.float32)
-                some += codes[span].astype(jnp.int32).astype(jnp.float32) * jnp.exp2(notes[r : r + 1] - 15.0)
+                notes = codes[rows * BLOCK : rows * BLOCK + 16, here].astype(jnp.int32).astype(jnp.float32)
+                some += codes[span, here].astype(jnp.int32).astype(jnp.float32) * jnp.exp2(notes[r : r + 1] - 15.0)
             for earlier in before:
-                some += earlier[span]
-            out_ref[span] = some
+                some += earlier[span, here]
+            out_ref[span, here] = some
+        if given and h == halves - 1:
+            over = jnp.max(over_ref[...])
+            for q in range(given):
+                remarks = codes_in[q * halves + h][-16:, :BLOCK].astype(jnp.int32).astype(jnp.float32)
+                over = jnp.maximum(over, jnp.max(remarks[15:]))
+            word_ref[0][0] = over.astype(jnp.int32)
 
     for h, b_ref in enumerate(b_refs):
 
         @pl.when((pl.program_id(0) >= starts[h]) & (pl.program_id(0) < ends[h]))
         def _():
-            b_here = b_ref[...].reshape(-1, b_ref.shape[-1])
-            total[...] = jnp.dot(dense[...], b_here, preferred_element_type=jnp.float32)
-            if pieces:
-                code(total)
-            else:
-                finish(total, h)
+            span = min(b_ref.shape[-1], 256)
+            for at in range(0, b_ref.shape[-1], span):
+                here = slice(at, at + span)
+                b_here = b_ref[..., here].reshape(-1, span)
+                total[:, here] = jnp.dot(dense[...], b_here, preferred_element_type=jnp.float32)
+                if pieces:
+                    code(here)
+                else:
+                    finish(here, h)
 
 
 def multiply(
-    parts, notes, hops, stages, k_blocks, cuts, b_halves, over, pieces=0, remarks=16, received=(), before=(), tokens=()
+    parts, notes, hops, by_hop, stages, k_blocks, cuts, b_halves, over, pieces=0, remarks=16, received=(), before=(), tokens=()
 ):
     shards, halves = parts[0].shape[0], len(b_halves)
     stage = stages[-1]
@@ -389,21 +402,26 @@
     in_specs += [whole] * len(tokens) + [pl.BlockSpec(memory_space=pltpu.VMEM)]
     operands += [*tokens, over]
     high = tall + remarks * pieces
-    plan = (stages, k_blocks, cuts, shards, halves, len(received), len(before), len(tokens), pieces, remarks, starts, ends)
+    out_specs = [pl.BlockSpec((high, tile), lambda j, *_: (0, j))]
+    out_shape = [jax.ShapeDtypeStruct((high, sum(widths)), jnp.int16 if pieces else jnp.float32)]
+    if received:
+        out_specs.append(pl.BlockSpec(memory_space=pltpu.SMEM))
+        out_shape.append(jax.ShapeDtypeStruct((1,), jnp.int32))
+    plan = (stages, k_blocks, cuts, shards, halves, len(received), len(before), len(tokens), pieces, remarks, starts, ends, by_hop)
     return pl.pallas_call(
         functools.partial(multiply_kernel, plan),
         grid_spec=pltpu.PrefetchScalarGridSpec(
             num_scalar_prefetch=2,
             grid=(ends[-1],),
             in_specs=in_specs,
-            out_specs=pl.BlockSpec((high, tile), lambda j, *_: (0, j)),
+            out_specs=out_specs,
             scratch_shapes=[
                 pltpu.VMEM((tall, shards * stage.wide * BLOCK), b_halves[0].dtype),
                 pltpu.SemaphoreType.DMA,
                 pltpu.VMEM((tall, tile), jnp.float32),
             ],
         ),
-        out_shape=jax.ShapeDtypeStruct((high, sum(widths)), jnp.int16 if pieces else jnp.float32),
+        out_shape=out_shape,
         compiler_params=pltpu.CompilerParams(vmem_limit_bytes=VMEM_LIMIT),
         cost_estimate=SMALL,
         name="multiply",
@@ -431,17 +449,20 @@
     half = b_columns // 2
     b_stages = [Stage(0, half, 0, b_k), Stage(half, b_columns - half, 0, b_k)]
     a_ends, b_cuts = cuts_for(a_stages, 1.77), cuts_for(b_stages, 2.0)
-    a_cuts = sorted({0, max(a_ends[1] // 14, 1), *a_ends})
+    a_cuts = sorted({0, max(a_ends[1] // 14, 1), a_ends[1] + max((a_ends[2] - a_ends[1]) // 6, 1), *a_ends})
+    assert len(a_cuts) == 6
     a_counts = [a_cuts.index(end) for end in a_ends[1:]]
 
-    a_parts, _ = pack(a_tiles, a_occupancy, turn, a_place, a_stages, a_ends, a_cuts, b_occupancy, (b_place, b_stages, b_cuts))
-    heads = [a_parts[0]]
-    for hop in range(1, cols):
-        heads.append(lax.ppermute(a_parts[0], "col", [(c, (c + hop) % cols) for c in range(cols)]))
-    a_parts = [lax.all_gather(part, "col", axis=0) for part in a_parts[1:]]
+    a_parts, _ = pack(a_tiles, a_occupancy, turn, a_place, a_stages, a_ends, a_cuts, b_occupancy, (b_stages, b_cuts))
+    def round_col(part):
+        return [part] + [lax.ppermute(part, "col", [(c, (c + hop) % cols) for c in range(cols)]) for hop in range(1, cols)]
+
+    heads = round_col(a_parts[0])
+    more_a = a_parts[2]
+    a_parts = [None if i in (0, 2) else lax.all_gather(part, "col", axis=0) for i, part in enumerate(a_parts)]
     b_parts, b_whole = pack(b_tiles, b_occupancy, turn, b_place, b_stages, b_cuts, b_cuts, b_occupancy, None)
     b_first, b_whole = after([b_parts[0], b_whole], heads[1:])
-    a_parts = [jnp.stack(heads), *a_parts]
+    a_parts[0] = jnp.stack(heads)
 
     notes = a_parts[0][:, 0, 0].astype(jnp.int32)
     places_of = lax.rem(me_col - jnp.arange(cols, dtype=jnp.int32) + cols, cols)
@@ -491,7 +512,7 @@
         token = unpack(0, place, parts, b_cuts[:2], token)
     def product_of(g, halves, over, **more):
         return multiply(
-            a_parts, notes, places_of, a_stages[: g + 1], a_k, a_cuts[: a_counts[g] + 1], halves, over, **more
+            a_parts, notes, places_of, (0, 2), a_stages[: g + 1], a_k, a_cuts[: a_counts[g] + 1], halves, over, **more
         )
 
     def exchange(codes):
@@ -501,27 +522,27 @@
             out.append(lax.ppermute(codes[q * high : (q + 1) * high], "layer", there))
         return out
 
-    codes = product_of(0, b_dense[:1], over, pieces=layers - 1, remarks=32, tokens=[token])
-
-    came = after(came, [codes])
+    (more_a,) = after([more_a], [token, a_parts[1]])
+    more_a = round_col(more_a)
+    (codes,) = product_of(0, b_dense[:1], over, pieces=layers - 1, remarks=32, tokens=[token])
+
+    came = after(came, [codes, *more_a[1:]])
+    a_parts[2] = jnp.stack(more_a)
     first = exchange(codes)
     more = [*came]
     if pair == 2:
         more += [lax.ppermute(part, "row", swap) for part in came]
     for place, parts, part in zip(places, sides, more):
         token = unpack(1, place, [*parts, part], b_cuts, token)
-    codes = product_of(0, b_dense[1:], over, pieces=layers - 1, tokens=[token])
+    (codes,) = product_of(0, b_dense[1:], over, pieces=layers - 1, tokens=[token])
 
     second = exchange(codes)
-    product = product_of(1, b_dense, over, tokens=[codes])
+    (product,) = product_of(1, b_dense, over, tokens=[codes])
 
     received = [*zip(first, second)]
-    product = product_of(2, b_dense, over, received=received, before=(product,))
-    over = over[0, 0]
-    for codes in second:
-        over = jnp.maximum(over, codes[-1, 0].astype(jnp.float32))
+    product, over = product_of(2, b_dense, over, received=received, before=(product,))
     return lax.cond(
-        over > 0,
+        over[0] > 0,
         lambda: whole_slab(sizes, a_tiles, a_occupancy, b_tiles, b_occupancy),
         lambda: product,
     )

time: 232 us -> 226 us (0.974)
  waiting for transfers between devices: 51.4 us -> 42.3 us
  starting transfers between devices: 13.4 us -> 17.1 us
    ppermute x2, waiting for transfers between devices: 10.2 us -> 4.32 us  [across(): lax.ppermute(part, 'row', [(r, (r + pair * hop) % rows) for r in range(ro...]
    ppermute x3 -> x6, starting transfers between devices: 7.05 us -> 11 us  [round_col(): lax.ppermute(part, 'col', [(c, (c + hop) % cols) for c in range(cols)])]
    all_gather x3, waiting for transfers between devices: 14.9 us -> 11.7 us  [per_device(): lax.all_gather(part, 'col', axis=0)]
    slice x2 -> x0, local copies, waits for them, and re-layouts: 2.41 us -> none  [the longest x1 1.25 us: per_device(): over = over[0, 0]]
  transfers between devices with their start and end apart: 15 -> 18, of which waited for: 5 -> 5; matrix products, arithmetic and copies ran while one was open for 5% -> 5% of each run, Pallas kernels for 51% -> 53%
where the time goes in v6:
time: 226 us; the launch traced here: 224 us
  Pallas kernels  137 us (61%)
  waiting for transfers between devices  42.3 us (19%)
  starting transfers between devices  17.1 us (8%)
  between operations  14.1 us (6%)
  other arithmetic  10.3 us (5%)
  local copies, waits for them, and re-layouts  2.75 us (1%)
    pallas_call x4, Pallas kernels, multiply(): pl.pallas_call(functools.partial(multiply_kernel, plan), grid_spec=pltpu....  70 us
    pallas_call x8, Pallas kernels, unpack_b(): pl.pallas_call(functools.partial(unpack_b_kernel, k_blocks, first, stop,...  51.1 us
    ppermute x1, waiting for transfers between devices, per_device(): lax.ppermute(over, 'row', [(r, r ^ step) for r in range(rows)])  26.2 us
    pallas_call x2, Pallas kernels, pack(): pl.pallas_call(functools.partial(pack_kernel, place, stages, ends, cuts,...  14.2 us
    all_gather x3, waiting for transfers between devices, per_device(): lax.all_gather(part, 'col', axis=0)  11.7 us
    ppermute x6, starting transfers between devices, round_col(): lax.ppermute(part, 'col', [(c, (c + hop) % cols) for c in range(cols)])  11 us
    convert_element_type x4, other arithmetic, unpack(): flags = parts[0][0, :b_k, :b_columns].astype(jnp.int32)  5.09 us
  transfers between devices with their start and end apart: 18, of which 5 were waited for; matrix products, arithmetic and copies ran while one was open for 5% of the time, Pallas kernels for 53%

profile of v6, /device:TPU:0, one launch (start us, length us, event | category | flops | bytes accessed | tf_op | source)
XLA Modules:
  0.0 224.0 jit_solution(3712725297444984226)
XLA Ops:
  6.5 5.8 %pack.2 = (bf16[3,128,128]{2,1,0:T(8,128)(2,1)}, bf16[40,128,128]{2,1,0:T(8,128)(2,1)}, bf16[4,128,128]{2,1,0:T(8,128)(2,1)}, bf16[22,128,128]{2,1,0:T(8,128)(2,...) custom-call(s32[1]{0:T(128)} %bitcast.turn_ref.refs_1_, s32[8,16]{1,0:T(8,128)} %flags_ref.2, ...), custom_call_target="tpu_custom_call" | custom-call | flops 1 | bytes 1 | tf_op jit(solution)/shard_map/pack/pallas_call | solution.py:172
  12.5 3.2 %collective-permute-start.7 = (bf16[3,128,128]{2,1,0:T(8,128)(2,1)}, bf16[3,128,128]{2,1,0:T(8,128)(2,1)S(1)}, u32[]{:S(2)}, u32[]{:S(2)}) collective-permute-start(bf16[3,128,128]{2,1,0:T(8,128)(2,1)} %get-tuple-element.58), channel_id=1, source_target_pairs={{0,2},{2,4},{4,6},{6,0},{1,3},{3,5},{5,7},{7,1},{8,10},{10,12},{12... | collective-permute-start | bytes 294920 | tf_op jit(solution)/shard_map/ppermute | solution.py:458
  15.6 2.6 %collective-permute-start.8 = (bf16[3,128,128]{2,1,0:T(8,128)(2,1)}, bf16[3,128,128]{2,1,0:T(8,128)(2,1)S(1)}, u32[]{:S(2)}, u32[]{:S(2)}) collective-permute-start(bf16[3,128,128]{2,1,0:T(8,128)(2,1)} %get-tuple-element.58), channel_id=1, source_target_pairs={{0,4},{2,6},{4,0},{6,2},{1,5},{3,7},{5,1},{7,3},{8,12},{10,14},{12... | collective-permute-start | bytes 294920 | tf_op jit(solution)/shard_map/ppermute | solution.py:458
  18.2 1.3 collective-permute-start.9
  20.2 8.3 %pack.3 = (bf16[80,128,128]{2,1,0:T(8,128)(2,1)}, bf16[65,128,128]{2,1,0:T(8,128)(2,1)}, bf16[145,128,128]{2,1,0:T(8,128)(2,1)}) custom-call(s32[1]{0:T(128)} %bitcast.turn_ref.refs_1_, s32[16,16]{1,0:T(8,128)S(1)} %copy-done.13, s32[16,16]{1,0:T(8,128)S(1)} %copy-done.13, bf16[128,128]{1,0:T(8,128)(2,1)} %pad.4.header_ref, bf16[2048,2048]{1,0:T(8,128)(2,1)} %values_ref.3), custom_call_target="tpu_custom_call" | custom-call | flops 1 | bytes 1 | tf_op jit(solution)/shard_map/pack/pallas_call | solution.py:172
  29.3 1.6 collective-permute-start.10
  30.8 1.0 pad_maximum_fusion.1.refs_0_
  32.4 1.3 bitcast_convert_fusion.1.flags_ref
  33.7 5.7 %unpack_b.8 = (bf16[8192,1024]{1,0:T(8,128)(2,1)}, s32[1]{0:T(128)}) custom-call(s32[1]{0:T(128)} %bitcast.11.shard_ref, s32[16,16]{1,0:T(8,128)} %bitcast_convert_fusion.1.flags_ref, bf16[145,128,128]{2,1,0:T(8,128)(2,1)} %get-tuple-element.65.refs_0_, s32[1]{0:T(128)} %bitcast.turn_ref.refs_1_), custom_call_target="tpu_custom_call" | custom-call | flops 1 | bytes 1 | tf_op jit(solution)/shard_map/unpack_b/pallas_call | solution.py:251
  39.4 6.9 %unpack_b.9 = (bf16[8192,1024]{1,0:T(8,128)(2,1)}, s32[1]{0:T(128)}) custom-call(s32[1]{0:T(128)} %bitcast.11.shard_ref, s32[16,16]{1,0:T(8,128)} %bitcast_convert_fusion.1.flags_ref, bf16[145,128,128]{2,1,0:T(8,128)(2,1)} %get-tuple-element.65.refs_0_, s32[1]{0:T(128)} %get-tuple-element.66.refs_1_), custom_call_target="tpu_custom_call" | custom-call | flops 1 | bytes 1 | tf_op jit(solution)/shard_map/unpack_b/pallas_call | solution.py:251
  47.0 1.3 fusion.13.flags_ref
  48.3 6.4 %unpack_b.10 = (bf16[8192,1024]{1,0:T(8,128)(2,1)}, s32[1]{0:T(128)}) custom-call(s32[1]{0:T(128)} %bitcast.8.shard_ref, s32[16,16]{1,0:T(8,128)} %fusion.13.flags_ref, bf16[145,128,128]{2,1,0:T(8,128)(2,1)} %collective-permute-done.11.refs_0_, s32[1]{0:T(128)} %get-tuple-element.67.refs_1_, ...), custom_call_target="tpu_custom_call", output_to_operand_aliasing={{0}: (4, {})} | custom-call | flops 1 | bytes 1 | tf_op jit(solution)/shard_map/unpack_b/pallas_call | solution.py:251
  54.7 6.8 %unpack_b.11 = (bf16[8192,1024]{1,0:T(8,128)(2,1)}, s32[1]{0:T(128)}) custom-call(s32[1]{0:T(128)} %bitcast.8.shard_ref, s32[16,16]{1,0:T(8,128)} %fusion.13.flags_ref, bf16[145,128,128]{2,1,0:T(8,128)(2,1)} %collective-permute-done.11.refs_0_, s32[1]{0:T(128)} %get-tuple-element.69.refs_1_, ...), custom_call_target="tpu_custom_call", output_to_operand_aliasing={{0}: (5, {})} | custom-call | flops 1 | bytes 1 | tf_op jit(solution)/shard_map/unpack_b/pallas_call | solution.py:251
  62.7 26.2 %collective-permute-done.13 = f32[8,128]{1,0:T(8,128)S(1)} collective-permute-done((f32[8,128]{1,0:T(8,128)}, f32[8,128]{1,0:T(8,128)S(1)}, u32[]{:S(2)}, u32[]{:S(2)}) %collective-permute-start.13) | collective-permute-done | bytes 4128 | tf_op jit(solution)/shard_map/ppermute | solution.py:503
  88.9 1.3 max.7.refs_3_.refs_4_.refs_7_.refs_10_
  91.0 1.6 collective-permute-start.18
  93.1 1.3 bitcast_convert_fusion.flags_ref
  94.4 5.8 %unpack_b.12 = (bf16[8192,1024]{1,0:T(8,128)(2,1)}, s32[1]{0:T(128)}) custom-call(s32[1]{0:T(128)} %bitcast.15.shard_ref, s32[16,16]{1,0:T(8,128)} %bitcast_convert_fusion.flags_ref, bf16[80,128,128]{2,1,0:T(8,128)(2,1)} %get-tuple-element.72.refs_0_, s32[1]{0:T(128)} %get-tuple-element.71.refs_1_.refs_2_, ...), custom_call_target="tpu_custom_call", output_to_operand_aliasing={{0}: (4, {})} | custom-call | flops 1 | bytes 1 | tf_op jit(solution)/shard_map/unpack_b/pallas_call | solution.py:251
  100.2 1.3 fusion.12.flags_ref
  101.5 5.8 %unpack_b.13 = (bf16[8192,1024]{1,0:T(8,128)(2,1)}, s32[1]{0:T(128)}) custom-call(s32[1]{0:T(128)} %bitcast.7.shard_ref, s32[16,16]{1,0:T(8,128)} %fusion.12.flags_ref, bf16[80,128,128]{2,1,0:T(8,128)(2,1)} %collective-permute-done.14.refs_0_, s32[1]{0:T(128)} %get-tuple-element.74.refs_1_, ...), custom_call_target="tpu_custom_call", output_to_operand_aliasing={{0}: (4, {})} | custom-call | flops 1 | bytes 1 | tf_op jit(solution)/shard_map/unpack_b/pallas_call | solution.py:251
  107.3 6.1 %all-gather.7.cloned.1.call-done = bf16[160,128,128]{2,1,0:T(8,128)(2,1)} async-done(((bf16[40,128,128]{2,1,0:T(8,128)(2,1)}), bf16[160,128,128]{2,1,0:T(8,128)(2,1)}) %all-gather.7.cloned.1.call-update) | async-done | bytes 5242896 | tf_op jit(solution)/shard_map/all_gather | solution.py:462
  114.0 1.0 collective-permute-start.16
  115.0 2.8 %collective-permute-start.17 = (bf16[4,128,128]{2,1,0:T(8,128)(2,1)}, bf16[4,128,128]{2,1,0:T(8,128)(2,1)S(1)}, u32[]{:S(2)}, u32[]{:S(2)}) collective-permute-start(bf16[4,128,128]{2,1,0:T(8,128)(2,1)} %after.8), channel_id=1, source_target_pairs={{0,6},{2,0},{4,2},{6,4},{1,7},{3,1},{5,3},{7,5},{8,14},{10,8},{12,... | collective-permute-start | bytes 393224 | tf_op jit(solution)/shard_map/ppermute | solution.py:458
  118.4 17.3 %multiply.4.refs_1_ = s16[544,1024]{1,0:T(8,128)(2,1)} custom-call(s32[4,128]{1,0:T(4,128)} %bitcast.75, s32[4]{0:T(128)} %compare_select_fusion.hop_ref, bf16[4,3,128,128]{3,2,1,0:T(8,128)(2,1)} %copy-done.2, bf16[4,40,128,128]{3,2,1,0:T(8,128)(2,1)} %bitcast.58, bf16[4,1,2048,1024]{3,2,1,0:T(8,128)(2,1)} %bitcast.54, ...), custom_call_target="tpu_custom_call" | custom-call | flops 1 | bytes 1 | tf_op jit(solution)/shard_map/multiply/pallas_call | solution.py:411
  135.8 4.3 %collective-permute-done.18.refs_0_ = bf16[65,128,128]{2,1,0:T(8,128)(2,1)} collective-permute-done((bf16[65,128,128]{2,1,0:T(8,128)(2,1)}, bf16[65,128,128]{2,1,0:T(8,128)(2,1)}, u32[]{:S(2)}, u32[]{:S(2)}) %collective-permute-start.18) | collective-permute-done | bytes 2129952 | tf_op jit(solution)/shard_map/ppermute | solution.py:479
  141.5 1.6 collective-permute-start.20
  143.1 6.9 %unpack_b.14 = (bf16[8192,1024]{1,0:T(8,128)(2,1)}, s32[1]{0:T(128)}) custom-call(s32[1]{0:T(128)} %bitcast.15.shard_ref, s32[16,16]{1,0:T(8,128)} %bitcast_convert_fusion.flags_ref, bf16[80,128,128]{2,1,0:T(8,128)(2,1)} %get-tuple-element.72.refs_0_, bf16[65,128,128]{2,1,0:T(8,128)(2,1)} %after.9.refs_1_, ...), custom_call_target="tpu_custom_call", output_to_operand_aliasing={{0}: (5, {})} | custom-call | flops 1 | bytes 1 | tf_op jit(solution)/shard_map/unpack_b/pallas_call | solution.py:251
  149.9 6.9 %unpack_b.15 = (bf16[8192,1024]{1,0:T(8,128)(2,1)}, s32[1]{0:T(128)}) custom-call(s32[1]{0:T(128)} %bitcast.7.shard_ref, s32[16,16]{1,0:T(8,128)} %fusion.12.flags_ref, bf16[80,128,128]{2,1,0:T(8,128)(2,1)} %collective-permute-done.14.refs_0_, bf16[65,128,128]{2,1,0:T(8,128)(2,1)} %collective-permute-done.19.refs_1_, ...), custom_call_target="tpu_custom_call", output_to_operand_aliasing={{0}: (5, {})} | custom-call | flops 1 | bytes 1 | tf_op jit(solution)/shard_map/unpack_b/pallas_call | solution.py:251
  156.9 17.2 %multiply.5.refs_6_ = s16[528,1024]{1,0:T(8,128)(2,1)} custom-call(s32[4,128]{1,0:T(4,128)} %bitcast.76, s32[4]{0:T(128)} %compare_select_fusion.hop_ref, bf16[4,3,128,128]{3,2,1,0:T(8,128)(2,1)} %copy-done.2, bf16[4,40,128,128]{3,2,1,0:T(8,128)(2,1)} %bitcast.59, bf16[4,1,2048,1024]{3,2,1,0:T(8,128)(2,1)} %bitcast.51, s32[1]{0:T(128)} %get-tuple-element.85.refs_3_, ...), custom_call_target="tpu_custom_call" | custom-call | flops 1 | bytes 1 | tf_op jit(solution)/shard_map/multiply/pallas_call | solution.py:411
  176.0 22.8 %multiply.6.refs_9_ = f32[512,2048]{1,0:T(8,128)} custom-call(s32[4,128]{1,0:T(4,128)} %bitcast.77, s32[4]{0:T(128)} %compare_select_fusion.hop_ref, bf16[4,3,128,128]{3,2,1,0:T(8,128)(2,1)} %copy-done.2, bf16[4,40,128,128]{3,2,1,0:T(8,128)(2,1)} %bitcast.60, bf16[4,4,128,128]{3,2,1,0:T(8,128)(2,1)} %pad_maximum_fusion.refs_2_, ...), custom_call_target="tpu_custom_call" | custom-call | flops 1 | bytes 1 | tf_op jit(solution)/shard_map/multiply/pallas_call | solution.py:411
  198.8 5.0 %all-gather.11.cloned.1.call-done = bf16[32,128,128]{2,1,0:T(8,128)(2,1)} async-done(((bf16[8,128,128]{2,1,0:T(8,128)(2,1)}), bf16[32,128,128]{2,1,0:T(8,128)(2,1)}) %all-gather.11.cloned.1.call-update) | async-done | bytes 1048592 | tf_op jit(solution)/shard_map/all_gather | solution.py:462
  203.9 12.6 %multiply.7 = (f32[512,2048]{1,0:T(8,128)}, s32[1]{0:T(128)}) custom-call(s32[4,128]{1,0:T(4,128)} %bitcast.78, s32[4]{0:T(128)} %compare_select_fusion.hop_ref, bf16[4,3,128,128]{3,2,1,0:T(8,128)(2,1)} %copy-done.2, bf16[4,40,128,128]{3,2,1,0:T(8,128)(2,1)} %bitcast.61, bf16[4,4,128,128]{3,2,1,0:T(8,128)(2,1)} %pad_maximum_fusion.refs_2_, ...), custom_call_target="tpu_custom_call" | custom-call | flops 1 | bytes 1 | tf_op jit(solution)/shard_map/multiply/pallas_call | solution.py:411
  (70 shorter events, 9.9 us)
Async XLA Ops:
  6.5 13.0 %copy-start.13 = (s32[16,16]{1,0:T(8,128)S(1)}, s32[16,16]{1,0:T(8,128)}, u32[]{:S(2)}) copy-start(s32[16,16]{1,0:T(8,128)} %other_ref.3) | copy-start | bytes 3076
  6.5 106.8 %all-gather.7.cloned.1.call-start = ((), (), s32[]{:S(2)}) async-start(), calls=%async_computation | async-start | bytes 6553600 | tf_op jit(solution)/shard_map/all_gather | solution.py:462
  12.4 18.4 %copy-start.14 = (bf16[3,128,128]{2,1,0:T(8,128)(2,1)S(1)}, bf16[3,128,128]{2,1,0:T(8,128)(2,1)}, u32[]{:S(2)}) copy-start(bf16[3,128,128]{2,1,0:T(8,128)(2,1)} %get-tuple-element.58) | copy-start | bytes 294916
  12.4 163.6 %all-gather.9.cloned.1.call-start = ((), (), s32[]{:S(2)}) async-start(), calls=%async_computation.1 | async-start | bytes 3604480 | tf_op jit(solution)/shard_map/all_gather | solution.py:462
  12.5 16.1 %collective-permute-start.7 = (bf16[3,128,128]{2,1,0:T(8,128)(2,1)}, bf16[3,128,128]{2,1,0:T(8,128)(2,1)S(1)}, u32[]{:S(2)}, u32[]{:S(2)}) collective-permute-start(bf16[3,128,128]{2,1,0:T(8,128)(2,1)} %get-tuple-element.58), channel_id=1, source_target_pairs={{0,2},{2,4},{4,6},{6,0},{1,3},{3,5},{5,7},{7,1},{8,10},{10,12},{12... | collective-permute-start | bytes 294920 | tf_op jit(solution)/shard_map/ppermute | solution.py:458
  15.6 12.9 %collective-permute-start.8 = (bf16[3,128,128]{2,1,0:T(8,128)(2,1)}, bf16[3,128,128]{2,1,0:T(8,128)(2,1)S(1)}, u32[]{:S(2)}, u32[]{:S(2)}) collective-permute-start(bf16[3,128,128]{2,1,0:T(8,128)(2,1)} %get-tuple-element.58), channel_id=1, source_target_pairs={{0,4},{2,6},{4,0},{6,2},{1,5},{3,7},{5,1},{7,3},{8,12},{10,14},{12... | collective-permute-start | bytes 294920 | tf_op jit(solution)/shard_map/ppermute | solution.py:458
  18.2 10.4 %collective-permute-start.9 = (bf16[3,128,128]{2,1,0:T(8,128)(2,1)}, bf16[3,128,128]{2,1,0:T(8,128)(2,1)S(1)}, u32[]{:S(2)}, u32[]{:S(2)}) collective-permute-start(bf16[3,128,128]{2,1,0:T(8,128)(2,1)} %get-tuple-element.58), channel_id=1, source_target_pairs={{0,6},{2,0},{4,2},{6,4},{1,7},{3,1},{5,3},{7,5},{8,14},{10,8},{12,... | collective-permute-start | bytes 294920 | tf_op jit(solution)/shard_map/ppermute | solution.py:458
  28.6 0.6 copy-start.10
  28.6 0.7 copy-start.11
  28.6 0.7 copy-start.12
  29.3 17.7 %collective-permute-start.11 = (bf16[145,128,128]{2,1,0:T(8,128)(2,1)}, bf16[145,128,128]{2,1,0:T(8,128)(2,1)}, u32[]{:S(2)}, u32[]{:S(2)}) collective-permute-start(bf16[145,128,128]{2,1,0:T(8,128)(2,1)} %get-tuple-element.65.refs_0_), channel_id=1, source_target_pairs={{0,8},{8,0},{16,24},{24,16},{1,9},{9,1},{17,25},{25,17},{2,10},{10... | collective-permute-start | bytes 14254088 | tf_op jit(solution)/shard_map/ppermute | solution.py:495
  29.3 60.9 %collective-permute-start.10 = (bf16[80,128,128]{2,1,0:T(8,128)(2,1)}, bf16[80,128,128]{2,1,0:T(8,128)(2,1)}, u32[]{:S(2)}, u32[]{:S(2)}) collective-permute-start(bf16[80,128,128]{2,1,0:T(8,128)(2,1)} %get-tuple-element.63), channel_id=1, source_target_pairs={{0,16},{8,24},{16,0},{24,8},{1,17},{9,25},{17,1},{25,9},{2,18},{10... | collective-permute-start | bytes 7864328 | tf_op jit(solution)/shard_map/ppermute | solution.py:479
  31.9 86.0 %copy-start.2 = (bf16[4,3,128,128]{3,2,1,0:T(8,128)(2,1)}, bf16[4,3,128,128]{3,2,1,0:T(8,128)(2,1)S(1)}, u32[]{:S(2)}) copy-start(bf16[4,3,128,128]{3,2,1,0:T(8,128)(2,1)S(1)} %pad_maximum_fusion.1.refs_0_) | copy-start | bytes 1179652
  32.2 14.1 %collective-permute-start.12 = (f32[8,128]{1,0:T(8,128)S(1)}, f32[8,128]{1,0:T(8,128)S(1)}, u32[]{:S(2)}, u32[]{:S(2)}) collective-permute-start(f32[8,128]{1,0:T(8,128)S(1)} %broadcast_in_dim.14), channel_id=1, source_target_pairs={{0,8},{8,0},{16,24},{24,16},{1,9},{9,1},{17,25},{25,17},{2,10},{10... | collective-permute-start | bytes 12296 | tf_op jit(solution)/shard_map/ppermute | solution.py:496
  62.1 26.8 %collective-permute-start.13 = (f32[8,128]{1,0:T(8,128)}, f32[8,128]{1,0:T(8,128)S(1)}, u32[]{:S(2)}, u32[]{:S(2)}) collective-permute-start(f32[8,128]{1,0:T(8,128)} %after.6), channel_id=1, source_target_pairs={{0,16},{8,24},{16,0},{24,8},{1,17},{9,25},{17,1},{25,9},{2,18},{10... | collective-permute-start | bytes 12296 | tf_op jit(solution)/shard_map/ppermute | solution.py:503
  90.8 9.3 %collective-permute-start.14 = (bf16[80,128,128]{2,1,0:T(8,128)(2,1)}, bf16[80,128,128]{2,1,0:T(8,128)(2,1)}, u32[]{:S(2)}, u32[]{:S(2)}) collective-permute-start(bf16[80,128,128]{2,1,0:T(8,128)(2,1)} %get-tuple-element.72.refs_0_), channel_id=1, source_target_pairs={{0,8},{8,0},{16,24},{24,16},{1,9},{9,1},{17,25},{25,17},{2,10},{10... | collective-permute-start | bytes 7864328 | tf_op jit(solution)/shard_map/ppermute | solution.py:508
  90.9 112.9 %all-gather.11.cloned.1.call-start = ((), (), s32[]{:S(2)}) async-start(), calls=%async_computation.2 | async-start | bytes 1310720 | tf_op jit(solution)/shard_map/all_gather | solution.py:462
  91.0 49.1 %collective-permute-start.18 = (bf16[65,128,128]{2,1,0:T(8,128)(2,1)}, bf16[65,128,128]{2,1,0:T(8,128)(2,1)}, u32[]{:S(2)}, u32[]{:S(2)}) collective-permute-start(bf16[65,128,128]{2,1,0:T(8,128)(2,1)} %get-tuple-element.80), channel_id=1, source_target_pairs={{0,16},{8,24},{16,0},{24,8},{1,17},{9,25},{17,1},{25,9},{2,18},{10... | collective-permute-start | bytes 6389768 | tf_op jit(solution)/shard_map/ppermute | solution.py:479
  114.0 26.1 %collective-permute-start.15 = (bf16[4,128,128]{2,1,0:T(8,128)(2,1)}, bf16[4,128,128]{2,1,0:T(8,128)(2,1)S(1)}, u32[]{:S(2)}, u32[]{:S(2)}) collective-permute-start(bf16[4,128,128]{2,1,0:T(8,128)(2,1)} %after.8), channel_id=1, source_target_pairs={{0,2},{2,4},{4,6},{6,0},{1,3},{3,5},{5,7},{7,1},{8,10},{10,12},{12... | collective-permute-start | bytes 393224 | tf_op jit(solution)/shard_map/ppermute | solution.py:458
  114.0 26.1 %collective-permute-start.16 = (bf16[4,128,128]{2,1,0:T(8,128)(2,1)}, bf16[4,128,128]{2,1,0:T(8,128)(2,1)S(1)}, u32[]{:S(2)}, u32[]{:S(2)}) collective-permute-start(bf16[4,128,128]{2,1,0:T(8,128)(2,1)} %after.8), channel_id=1, source_target_pairs={{0,4},{2,6},{4,0},{6,2},{1,5},{3,7},{5,1},{7,3},{8,12},{10,14},{12... | collective-permute-start | bytes 393224 | tf_op jit(solution)/shard_map/ppermute | solution.py:458
  115.0 25.1 %collective-permute-start.17 = (bf16[4,128,128]{2,1,0:T(8,128)(2,1)}, bf16[4,128,128]{2,1,0:T(8,128)(2,1)S(1)}, u32[]{:S(2)}, u32[]{:S(2)}) collective-permute-start(bf16[4,128,128]{2,1,0:T(8,128)(2,1)} %after.8), channel_id=1, source_target_pairs={{0,6},{2,0},{4,2},{6,4},{1,7},{3,1},{5,3},{7,5},{8,14},{10,8},{12,... | collective-permute-start | bytes 393224 | tf_op jit(solution)/shard_map/ppermute | solution.py:458
  140.1 0.6 copy-start.4
  140.1 0.7 copy-start.6
  140.8 0.7 copy-start.8
  141.5 8.5 %collective-permute-start.19 = (bf16[65,128,128]{2,1,0:T(8,128)(2,1)}, bf16[65,128,128]{2,1,0:T(8,128)(2,1)}, u32[]{:S(2)}, u32[]{:S(2)}) collective-permute-start(bf16[65,128,128]{2,1,0:T(8,128)(2,1)} %after.9.refs_1_), channel_id=1, source_target_pairs={{0,8},{8,0},{16,24},{24,16},{1,9},{9,1},{17,25},{25,17},{2,10},{10... | collective-permute-start | bytes 6389768 | tf_op jit(solution)/shard_map/ppermute | solution.py:534
  141.5 62.4 %collective-permute-start.20 = (s16[544,1024]{1,0:T(8,128)(2,1)}, s16[544,1024]{1,0:T(8,128)(2,1)}, u32[]{:S(2)}, u32[]{:S(2)}) collective-permute-start(s16[544,1024]{1,0:T(8,128)(2,1)} %multiply.4.refs_1_), channel_id=1, source_target_pairs={{0,1},{1,0},{2,3},{3,2},{4,5},{5,4},{6,7},{7,6},{8,9},{9,8},{10,11... | collective-permute-start | bytes 3342344 | tf_op jit(solution)/shard_map/ppermute | solution.py:522
  156.8 17.7 %copy-start.3 = (bf16[4,128,128]{2,1,0:T(8,128)(2,1)S(1)}, bf16[4,128,128]{2,1,0:T(8,128)(2,1)}, u32[]{:S(2)}) copy-start(bf16[4,128,128]{2,1,0:T(8,128)(2,1)} %after.8) | copy-start | bytes 393220
  156.9 17.7 %copy-start.5 = (bf16[4,128,128]{2,1,0:T(8,128)(2,1)S(1)}, bf16[4,128,128]{2,1,0:T(8,128)(2,1)}, u32[]{:S(2)}) copy-start(bf16[4,128,128]{2,1,0:T(8,128)(2,1)} %copy-done.4) | copy-start | bytes 393220
  156.9 17.7 %copy-start.7 = (bf16[4,128,128]{2,1,0:T(8,128)(2,1)S(1)}, bf16[4,128,128]{2,1,0:T(8,128)(2,1)}, u32[]{:S(2)}) copy-start(bf16[4,128,128]{2,1,0:T(8,128)(2,1)} %copy-done.6) | copy-start | bytes 393220
  156.9 17.7 %copy-start.9 = (bf16[4,128,128]{2,1,0:T(8,128)(2,1)S(1)}, bf16[4,128,128]{2,1,0:T(8,128)(2,1)}, u32[]{:S(2)}) copy-start(bf16[4,128,128]{2,1,0:T(8,128)(2,1)} %copy-done.8) | copy-start | bytes 393220
  174.1 29.8 %collective-permute-start.21 = (s16[528,1024]{1,0:T(8,128)(2,1)}, s16[528,1024]{1,0:T(8,128)(2,1)}, u32[]{:S(2)}, u32[]{:S(2)}) collective-permute-start(s16[528,1024]{1,0:T(8,128)(2,1)} %multiply.5.refs_6_), channel_id=1, source_target_pairs={{0,1},{1,0},{2,3},{3,2},{4,5},{5,4},{6,7},{7,6},{8,9},{9,8},{10,11... | collective-permute-start | bytes 3244040 | tf_op jit(solution)/shard_map/ppermute | solution.py:522
  203.9 13.3 %copy-start.15 = (s32[8,16]{1,0:T(8,128)S(1)}, s32[8,16]{1,0:T(8,128)}, u32[]{:S(2)}) copy-start(s32[8,16]{1,0:T(8,128)} %flags_ref.2) | copy-start | bytes 1540
Sparse Core Ops, SparseCore 0:
  12.5 100.8 all-gather.6
  114.9 61.0 all-gather.8
  177.6 26.2 all-gather.10

commit v7 on v6

--- a/solution.py
+++ b/solution.py
@@ -311,11 +311,16 @@
                 lax.fori_loop(first, stop, put, 0)
                 started += stop - first
 
-        def settle(t, _):
-            pltpu.make_async_copy(parts[0].at[0, 0], dense.at[:BLOCK, :BLOCK], sem).wait()
-            return 0
-
-        lax.fori_loop(0, started, settle, 0)
+        some = 1 << ((rows * wide * shards).bit_length() - 1)
+        while some:
+            broad = min(some, 1 << ((wide * shards).bit_length() - 1))
+            here = dense.at[: some // broad * BLOCK, : broad * BLOCK]
+
+            @pl.when(lax.rem(lax.div(started, some), 2) == 1)
+            def _(here=here):
+                pltpu.make_async_copy(here, here, sem).wait()
+
+            some //= 2
 
     pl.when(pl.program_id(0) == 0)(fill)
 

time: 226 us -> 226 us (level)
  no operation moved by 1% of the time
where the time goes in v7:
time: 226 us; the launch traced here: 224 us
  Pallas kernels  137 us (61%)
  waiting for transfers between devices  42.9 us (19%)
  starting transfers between devices  17 us (8%)
  between operations  14.1 us (6%)
  other arithmetic  10.3 us (5%)
  local copies, waits for them, and re-layouts  2.75 us (1%)
    pallas_call x4, Pallas kernels, multiply(): pl.pallas_call(functools.partial(multiply_kernel, plan), grid_spec=pltpu....  69.5 us
    pallas_call x8, Pallas kernels, unpack_b(): pl.pallas_call(functools.partial(unpack_b_kernel, k_blocks, first, stop,...  51.1 us
    ppermute x1, waiting for transfers between devices, per_device(): lax.ppermute(over, 'row', [(r, r ^ step) for r in range(rows)])  26.2 us
    pallas_call x2, Pallas kernels, pack(): pl.pallas_call(functools.partial(pack_kernel, place, stages, ends, cuts,...  14.3 us
    all_gather x3, waiting for transfers between devices, per_device(): lax.all_gather(part, 'col', axis=0)  12.2 us
    ppermute x6, starting transfers between devices, round_col(): lax.ppermute(part, 'col', [(c, (c + hop) % cols) for c in range(cols)])  10.9 us
    convert_element_type x4, other arithmetic, unpack(): flags = parts[0][0, :b_k, :b_columns].astype(jnp.int32)  5.09 us
  transfers between devices with their start and end apart: 18, of which 5 were waited for; matrix products, arithmetic and copies ran while one was open for 5% of the time, Pallas kernels for 53%

profile of v7, /device:TPU:0, one launch (start us, length us, event | category | flops | bytes accessed | tf_op | source)
XLA Modules:
  0.0 224.1 jit_solution(4768668873459493250)
XLA Ops:
  6.5 5.9 %pack.2 = (bf16[3,128,128]{2,1,0:T(8,128)(2,1)}, bf16[40,128,128]{2,1,0:T(8,128)(2,1)}, bf16[4,128,128]{2,1,0:T(8,128)(2,1)}, bf16[22,128,128]{2,1,0:T(8,128)(2,...) custom-call(s32[1]{0:T(128)} %bitcast.turn_ref.refs_1_, s32[8,16]{1,0:T(8,128)} %flags_ref.2, ...), custom_call_target="tpu_custom_call" | custom-call | flops 1 | bytes 1 | tf_op jit(solution)/shard_map/pack/pallas_call | solution.py:172
  12.5 3.1 %collective-permute-start.7 = (bf16[3,128,128]{2,1,0:T(8,128)(2,1)}, bf16[3,128,128]{2,1,0:T(8,128)(2,1)S(1)}, u32[]{:S(2)}, u32[]{:S(2)}) collective-permute-start(bf16[3,128,128]{2,1,0:T(8,128)(2,1)} %get-tuple-element.58), channel_id=1, source_target_pairs={{0,2},{2,4},{4,6},{6,0},{1,3},{3,5},{5,7},{7,1},{8,10},{10,12},{12... | collective-permute-start | bytes 294920 | tf_op jit(solution)/shard_map/ppermute | solution.py:463
  15.6 2.5 %collective-permute-start.8 = (bf16[3,128,128]{2,1,0:T(8,128)(2,1)}, bf16[3,128,128]{2,1,0:T(8,128)(2,1)S(1)}, u32[]{:S(2)}, u32[]{:S(2)}) collective-permute-start(bf16[3,128,128]{2,1,0:T(8,128)(2,1)} %get-tuple-element.58), channel_id=1, source_target_pairs={{0,4},{2,6},{4,0},{6,2},{1,5},{3,7},{5,1},{7,3},{8,12},{10,14},{12... | collective-permute-start | bytes 294920 | tf_op jit(solution)/shard_map/ppermute | solution.py:463
  18.2 1.4 collective-permute-start.9
  20.2 8.4 %pack.3 = (bf16[80,128,128]{2,1,0:T(8,128)(2,1)}, bf16[65,128,128]{2,1,0:T(8,128)(2,1)}, bf16[145,128,128]{2,1,0:T(8,128)(2,1)}) custom-call(s32[1]{0:T(128)} %bitcast.turn_ref.refs_1_, s32[16,16]{1,0:T(8,128)S(1)} %copy-done.13, s32[16,16]{1,0:T(8,128)S(1)} %copy-done.13, bf16[128,128]{1,0:T(8,128)(2,1)} %pad.4.header_ref, bf16[2048,2048]{1,0:T(8,128)(2,1)} %values_ref.3), custom_call_target="tpu_custom_call" | custom-call | flops 1 | bytes 1 | tf_op jit(solution)/shard_map/pack/pallas_call | solution.py:172
  29.3 1.4 collective-permute-start.10
  30.7 1.0 pad_maximum_fusion.1.refs_0_
  32.3 1.3 bitcast_convert_fusion.1.flags_ref
  33.6 5.7 %unpack_b.8 = (bf16[8192,1024]{1,0:T(8,128)(2,1)}, s32[1]{0:T(128)}) custom-call(s32[1]{0:T(128)} %bitcast.11.shard_ref, s32[16,16]{1,0:T(8,128)} %bitcast_convert_fusion.1.flags_ref, bf16[145,128,128]{2,1,0:T(8,128)(2,1)} %get-tuple-element.65.refs_0_, s32[1]{0:T(128)} %bitcast.turn_ref.refs_1_), custom_call_target="tpu_custom_call" | custom-call | flops 1 | bytes 1 | tf_op jit(solution)/shard_map/unpack_b/pallas_call | solution.py:251
  39.3 6.9 %unpack_b.9 = (bf16[8192,1024]{1,0:T(8,128)(2,1)}, s32[1]{0:T(128)}) custom-call(s32[1]{0:T(128)} %bitcast.11.shard_ref, s32[16,16]{1,0:T(8,128)} %bitcast_convert_fusion.1.flags_ref, bf16[145,128,128]{2,1,0:T(8,128)(2,1)} %get-tuple-element.65.refs_0_, s32[1]{0:T(128)} %get-tuple-element.66.refs_1_), custom_call_target="tpu_custom_call" | custom-call | flops 1 | bytes 1 | tf_op jit(solution)/shard_map/unpack_b/pallas_call | solution.py:251
  46.9 1.3 fusion.13.flags_ref
  48.2 6.4 %unpack_b.10 = (bf16[8192,1024]{1,0:T(8,128)(2,1)}, s32[1]{0:T(128)}) custom-call(s32[1]{0:T(128)} %bitcast.8.shard_ref, s32[16,16]{1,0:T(8,128)} %fusion.13.flags_ref, bf16[145,128,128]{2,1,0:T(8,128)(2,1)} %collective-permute-done.11.refs_0_, s32[1]{0:T(128)} %get-tuple-element.67.refs_1_, ...), custom_call_target="tpu_custom_call", output_to_operand_aliasing={{0}: (4, {})} | custom-call | flops 1 | bytes 1 | tf_op jit(solution)/shard_map/unpack_b/pallas_call | solution.py:251
  54.6 6.8 %unpack_b.11 = (bf16[8192,1024]{1,0:T(8,128)(2,1)}, s32[1]{0:T(128)}) custom-call(s32[1]{0:T(128)} %bitcast.8.shard_ref, s32[16,16]{1,0:T(8,128)} %fusion.13.flags_ref, bf16[145,128,128]{2,1,0:T(8,128)(2,1)} %collective-permute-done.11.refs_0_, s32[1]{0:T(128)} %get-tuple-element.69.refs_1_, ...), custom_call_target="tpu_custom_call", output_to_operand_aliasing={{0}: (5, {})} | custom-call | flops 1 | bytes 1 | tf_op jit(solution)/shard_map/unpack_b/pallas_call | solution.py:251
  62.7 26.2 %collective-permute-done.13 = f32[8,128]{1,0:T(8,128)S(1)} collective-permute-done((f32[8,128]{1,0:T(8,128)}, f32[8,128]{1,0:T(8,128)S(1)}, u32[]{:S(2)}, u32[]{:S(2)}) %collective-permute-start.13) | collective-permute-done | bytes 4128 | tf_op jit(solution)/shard_map/ppermute | solution.py:508
  88.9 1.3 max.7.refs_3_.refs_4_.refs_7_.refs_10_
  91.0 1.5 collective-permute-start.18
  93.0 1.3 bitcast_convert_fusion.flags_ref
  94.3 5.8 %unpack_b.12 = (bf16[8192,1024]{1,0:T(8,128)(2,1)}, s32[1]{0:T(128)}) custom-call(s32[1]{0:T(128)} %bitcast.15.shard_ref, s32[16,16]{1,0:T(8,128)} %bitcast_convert_fusion.flags_ref, bf16[80,128,128]{2,1,0:T(8,128)(2,1)} %get-tuple-element.72.refs_0_, s32[1]{0:T(128)} %get-tuple-element.71.refs_1_.refs_2_, ...), custom_call_target="tpu_custom_call", output_to_operand_aliasing={{0}: (4, {})} | custom-call | flops 1 | bytes 1 | tf_op jit(solution)/shard_map/unpack_b/pallas_call | solution.py:251
  100.1 1.3 fusion.12.flags_ref
  101.4 5.8 %unpack_b.13 = (bf16[8192,1024]{1,0:T(8,128)(2,1)}, s32[1]{0:T(128)}) custom-call(s32[1]{0:T(128)} %bitcast.7.shard_ref, s32[16,16]{1,0:T(8,128)} %fusion.12.flags_ref, bf16[80,128,128]{2,1,0:T(8,128)(2,1)} %collective-permute-done.14.refs_0_, s32[1]{0:T(128)} %get-tuple-element.74.refs_1_, ...), custom_call_target="tpu_custom_call", output_to_operand_aliasing={{0}: (4, {})} | custom-call | flops 1 | bytes 1 | tf_op jit(solution)/shard_map/unpack_b/pallas_call | solution.py:251
  107.2 6.2 %all-gather.7.cloned.1.call-done = bf16[160,128,128]{2,1,0:T(8,128)(2,1)} async-done(((bf16[40,128,128]{2,1,0:T(8,128)(2,1)}), bf16[160,128,128]{2,1,0:T(8,128)(2,1)}) %all-gather.7.cloned.1.call-update) | async-done | bytes 5242896 | tf_op jit(solution)/shard_map/all_gather | solution.py:467
  114.1 1.0 collective-permute-start.16
  115.0 2.8 %collective-permute-start.17 = (bf16[4,128,128]{2,1,0:T(8,128)(2,1)}, bf16[4,128,128]{2,1,0:T(8,128)(2,1)S(1)}, u32[]{:S(2)}, u32[]{:S(2)}) collective-permute-start(bf16[4,128,128]{2,1,0:T(8,128)(2,1)} %after.8), channel_id=1, source_target_pairs={{0,6},{2,0},{4,2},{6,4},{1,7},{3,1},{5,3},{7,5},{8,14},{10,8},{12,... | collective-permute-start | bytes 393224 | tf_op jit(solution)/shard_map/ppermute | solution.py:463
  118.5 17.3 %multiply.4.refs_1_ = s16[544,1024]{1,0:T(8,128)(2,1)} custom-call(s32[4,128]{1,0:T(4,128)} %bitcast.75, s32[4]{0:T(128)} %compare_select_fusion.hop_ref, bf16[4,3,128,128]{3,2,1,0:T(8,128)(2,1)} %copy-done.2, bf16[4,40,128,128]{3,2,1,0:T(8,128)(2,1)} %bitcast.58, bf16[4,1,2048,1024]{3,2,1,0:T(8,128)(2,1)} %bitcast.54, ...), custom_call_target="tpu_custom_call" | custom-call | flops 1 | bytes 1 | tf_op jit(solution)/shard_map/multiply/pallas_call | solution.py:416
  135.7 4.4 %collective-permute-done.18.refs_0_ = bf16[65,128,128]{2,1,0:T(8,128)(2,1)} collective-permute-done((bf16[65,128,128]{2,1,0:T(8,128)(2,1)}, bf16[65,128,128]{2,1,0:T(8,128)(2,1)}, u32[]{:S(2)}, u32[]{:S(2)}) %collective-permute-start.18) | collective-permute-done | bytes 2129952 | tf_op jit(solution)/shard_map/ppermute | solution.py:484
  141.5 1.6 collective-permute-start.20
  143.1 6.9 %unpack_b.14 = (bf16[8192,1024]{1,0:T(8,128)(2,1)}, s32[1]{0:T(128)}) custom-call(s32[1]{0:T(128)} %bitcast.15.shard_ref, s32[16,16]{1,0:T(8,128)} %bitcast_convert_fusion.flags_ref, bf16[80,128,128]{2,1,0:T(8,128)(2,1)} %get-tuple-element.72.refs_0_, bf16[65,128,128]{2,1,0:T(8,128)(2,1)} %after.9.refs_1_, ...), custom_call_target="tpu_custom_call", output_to_operand_aliasing={{0}: (5, {})} | custom-call | flops 1 | bytes 1 | tf_op jit(solution)/shard_map/unpack_b/pallas_call | solution.py:251
  150.0 6.9 %unpack_b.15 = (bf16[8192,1024]{1,0:T(8,128)(2,1)}, s32[1]{0:T(128)}) custom-call(s32[1]{0:T(128)} %bitcast.7.shard_ref, s32[16,16]{1,0:T(8,128)} %fusion.12.flags_ref, bf16[80,128,128]{2,1,0:T(8,128)(2,1)} %collective-permute-done.14.refs_0_, bf16[65,128,128]{2,1,0:T(8,128)(2,1)} %collective-permute-done.19.refs_1_, ...), custom_call_target="tpu_custom_call", output_to_operand_aliasing={{0}: (5, {})} | custom-call | flops 1 | bytes 1 | tf_op jit(solution)/shard_map/unpack_b/pallas_call | solution.py:251
  156.9 17.1 %multiply.5.refs_6_ = s16[528,1024]{1,0:T(8,128)(2,1)} custom-call(s32[4,128]{1,0:T(4,128)} %bitcast.76, s32[4]{0:T(128)} %compare_select_fusion.hop_ref, bf16[4,3,128,128]{3,2,1,0:T(8,128)(2,1)} %copy-done.2, bf16[4,40,128,128]{3,2,1,0:T(8,128)(2,1)} %bitcast.59, bf16[4,1,2048,1024]{3,2,1,0:T(8,128)(2,1)} %bitcast.51, s32[1]{0:T(128)} %get-tuple-element.85.refs_3_, ...), custom_call_target="tpu_custom_call" | custom-call | flops 1 | bytes 1 | tf_op jit(solution)/shard_map/multiply/pallas_call | solution.py:416
  176.1 22.4 %multiply.6.refs_9_ = f32[512,2048]{1,0:T(8,128)} custom-call(s32[4,128]{1,0:T(4,128)} %bitcast.77, s32[4]{0:T(128)} %compare_select_fusion.hop_ref, bf16[4,3,128,128]{3,2,1,0:T(8,128)(2,1)} %copy-done.2, bf16[4,40,128,128]{3,2,1,0:T(8,128)(2,1)} %bitcast.60, bf16[4,4,128,128]{3,2,1,0:T(8,128)(2,1)} %pad_maximum_fusion.refs_2_, ...), custom_call_target="tpu_custom_call" | custom-call | flops 1 | bytes 1 | tf_op jit(solution)/shard_map/multiply/pallas_call | solution.py:416
  198.5 5.4 %all-gather.11.cloned.1.call-done = bf16[32,128,128]{2,1,0:T(8,128)(2,1)} async-done(((bf16[8,128,128]{2,1,0:T(8,128)(2,1)}), bf16[32,128,128]{2,1,0:T(8,128)(2,1)}) %all-gather.11.cloned.1.call-update) | async-done | bytes 1048592 | tf_op jit(solution)/shard_map/all_gather | solution.py:467
  203.9 12.7 %multiply.7 = (f32[512,2048]{1,0:T(8,128)}, s32[1]{0:T(128)}) custom-call(s32[4,128]{1,0:T(4,128)} %bitcast.78, s32[4]{0:T(128)} %compare_select_fusion.hop_ref, bf16[4,3,128,128]{3,2,1,0:T(8,128)(2,1)} %copy-done.2, bf16[4,40,128,128]{3,2,1,0:T(8,128)(2,1)} %bitcast.61, bf16[4,4,128,128]{3,2,1,0:T(8,128)(2,1)} %pad_maximum_fusion.refs_2_, ...), custom_call_target="tpu_custom_call" | custom-call | flops 1 | bytes 1 | tf_op jit(solution)/shard_map/multiply/pallas_call | solution.py:416
  (70 shorter events, 10.1 us)
Async XLA Ops:
  6.5 13.0 %copy-start.13 = (s32[16,16]{1,0:T(8,128)S(1)}, s32[16,16]{1,0:T(8,128)}, u32[]{:S(2)}) copy-start(s32[16,16]{1,0:T(8,128)} %other_ref.3) | copy-start | bytes 3076
  6.5 106.9 %all-gather.7.cloned.1.call-start = ((), (), s32[]{:S(2)}) async-start(), calls=%async_computation | async-start | bytes 6553600 | tf_op jit(solution)/shard_map/all_gather | solution.py:467
  12.5 18.3 %copy-start.14 = (bf16[3,128,128]{2,1,0:T(8,128)(2,1)S(1)}, bf16[3,128,128]{2,1,0:T(8,128)(2,1)}, u32[]{:S(2)}) copy-start(bf16[3,128,128]{2,1,0:T(8,128)(2,1)} %get-tuple-element.58) | copy-start | bytes 294916
  12.5 163.6 %all-gather.9.cloned.1.call-start = ((), (), s32[]{:S(2)}) async-start(), calls=%async_computation.1 | async-start | bytes 3604480 | tf_op jit(solution)/shard_map/all_gather | solution.py:467
  12.5 16.0 %collective-permute-start.7 = (bf16[3,128,128]{2,1,0:T(8,128)(2,1)}, bf16[3,128,128]{2,1,0:T(8,128)(2,1)S(1)}, u32[]{:S(2)}, u32[]{:S(2)}) collective-permute-start(bf16[3,128,128]{2,1,0:T(8,128)(2,1)} %get-tuple-element.58), channel_id=1, source_target_pairs={{0,2},{2,4},{4,6},{6,0},{1,3},{3,5},{5,7},{7,1},{8,10},{10,12},{12... | collective-permute-start | bytes 294920 | tf_op jit(solution)/shard_map/ppermute | solution.py:463
  15.6 13.0 %collective-permute-start.8 = (bf16[3,128,128]{2,1,0:T(8,128)(2,1)}, bf16[3,128,128]{2,1,0:T(8,128)(2,1)S(1)}, u32[]{:S(2)}, u32[]{:S(2)}) collective-permute-start(bf16[3,128,128]{2,1,0:T(8,128)(2,1)} %get-tuple-element.58), channel_id=1, source_target_pairs={{0,4},{2,6},{4,0},{6,2},{1,5},{3,7},{5,1},{7,3},{8,12},{10,14},{12... | collective-permute-start | bytes 294920 | tf_op jit(solution)/shard_map/ppermute | solution.py:463
  18.2 10.4 %collective-permute-start.9 = (bf16[3,128,128]{2,1,0:T(8,128)(2,1)}, bf16[3,128,128]{2,1,0:T(8,128)(2,1)S(1)}, u32[]{:S(2)}, u32[]{:S(2)}) collective-permute-start(bf16[3,128,128]{2,1,0:T(8,128)(2,1)} %get-tuple-element.58), channel_id=1, source_target_pairs={{0,6},{2,0},{4,2},{6,4},{1,7},{3,1},{5,3},{7,5},{8,14},{10,8},{12,... | collective-permute-start | bytes 294920 | tf_op jit(solution)/shard_map/ppermute | solution.py:463
  28.6 0.6 copy-start.10
  28.6 0.7 copy-start.11
  28.6 0.7 copy-start.12
  29.3 17.6 %collective-permute-start.11 = (bf16[145,128,128]{2,1,0:T(8,128)(2,1)}, bf16[145,128,128]{2,1,0:T(8,128)(2,1)}, u32[]{:S(2)}, u32[]{:S(2)}) collective-permute-start(bf16[145,128,128]{2,1,0:T(8,128)(2,1)} %get-tuple-element.65.refs_0_), channel_id=1, source_target_pairs={{0,8},{8,0},{16,24},{24,16},{1,9},{9,1},{17,25},{25,17},{2,10},{10... | collective-permute-start | bytes 14254088 | tf_op jit(solution)/shard_map/ppermute | solution.py:500
  29.3 60.9 %collective-permute-start.10 = (bf16[80,128,128]{2,1,0:T(8,128)(2,1)}, bf16[80,128,128]{2,1,0:T(8,128)(2,1)}, u32[]{:S(2)}, u32[]{:S(2)}) collective-permute-start(bf16[80,128,128]{2,1,0:T(8,128)(2,1)} %get-tuple-element.63), channel_id=1, source_target_pairs={{0,16},{8,24},{16,0},{24,8},{1,17},{9,25},{17,1},{25,9},{2,18},{10... | collective-permute-start | bytes 7864328 | tf_op jit(solution)/shard_map/ppermute | solution.py:484
  31.8 86.1 %copy-start.2 = (bf16[4,3,128,128]{3,2,1,0:T(8,128)(2,1)}, bf16[4,3,128,128]{3,2,1,0:T(8,128)(2,1)S(1)}, u32[]{:S(2)}) copy-start(bf16[4,3,128,128]{3,2,1,0:T(8,128)(2,1)S(1)} %pad_maximum_fusion.1.refs_0_) | copy-start | bytes 1179652
  32.1 14.1 %collective-permute-start.12 = (f32[8,128]{1,0:T(8,128)S(1)}, f32[8,128]{1,0:T(8,128)S(1)}, u32[]{:S(2)}, u32[]{:S(2)}) collective-permute-start(f32[8,128]{1,0:T(8,128)S(1)} %broadcast_in_dim.14), channel_id=1, source_target_pairs={{0,8},{8,0},{16,24},{24,16},{1,9},{9,1},{17,25},{25,17},{2,10},{10... | collective-permute-start | bytes 12296 | tf_op jit(solution)/shard_map/ppermute | solution.py:501
  62.0 26.9 %collective-permute-start.13 = (f32[8,128]{1,0:T(8,128)}, f32[8,128]{1,0:T(8,128)S(1)}, u32[]{:S(2)}, u32[]{:S(2)}) collective-permute-start(f32[8,128]{1,0:T(8,128)} %after.6), channel_id=1, source_target_pairs={{0,16},{8,24},{16,0},{24,8},{1,17},{9,25},{17,1},{25,9},{2,18},{10... | collective-permute-start | bytes 12296 | tf_op jit(solution)/shard_map/ppermute | solution.py:508
  90.8 9.2 %collective-permute-start.14 = (bf16[80,128,128]{2,1,0:T(8,128)(2,1)}, bf16[80,128,128]{2,1,0:T(8,128)(2,1)}, u32[]{:S(2)}, u32[]{:S(2)}) collective-permute-start(bf16[80,128,128]{2,1,0:T(8,128)(2,1)} %get-tuple-element.72.refs_0_), channel_id=1, source_target_pairs={{0,8},{8,0},{16,24},{24,16},{1,9},{9,1},{17,25},{25,17},{2,10},{10... | collective-permute-start | bytes 7864328 | tf_op jit(solution)/shard_map/ppermute | solution.py:513
  91.0 112.9 %all-gather.11.cloned.1.call-start = ((), (), s32[]{:S(2)}) async-start(), calls=%async_computation.2 | async-start | bytes 1310720 | tf_op jit(solution)/shard_map/all_gather | solution.py:467
  91.0 49.1 %collective-permute-start.18 = (bf16[65,128,128]{2,1,0:T(8,128)(2,1)}, bf16[65,128,128]{2,1,0:T(8,128)(2,1)}, u32[]{:S(2)}, u32[]{:S(2)}) collective-permute-start(bf16[65,128,128]{2,1,0:T(8,128)(2,1)} %get-tuple-element.80), channel_id=1, source_target_pairs={{0,16},{8,24},{16,0},{24,8},{1,17},{9,25},{17,1},{25,9},{2,18},{10... | collective-permute-start | bytes 6389768 | tf_op jit(solution)/shard_map/ppermute | solution.py:484
  114.0 26.1 %collective-permute-start.15 = (bf16[4,128,128]{2,1,0:T(8,128)(2,1)}, bf16[4,128,128]{2,1,0:T(8,128)(2,1)S(1)}, u32[]{:S(2)}, u32[]{:S(2)}) collective-permute-start(bf16[4,128,128]{2,1,0:T(8,128)(2,1)} %after.8), channel_id=1, source_target_pairs={{0,2},{2,4},{4,6},{6,0},{1,3},{3,5},{5,7},{7,1},{8,10},{10,12},{12... | collective-permute-start | bytes 393224 | tf_op jit(solution)/shard_map/ppermute | solution.py:463
  114.1 26.1 %collective-permute-start.16 = (bf16[4,128,128]{2,1,0:T(8,128)(2,1)}, bf16[4,128,128]{2,1,0:T(8,128)(2,1)S(1)}, u32[]{:S(2)}, u32[]{:S(2)}) collective-permute-start(bf16[4,128,128]{2,1,0:T(8,128)(2,1)} %after.8), channel_id=1, source_target_pairs={{0,4},{2,6},{4,0},{6,2},{1,5},{3,7},{5,1},{7,3},{8,12},{10,14},{12... | collective-permute-start | bytes 393224 | tf_op jit(solution)/shard_map/ppermute | solution.py:463
  115.0 25.1 %collective-permute-start.17 = (bf16[4,128,128]{2,1,0:T(8,128)(2,1)}, bf16[4,128,128]{2,1,0:T(8,128)(2,1)S(1)}, u32[]{:S(2)}, u32[]{:S(2)}) collective-permute-start(bf16[4,128,128]{2,1,0:T(8,128)(2,1)} %after.8), channel_id=1, source_target_pairs={{0,6},{2,0},{4,2},{6,4},{1,7},{3,1},{5,3},{7,5},{8,14},{10,8},{12,... | collective-permute-start | bytes 393224 | tf_op jit(solution)/shard_map/ppermute | solution.py:463
  140.1 0.6 copy-start.4
  140.1 0.7 copy-start.6
  140.8 0.7 copy-start.8
  141.5 8.4 %collective-permute-start.19 = (bf16[65,128,128]{2,1,0:T(8,128)(2,1)}, bf16[65,128,128]{2,1,0:T(8,128)(2,1)}, u32[]{:S(2)}, u32[]{:S(2)}) collective-permute-start(bf16[65,128,128]{2,1,0:T(8,128)(2,1)} %after.9.refs_1_), channel_id=1, source_target_pairs={{0,8},{8,0},{16,24},{24,16},{1,9},{9,1},{17,25},{25,17},{2,10},{10... | collective-permute-start | bytes 6389768 | tf_op jit(solution)/shard_map/ppermute | solution.py:539
  141.5 62.4 %collective-permute-start.20 = (s16[544,1024]{1,0:T(8,128)(2,1)}, s16[544,1024]{1,0:T(8,128)(2,1)}, u32[]{:S(2)}, u32[]{:S(2)}) collective-permute-start(s16[544,1024]{1,0:T(8,128)(2,1)} %multiply.4.refs_1_), channel_id=1, source_target_pairs={{0,1},{1,0},{2,3},{3,2},{4,5},{5,4},{6,7},{7,6},{8,9},{9,8},{10,11... | collective-permute-start | bytes 3342344 | tf_op jit(solution)/shard_map/ppermute | solution.py:527
  156.9 17.7 %copy-start.3 = (bf16[4,128,128]{2,1,0:T(8,128)(2,1)S(1)}, bf16[4,128,128]{2,1,0:T(8,128)(2,1)}, u32[]{:S(2)}) copy-start(bf16[4,128,128]{2,1,0:T(8,128)(2,1)} %after.8) | copy-start | bytes 393220
  156.9 17.7 %copy-start.5 = (bf16[4,128,128]{2,1,0:T(8,128)(2,1)S(1)}, bf16[4,128,128]{2,1,0:T(8,128)(2,1)}, u32[]{:S(2)}) copy-start(bf16[4,128,128]{2,1,0:T(8,128)(2,1)} %copy-done.4) | copy-start | bytes 393220
  156.9 17.7 %copy-start.7 = (bf16[4,128,128]{2,1,0:T(8,128)(2,1)S(1)}, bf16[4,128,128]{2,1,0:T(8,128)(2,1)}, u32[]{:S(2)}) copy-start(bf16[4,128,128]{2,1,0:T(8,128)(2,1)} %copy-done.6) | copy-start | bytes 393220
  156.9 17.7 %copy-start.9 = (bf16[4,128,128]{2,1,0:T(8,128)(2,1)S(1)}, bf16[4,128,128]{2,1,0:T(8,128)(2,1)}, u32[]{:S(2)}) copy-start(bf16[4,128,128]{2,1,0:T(8,128)(2,1)} %copy-done.8) | copy-start | bytes 393220
  174.0 29.9 %collective-permute-start.21 = (s16[528,1024]{1,0:T(8,128)(2,1)}, s16[528,1024]{1,0:T(8,128)(2,1)}, u32[]{:S(2)}, u32[]{:S(2)}) collective-permute-start(s16[528,1024]{1,0:T(8,128)(2,1)} %multiply.5.refs_6_), channel_id=1, source_target_pairs={{0,1},{1,0},{2,3},{3,2},{4,5},{5,4},{6,7},{7,6},{8,9},{9,8},{10,11... | collective-permute-start | bytes 3244040 | tf_op jit(solution)/shard_map/ppermute | solution.py:527
  203.9 13.3 %copy-start.15 = (s32[8,16]{1,0:T(8,128)S(1)}, s32[8,16]{1,0:T(8,128)}, u32[]{:S(2)}) copy-start(s32[8,16]{1,0:T(8,128)} %flags_ref.2) | copy-start | bytes 1540
Sparse Core Ops, SparseCore 0:
  12.6 100.7 all-gather.6
  115.0 61.0 all-gather.8
  177.6 26.2 all-gather.10
